TPU v7x, 128 devices: a whole 4x4x4 slice. The times are simulated.
128 devices in a mesh: dp: 8 (over y_hi, x), field: 16 (over y_lo, z, core).
Axes of the slice: x: 4, y: 4 (y_hi: 2, y_lo: 2; y = y_hi * 2 + y_lo), z: 4, core: 2. Of those that a mesh axis runs over, the one named last changes fastest.
Arguments:
- emb: bfloat16 [1024, 512, 192], P('dp', 'field'), may hold values from -6 to 6
- comp: bfloat16 [512, 128], P('field'), may hold values from -0.15625 to 0.15625
- cot: bfloat16 [1024, 512, 128], P('dp', 'field'), may hold values from -6 to 6
- pairs: int32 [1152, 2], P('field'), may hold values from 0 to 15, as said below
- counts: int32 [16], P('field'), may hold values from 1 to 72, as said below
Outputs:
- mixed: bfloat16 [1024, 512, 128], P('dp', 'field')
- emb_grad: bfloat16 [1024, 512, 192], P('dp', 'field')
- weight_grad: float32 [512, 128], P('field')
Inputs may be any that keep to these rules, and one draw needn't show every extreme that they name: `pairs`: each row names two field tiles, the first at most the second; rows may repeat. Field index f uses its first counts[f] rows; the counts sum to 384; the largest is exactly 72.
All inputs are finite; a program needn't handle non-finite values.
Results may differ from a plain program's by a relative error of at most 0.011.
Values may be sent and summed in bfloat16 or wider, within the bound.
No kernel may reach another device: no remote copies, remote signals or barrier semaphores. Data moves between devices by JAX's collectives and lax.ppermute only.
A program may use at most 192 MiB of HBM per device.

v0:
```python
import jax
import jax.numpy as jnp
from jax import lax
from jax.sharding import PartitionSpec as P


def pair_mult(all_pairs, all_counts, fields):
    slots = all_pairs.shape[0] // fields
    live = (jnp.arange(slots)[None, :] < all_counts[:, None]).reshape(-1).astype(jnp.float32)
    first = jax.nn.one_hot(all_pairs[:, 0], fields, dtype=jnp.float32) * live[:, None]
    second = jax.nn.one_hot(all_pairs[:, 1], fields, dtype=jnp.float32)
    table = jnp.dot(first.T, second, precision=lax.Precision.HIGHEST)
    return table + table.T - jnp.diag(jnp.diag(table))


def per_device(emb, comp, cot, pairs, counts):
    samp_rows, tile, width = emb.shape
    compressed = comp.shape[1]
    fields = lax.axis_size("field")
    embeds = tile * fields
    scale = width ** (-0.5)
    f32 = jnp.float32
    weights = lax.all_gather(comp, "field", axis=0, tiled=True)
    wtiles = weights.reshape(fields, tile, compressed)
    table_pairs, table_counts = (
        lax.all_gather(pairs, "field", axis=0, tiled=True),
        lax.all_gather(counts, "field", axis=0, tiled=True),
    )
    mult = pair_mult(table_pairs, table_counts, fields)
    features, cotangent = (
        lax.all_gather(emb, "field", axis=1, tiled=True),
        lax.all_gather(cot, "field", axis=1, tiled=True),
    )
    mult_row = lax.dynamic_index_in_dim(mult, lax.axis_index("field"), 0, keepdims=False)
    gram = (scale * jnp.einsum("brd,bcd->brc", emb, features, preferred_element_type=f32)).astype(
        jnp.bfloat16
    )
    gram_tiles = gram.reshape(samp_rows, tile, fields, tile)
    blocks = jnp.einsum("brBc,Bck->bBrk", gram_tiles, wtiles, preferred_element_type=f32)
    mixed = jnp.einsum("bBrk,B->brk", blocks, mult_row).astype(jnp.bfloat16)
    hmat_rows = jnp.einsum("brk,ck->brc", cot, weights, preferred_element_type=f32)
    hmat_cols = jnp.einsum("bck,rk->brc", cotangent, comp, preferred_element_type=f32)
    sym = (scale * (hmat_rows + hmat_cols)).astype(jnp.bfloat16)
    sym_tiles = sym.reshape(samp_rows, tile, fields, tile)
    feat_tiles = features.reshape(samp_rows, fields, tile, width)
    fblocks = jnp.einsum("brBc,bBcd->bBrd", sym_tiles, feat_tiles, preferred_element_type=f32)
    emb_grad = jnp.einsum("bBrd,B->brd", fblocks, mult_row).astype(jnp.bfloat16)
    terms = jnp.einsum("brBc,brk->Bck", gram_tiles, cot, preferred_element_type=f32)
    partial_value = (terms * mult_row[:, None, None]).reshape(embeds, compressed)
    own_tile = lax.psum_scatter(partial_value, "field", scatter_dimension=0, tiled=True)
    weight_grad = lax.psum(own_tile, "dp") / (samp_rows * lax.axis_size("dp"))
    return (mixed, emb_grad, weight_grad)


def solution(mesh):
    in_specs = (
        P("dp", "field", None),
        P("field", None),
        P("dp", "field", None),
        P("field", None),
        P("field"),
    )
    out_specs = (P("dp", "field", None), P("dp", "field", None), P("field", None))
    return jax.shard_map(
        per_device, mesh=mesh, in_specs=in_specs, out_specs=out_specs, check_vma=False
    )
```

profile of v0, /device:TPU:0, one launch (start us, length us, event | category | flops | bytes accessed | tf_op | source)
XLA Modules:
  0.0 542.3 jit_solution(18271531606996872884)
XLA Ops:
  7.2 0.0 copy-start.2
  7.2 0.0 all-gather.6.cloned.1.call-start
  7.2 0.7 all-gather.6.cloned.1.call-update
  7.9 0.0 all-gather.4.cloned.1.call-start
  8.0 4.5 copy.26
  12.5 0.0 all-gather.4.cloned.1.call-update
  12.5 0.0 reduce-scatter.2.cloned.1.call-start
  12.5 21.3 %all-gather = s32[16,72,2]{1,2,0:T(2,128)S(1)} all-gather(s32[1,72,2]{1,2,0:T(2,128)} %bitcast.89), channel_id=1, replica_groups=mesh['dp'=8,'field'=16] {'field'}, dimensions={0}, use_global_device_ids=true | all-gather | bytes 9792 | tf_op jit(solution)/shard_map/all_gather | solution.py:26
  33.9 0.1 reshape.57
  34.6 1.2 dynamic-slice
  35.8 0.8 dynamic-update-slice
  36.6 8.2 %all-reduce = s32[16]{0:T(128)S(1)} all-reduce(s32[16]{0:T(128)S(1)} %dynamic-update-slice), channel_id=1, replica_groups=mesh['dp'=8,'field'=16] {'field'}, use_global_device_ids=true, to_apply=%add | all-reduce | flops 16 | bytes 128
  44.8 0.1 fusion.15
  44.9 0.1 reshape.46
  45.0 1.1 fusion.6
  46.1 0.1 copy.30
  46.2 0.7 gather_fusion
  46.9 0.6 dynamic-slice.1
  47.5 22.0 %all_gather.16 = bf16[512,128]{1,0:T(8,128)(2,1)S(1)} all-gather(bf16[32,128]{1,0:T(8,128)(2,1)} %param.6), channel_id=1, replica_groups=mesh['dp'=8,'field'=16] {'field'}, dimensions={0}, use_global_device_ids=true | all-gather | bytes 139264 | tf_op jit(solution)/shard_map/all_gather | solution.py:23
  69.5 0.7 fusion.16
  70.1 5.7 %fusion.12 = f32[128,32,512]{2,1,0:T(8,128)} fusion(bf16[128,32,128]{2,1,0:T(8,128)(2,1)} %param.7, bf16[512,128]{1,0:T(8,128)(2,1)S(1)} %all_gather.16), kind=kOutput, calls=%fused_computation.19 | convolution fusion | flops 536870912 | bytes 9568256 | tf_op jit(solution)/shard_map/brk,ck->brc/dot_general | solution.py:41
  75.8 28.7 %all-gather.6.cloned.1.call-done = bf16[128,512,128]{2,1,0:T(8,128)(2,1)} async-done(((bf16[128,32,128]{2,1,0:T(8,128)(2,1)}), bf16[128,512,128]{2,1,0:T(8,128)(2,1)}) %all-gather.6.cloned.1.call-update) | async-done | bytes 16777232 | tf_op jit(solution)/shard_map/all_gather | solution.py:32
  104.5 0.0 copy-done.2
  104.5 12.6 %fusion.3 = bf16[128,32,512]{2,1,0:T(8,128)(2,1)} fusion(f32[128,32,512]{2,1,0:T(8,128)} %fusion.12, bf16[128,512,128]{2,1,0:T(8,128)(2,1)} %all-gather.6.cloned.1.call-done, bf16[32,128]{1,0:T(8,128)(2,1)S(1)} %copy-done.2), kind=kOutput, calls=%fused_computation.6 | convolution fusion | flops 543162368 | bytes 29368320 | tf_op jit(solution)/shard_map/bck,rk->brc/dot_general | solution.py:42
  117.1 0.0 copy-start
  117.1 8.2 %copy.33 = bf16[128,32,512]{0,2,1:T(8,128)(2,1)} copy(bf16[128,32,512]{2,1,0:T(8,128)(2,1)} %fusion.3) | data formatting | bytes 8388608 | tf_op jit(solution)/shard_map/convert_element_type | solution.py:43
  125.3 23.1 %copy.34 = bf16[128,32,16,32]{3,1,2,0:T(8,128)(2,1)} copy(bf16[128,32,16,32]{0,3,2,1:T(8,128)(2,1)} %bitcast.82) | data formatting | bytes 8388608 | tf_op jit(solution)/shard_map/reshape | solution.py:44
  148.4 129.4 %all-gather.4.cloned.1.call-done = bf16[128,512,192]{2,1,0:T(8,128)(2,1)} async-done(((bf16[128,32,192]{2,1,0:T(8,128)(2,1)}), bf16[128,512,192]{2,1,0:T(8,128)(2,1)}) %all-gather.4.cloned.1.call-update) | async-done | bytes 25165840 | tf_op jit(solution)/shard_map/all_gather | solution.py:31
  277.8 0.0 copy-done
  277.8 17.1 %multiply_convert_fusion = bf16[128,32,512]{2,1,0:T(8,128)(2,1)} fusion(bf16[128,32,192]{2,1,0:T(8,128)(2,1)S(1)} %copy-done, bf16[128,512,192]{2,1,0:T(8,128)(2,1)} %all-gather.4.cloned.1.call-done), kind=kOutput, calls=%fused_computation.7 | convolution fusion | flops 809500672 | bytes 30932992 | tf_op jit(solution)/shard_map/brd,bcd->brc/dot_general | solution.py:35
  294.9 7.9 %copy.27 = bf16[128,32,512]{0,2,1:T(8,128)(2,1)} copy(bf16[128,32,512]{2,1,0:T(8,128)(2,1)} %multiply_convert_fusion) | data formatting | bytes 8388608 | tf_op jit(solution)/shard_map/convert_element_type | solution.py:35
  302.8 23.1 %copy.28 = bf16[128,32,16,32]{3,1,0,2:T(8,128)(2,1)} copy(bf16[128,32,16,32]{0,3,2,1:T(8,128)(2,1)} %bitcast.80) | data formatting | bytes 8388608 | tf_op jit(solution)/shard_map/reshape | solution.py:38
  325.9 11.4 %convolution_bitcast_fusion = bf16[128,16,32,128]{3,2,0,1:T(8,128)(2,1)} fusion(bf16[128,32,16,32]{3,1,0,2:T(8,128)(2,1)} %copy.28, bf16[16,32,128,1]{2,1,3,0:T(8,128)(2,1)S(1)} %bitcast.85), kind=kOutput, calls=%fused_computation.3 | convolution fusion | flops 536870912 | bytes 21102592 | tf_op jit(solution)/shard_map/brBc,Bck->bBrk/dot_general | solution.py:39
  337.3 0.0 copy-start.1
  337.3 15.9 %fusion = f32[1,128,32,128]{3,0,2,1:T(1,128)S(1)} fusion(bf16[128,16,32,128]{3,2,0,1:T(8,128)(2,1)} %convolution_bitcast_fusion, f32[1,16]{1,0:T(1,128)S(1)} %fusion.16), kind=kOutput, calls=%fused_computation.1 | convolution fusion | flops 16777216 | bytes 18874432 | tf_op jit(solution)/shard_map/bBrk,B->brk/dot_general | solution.py:40
  353.2 0.0 copy-done.1
  353.2 4.2 fusion.4
  357.4 0.0 reduce-scatter.2.cloned.1.call-update
  357.4 27.3 %fusion.28 = bf16[128,16,32,192]{3,2,1,0:T(8,128)(2,1)} fusion(bf16[128,32,16,32]{3,1,2,0:T(8,128)(2,1)} %copy.34, bf16[128,16,32,192]{3,2,1,0:T(8,128)(2,1)} %bitcast.78), kind=kOutput, calls=%fused_computation.38 | convolution fusion | flops 805306368 | bytes 54525952 | tf_op jit(solution)/shard_map/brBc,bBcd->bBrd/dot_general | solution.py:46
  384.7 96.3 %copy.42 = bf16[128,16,32,192]{0,1,3,2:T(8,128)(2,1)} copy(bf16[128,16,32,192]{3,2,1,0:T(8,128)(2,1)} %fusion.28) | data formatting | bytes 50331648 | tf_op jit(solution)/shard_map/brBc,bBcd->bBrd/dot_general | solution.py:46
  480.9 9.9 %fusion.23 = f32[1,128,32,192]{1,0,3,2:T(1,128)S(1)} fusion(bf16[128,16,32,192]{0,1,3,2:T(8,128)(2,1)} %copy.42, f32[1,16]{1,0:T(1,128)S(1)} %fusion.16), kind=kOutput, calls=%fused_computation.35 | convolution fusion | flops 25165824 | bytes 28311616 | tf_op jit(solution)/shard_map/bBrd,B->brd/dot_general | solution.py:47
  490.9 1.2 convert_element_type.28
  492.1 1.4 convert_element_type.30
  493.5 0.0 reduce-scatter.2.cloned.1.call-done
  493.5 41.7 %psum.7 = f32[32,128]{1,0:T(8,128)S(1)} all-reduce(f32[32,128]{1,0:T(8,128)} %reduce-scatter.2.cloned.1.call-done), channel_id=1, replica_groups=mesh['dp'=8,'field'=16] {'dp'}, use_global_device_ids=true, to_apply=%region_1.2 | all-reduce | flops 4096 | bytes 32768 | tf_op jit(solution)/shard_map/psum | solution.py:51
  535.2 0.6 broadcast_multiply_fusion
  (4 shorter events, 0.0 us)
Async XLA Ops:
  7.2 97.4 %copy-start.2 = (bf16[32,128]{1,0:T(8,128)(2,1)S(1)}, bf16[32,128]{1,0:T(8,128)(2,1)}, u32[]{:S(2)}) copy-start(bf16[32,128]{1,0:T(8,128)(2,1)} %param.6) | copy-start | bytes 24580
  7.2 97.4 %all-gather.6.cloned.1.call-start = ((), (), s32[]{:S(2)}) async-start(), calls=%async_computation.2 | async-start | bytes 17825792 | tf_op jit(solution)/shard_map/all_gather | solution.py:32
  7.9 269.9 %all-gather.4.cloned.1.call-start = ((), (), s32[]{:S(2)}) async-start(), calls=%async_computation.1 | async-start | bytes 35651584 | tf_op jit(solution)/shard_map/all_gather | solution.py:31
  12.5 481.0 %reduce-scatter.2.cloned.1.call-start = ((), (), s32[]{:S(2)}) async-start(), calls=%async_computation.3 | async-start | bytes 278528 | tf_op jit(solution)/shard_map/reduce_scatter | solution.py:50
  117.1 160.7 %copy-start = (bf16[128,32,192]{2,1,0:T(8,128)(2,1)S(1)}, bf16[128,32,192]{2,1,0:T(8,128)(2,1)}, u32[]{:S(2)}) copy-start(bf16[128,32,192]{2,1,0:T(8,128)(2,1)} %copy.26) | copy-start | bytes 4718596
  337.3 15.9 %copy-start.1 = (bf16[128,32,128]{2,1,0:T(8,128)(2,1)S(1)}, bf16[128,32,128]{2,1,0:T(8,128)(2,1)}, u32[]{:S(2)}) copy-start(bf16[128,32,128]{2,1,0:T(8,128)(2,1)} %param.7) | copy-start | bytes 3145732
Sparse Core Ops, SparseCore 0:
  9.7 94.8 all-gather.5
  106.2 171.6 all-gather.3
  357.5 61.3 reduce-scatter.1
where the time goes:
time: 544 us; the launch traced here: 542 us
  local copies, waits for them, and re-layouts  167 us (31%)
  waiting for transfers between devices  159 us (29%)
  matrix products  105 us (19%)
  blocking collectives  93.2 us (17%)
  between operations  14.5 us (3%)
    all_gather x1, waiting for transfers between devices, per_device(): lax.all_gather(emb, 'field', axis=1, tiled=True)  129 us
    dot_general x1, local copies, waits for them, and re-layouts, per_device(): jnp.einsum('brBc,bBcd->bBrd', sym_tiles, feat_tiles, preferred_element_ty...  96.3 us
    psum x1, blocking collectives, per_device(): weight_grad = lax.psum(own_tile, 'dp') / (samp_rows * lax.axis_size('dp'))  41.7 us
    all_gather x1, waiting for transfers between devices, per_device(): lax.all_gather(cot, 'field', axis=1, tiled=True)  28.7 us
    dot_general x1, matrix products, per_device(): jnp.einsum('brBc,bBcd->bBrd', sym_tiles, feat_tiles, preferred_element_ty...  27.3 us
    reshape x1, local copies, waits for them, and re-layouts, per_device(): sym_tiles = sym.reshape(samp_rows, tile, fields, tile)  23.1 us
    reshape x1, local copies, waits for them, and re-layouts, per_device(): gram_tiles = gram.reshape(samp_rows, tile, fields, tile)  23.1 us
    all_gather x1, blocking collectives, per_device(): weights = lax.all_gather(comp, 'field', axis=0, tiled=True)  22 us
  transfers between devices with their start and end apart: 3, of which 2 were waited for; matrix products, arithmetic and copies ran while one was open for 36% of the time, Pallas kernels for 0%

commit v1 on v0

v1 whole, which is shorter than its diff:
```python
import functools

import jax
import jax.numpy as jnp
from jax import lax
from jax.experimental import pallas as pl
from jax.experimental.pallas import tpu as pltpu
from jax.sharding import PartitionSpec as P

LANES = 128
VMEM_LIMIT = 56 * 1024 * 1024


def identity():
    shape = (LANES, LANES)
    same = lax.broadcasted_iota(jnp.int32, shape, 0) == lax.broadcasted_iota(jnp.int32, shape, 1)
    return jnp.where(same, 1.0, 0.0).astype(jnp.bfloat16)


def pack_kernel(emb_ref, cot_ref, comp_ref, pairs_ref, counts_ref, out_ref, turned):
    tile, width, samples = emb_ref.shape
    fields = out_ref.shape[0]
    per_peer = samples // fields
    half = tile // 2
    rows = 2 * tile + half
    f32, bf16 = jnp.float32, jnp.bfloat16
    eye = identity()
    turn = (((1,), (1,)), ((), ()))
    for r in range(tile + half):
        if r < tile:
            block = emb_ref[r, :LANES]
        else:
            block = jnp.concatenate([emb_ref[r - tile, LANES:], emb_ref[r - half, LANES:]], axis=0)
        turned[r * samples : (r + 1) * samples] = lax.dot_general(
            eye, block, turn, preferred_element_type=f32
        )

    slots = pairs_ref.shape[1]
    number = lax.broadcasted_iota(jnp.int32, (LANES, slots), 0)
    live = lax.broadcasted_iota(jnp.int32, (LANES, slots), 1) < counts_ref[0]
    first = jnp.where((pairs_ref[0:1] == number) & live, 1.0, 0.0).astype(bf16)
    second = jnp.where(pairs_ref[1:2] == number, 1.0, 0.0).astype(bf16)
    table = lax.dot_general(first, second, turn, preferred_element_type=f32)[:16].astype(bf16)

    def peer(p, carry):
        for s in range(per_peer):
            number = p * per_peer + s
            both = turned[pl.ds(number, tile + half, stride=samples), :].astype(bf16)
            base = s * rows
            out_ref[p, base : base + tile] = both[:tile]
            out_ref[p, base + tile : base + 2 * tile] = cot_ref[number]
            out_ref[p, base + 2 * tile : base + rows] = both[tile:]
        base = per_peer * rows
        out_ref[p, base : base + tile] = comp_ref[...]
        out_ref[p, base + tile : base + tile + 16] = table
        return carry

    lax.fori_loop(0, fields, peer, 0)


def block_kernel(per_peer, scale, x_ref, y_ref, emb, sides, other, mask, grad):
    fields = x_ref.shape[0]
    tile = 32
    half, rest = tile // 2, emb.shape[1] - LANES
    rows = 2 * tile + half
    embeds = fields * tile
    f32, bf16 = jnp.float32, jnp.bfloat16
    base = per_peer * rows

    table = jnp.zeros((16, LANES), f32)
    for f in range(fields):
        table += x_ref[f, base + tile : base + tile + 16].astype(f32)
    square = jnp.concatenate([table, jnp.zeros((LANES - 16, LANES), f32)], axis=0)
    on_diag = lax.broadcasted_iota(jnp.int32, square.shape, 0) == lax.broadcasted_iota(
        jnp.int32, square.shape, 1
    )
    mult = (square + square.T - jnp.where(on_diag, square, 0.0)) * scale
    for a in range(fields):
        row = jnp.concatenate(
            [jnp.broadcast_to(mult[a : a + 1, b : b + 1], (1, tile)) for b in range(fields)], axis=1
        )
        mask[a * tile : (a + 1) * tile] = jnp.broadcast_to(row, (tile, embeds))

    weights = x_ref[:, base : base + tile].reshape(embeds, LANES)
    sides[:, :LANES] = weights
    other[:, LANES:] = weights
    grad[...] = jnp.zeros_like(grad)
    lane = lax.broadcasted_iota(jnp.int32, (fields, half, LANES), 2)

    def sample(s, carry):
        start = pl.multiple_of(s * rows, 16)
        emb[:, :LANES] = x_ref[:, pl.ds(start, tile)].reshape(embeds, LANES)
        cot = x_ref[:, pl.ds(start + tile, tile)].reshape(embeds, LANES)
        sides[:, LANES:] = cot
        other[:, :LANES] = cot
        tail = x_ref[:, pl.ds(start + 2 * tile, half)]
        upper = jnp.concatenate([tail[:, :, rest:], tail[:, :, :rest]], axis=2)
        both = jnp.concatenate([tail, upper], axis=1).reshape(embeds, LANES)
        emb[:, LANES:] = both[:, :rest]
        feats = emb[...]
        gram = lax.dot_general(feats, feats, (((1,), (1,)), ((), ())), preferred_element_type=f32)
        masked = (mask[...] * gram).astype(bf16)
        both = jnp.dot(masked, sides[...], preferred_element_type=f32)
        grad[...] += both[:, LANES:]
        y_ref[:, pl.ds(start, tile)] = both[:, :LANES].astype(bf16).reshape(fields, tile, LANES)
        hmat = lax.dot_general(
            other[...], sides[...], (((1,), (1,)), ((), ())), preferred_element_type=f32
        )
        sym = (mask[...] * hmat).astype(bf16)
        dfeat = jnp.dot(sym, feats, preferred_element_type=f32).astype(bf16)
        y_ref[:, pl.ds(start + tile, tile)] = dfeat[:, :LANES].reshape(fields, tile, LANES)
        last = dfeat[:, LANES:].reshape(fields, tile, rest)
        y_ref[:, pl.ds(start + 2 * tile, half)] = jnp.concatenate(
            [last[:, :half], last[:, half:]], axis=2
        )
        return carry

    lax.fori_loop(0, per_peer, sample, 0)
    y_ref[:, base : base + tile] = grad[...].astype(bf16).reshape(fields, tile, LANES)


def unpack_kernel(y_ref, mixed_ref, dfeat_ref, turned):
    tile, width, samples = dfeat_ref.shape
    fields = y_ref.shape[0]
    per_peer = samples // fields
    half, rest = tile // 2, width - LANES
    rows = 2 * tile + half
    f32, bf16 = jnp.float32, jnp.bfloat16

    def peer(p, carry):
        for s in range(per_peer):
            number = p * per_peer + s
            base = s * rows
            mixed_ref[number] = y_ref[p, base : base + tile]
            turned[pl.ds(number, tile + half, stride=samples), :] = y_ref[
                p, base + tile : base + rows
            ].astype(f32)
        return carry

    lax.fori_loop(0, fields, peer, 0)
    eye = identity()
    for r in range(tile + half):
        block = turned[r * samples : (r + 1) * samples].astype(bf16)
        block = lax.dot_general(
            block, eye, (((0,), (0,)), ((), ())), preferred_element_type=f32
        ).astype(bf16)
        if r < tile:
            dfeat_ref[r, :LANES] = block
        else:
            dfeat_ref[r - tile, LANES:] = block[:rest]
            dfeat_ref[r - half, LANES:] = block[rest:]


def dp_sum(x):
    size = lax.axis_size("dp")
    total = x
    for k in range(1, size):
        total = total + lax.ppermute(x, "dp", [(i, i ^ k) for i in range(size)])
    return total


def per_device(emb, comp, cot, pairs, counts):
    samp_rows, tile, width = emb.shape
    fields = lax.axis_size("field")
    per_peer = samp_rows // fields
    embeds = tile * fields
    packed = tile + tile // 2
    rows = packed + tile
    f32, bf16 = jnp.float32, jnp.bfloat16
    params = pltpu.CompilerParams(vmem_limit_bytes=VMEM_LIMIT)
    vmem = pl.BlockSpec(memory_space=pltpu.VMEM)
    sent = per_peer * rows + tile + 16
    back = per_peer * rows + tile
    x = pl.pallas_call(
        pack_kernel,
        out_shape=jax.ShapeDtypeStruct((fields, sent, LANES), bf16),
        in_specs=[vmem, vmem, vmem, vmem, pl.BlockSpec(memory_space=pltpu.SMEM)],
        out_specs=vmem,
        scratch_shapes=[pltpu.VMEM((packed * samp_rows, LANES), f32)],
        compiler_params=params,
    )(jnp.transpose(emb, (1, 2, 0)), cot, comp, pairs.T, counts)
    x = lax.all_to_all(x, "field", 0, 0)
    y = pl.pallas_call(
        functools.partial(block_kernel, per_peer, width ** (-0.5)),
        out_shape=jax.ShapeDtypeStruct((fields, back, LANES), bf16),
        in_specs=[vmem],
        out_specs=vmem,
        scratch_shapes=[
            pltpu.VMEM((embeds, width), bf16),
            pltpu.VMEM((embeds, 2 * LANES), bf16),
            pltpu.VMEM((embeds, 2 * LANES), bf16),
            pltpu.VMEM((embeds, embeds), f32),
            pltpu.VMEM((embeds, LANES), f32),
        ],
        compiler_params=params,
    )(x)
    y = lax.all_to_all(y, "field", 0, 0)
    grad = dp_sum(jnp.sum(y[:, per_peer * rows :].astype(f32), axis=0))
    mixed, emb_grad = pl.pallas_call(
        unpack_kernel,
        out_shape=(
            jax.ShapeDtypeStruct((samp_rows, tile, LANES), bf16),
            jax.ShapeDtypeStruct((tile, width, samp_rows), bf16),
        ),
        in_specs=[vmem],
        out_specs=(vmem, vmem),
        scratch_shapes=[pltpu.VMEM((packed * samp_rows, LANES), f32)],
        compiler_params=params,
        cost_estimate=pl.CostEstimate(flops=10**9, bytes_accessed=6 * 10**6, transcendentals=0),
    )(y)
    weight_grad = grad / (samp_rows * lax.axis_size("dp"))
    return mixed, jnp.transpose(emb_grad, (2, 0, 1)), weight_grad


def solution(mesh):
    in_specs = (
        P("dp", "field", None),
        P("field", None),
        P("dp", "field", None),
        P("field", None),
        P("field"),
    )
    out_specs = (P("dp", "field", None), P("dp", "field", None), P("field", None))
    return jax.shard_map(
        per_device, mesh=mesh, in_specs=in_specs, out_specs=out_specs, check_vma=False
    )
```

time: 544 us -> 122 us (0.22)
  local copies, waits for them, and re-layouts: 167 us -> 0.01 us
  waiting for transfers between devices: 159 us -> 0.02 us
  matrix products: 105 us -> 0 us
  Pallas kernels: 0 us -> 25.1 us
  starting transfers between devices: 0.12 us -> 13.6 us
  between operations: 14.5 us -> 1.31 us
  blocking collectives: 93.2 us -> 80.6 us
    all_gather x2 -> x0, waiting for transfers between devices: 158 us -> none  [the longest x1 129 us: per_device(): lax.all_gather(emb, 'field', axis=1, tiled=True)]
    dot_general x9 -> x0, matrix products: 105 us -> none  [the longest x1 27.3 us: per_device(): jnp.einsum('brBc,bBcd->bBrd', sym_tiles, feat_tiles, preferred_element_ty...]
    dot_general x2 -> x0, local copies, waits for them, and re-layouts: 96.3 us -> none  [the longest x1 96.3 us: per_device(): jnp.einsum('brBc,bBcd->bBrd', sym_tiles, feat_tiles, preferred_element_ty...]
    all_to_all x0 -> x2, blocking collectives: none -> 80.6 us  [the longest x1 42.1 us: per_device(): x = lax.all_to_all(x, 'field', 0, 0)]
    reshape x2 -> x0, local copies, waits for them, and re-layouts: 46.2 us -> none  [the longest x1 23.1 us: per_device(): sym_tiles = sym.reshape(samp_rows, tile, fields, tile)]
    all_gather x2 -> x0, blocking collectives: 43.3 us -> none  [the longest x1 22 us: per_device(): weights = lax.all_gather(comp, 'field', axis=0, tiled=True)]
    psum x1 -> x0, blocking collectives: 41.7 us -> none  [per_device(): weight_grad = lax.psum(own_tile, 'dp') / (samp_rows * lax.axis_size('dp'))]
    pallas_call x0 -> x3, Pallas kernels: none -> 25.1 us  [the longest x1 11.8 us: per_device(): pl.pallas_call(functools.partial(block_kernel, per_peer, width ** (-0.5))...]
  transfers between devices with their start and end apart: 3 -> 7, of which waited for: 2 -> 0; matrix products, arithmetic and copies ran while one was open for 36% -> 0% of each run, Pallas kernels for 0% -> 6%
where the time goes in v1:
time: 122 us; the launch traced here: 121 us
  blocking collectives  80.6 us (66%)
  Pallas kernels  25.1 us (21%)
  starting transfers between devices  13.6 us (11%)
  between operations  1.31 us (1%)
    all_to_all x1, blocking collectives, per_device(): x = lax.all_to_all(x, 'field', 0, 0)  42.1 us
    all_to_all x1, blocking collectives, per_device(): y = lax.all_to_all(y, 'field', 0, 0)  38.5 us
    ppermute x7, starting transfers between devices, dp_sum(): total = total + lax.ppermute(x, 'dp', [(i, i ^ k) for i in range(size)])  13.6 us
    pallas_call x1, Pallas kernels, per_device(): pl.pallas_call(functools.partial(block_kernel, per_peer, width ** (-0.5))...  11.8 us
    pallas_call x1, Pallas kernels, per_device(): pl.pallas_call(unpack_kernel, out_shape=(jax.ShapeDtypeStruct((samp_rows,...  6.68 us
    pallas_call x1, Pallas kernels, per_device(): pl.pallas_call(pack_kernel, out_shape=jax.ShapeDtypeStruct((fields, sent,...  6.58 us
  transfers between devices with their start and end apart: 7, of which 0 were waited for; matrix products, arithmetic and copies ran while one was open for 0% of the time, Pallas kernels for 6%

profile of v1, /device:TPU:0, one launch (start us, length us, event | category | flops | bytes accessed | tf_op | source)
XLA Modules:
  0.0 121.3 jit_solution(6317642751643169699)
XLA Ops:
  1.3 6.6 %shard_map.76 = bf16[16,688,128]{2,1,0:T(8,128)(2,1)} custom-call(bf16[32,192,128]{2,1,0:T(8,128)(2,1)} %bitcast.3, bf16[128,32,128]{2,1,0:T(8,128)(2,1)} %cot_ref.1, bf16[32,128]{1,0:T(8,128)(2,1)} %comp_ref.1, s32[2,72]{1,0:T(2,128)} %bitcast.4, s32[1]{0:T(128)S(6)} %copy.8.counts_ref), custom_call_target="tpu_custom_call" | custom-call | tf_op jit(solution)/shard_map/pallas_call | solution.py:174
  7.9 42.1 %all_to_all.10.x_ref = bf16[16,688,128]{2,1,0:T(8,128)(2,1)} all-to-all(bf16[16,688,128]{2,1,0:T(8,128)(2,1)} %shard_map.76), channel_id=1, replica_groups=mesh['dp'=8,'field'=16] {'field'}, dimensions={0} | all-to-all | bytes 5636096 | tf_op jit(solution)/shard_map/all_to_all | solution.py:182
  49.9 11.8 %shard_map.77 = bf16[16,672,128]{2,1,0:T(8,128)(2,1)} custom-call(bf16[16,688,128]{2,1,0:T(8,128)(2,1)} %all_to_all.10.x_ref), custom_call_target="tpu_custom_call" | custom-call | tf_op jit(solution)/shard_map/pallas_call | solution.py:183
  61.7 38.5 %all_to_all.11.y_ref = bf16[16,672,128]{2,1,0:T(8,128)(2,1)S(1)} all-to-all(bf16[16,672,128]{2,1,0:T(8,128)(2,1)} %shard_map.77), channel_id=1, replica_groups=mesh['dp'=8,'field'=16] {'field'}, dimensions={0} | all-to-all | bytes 5505024 | tf_op jit(solution)/shard_map/all_to_all | solution.py:197
  100.3 0.0 copy-start
  100.3 5.2 %collective-permute-start.6 = (f32[32,128]{1,0:T(8,128)S(1)}, f32[32,128]{1,0:T(8,128)S(1)}, u32[]{:S(2)}, u32[]{:S(2)}) collective-permute-start(f32[32,128]{1,0:T(8,128)S(1)} %convert_reduce_fusion), channel_id=1, source_target_pairs={{0,112},{16,96},{32,80},{48,64},{64,48},{80,32},{96,16},{112,0},{1... | collective-permute-start | bytes 49160 | tf_op jit(solution)/shard_map/ppermute | solution.py:158
  105.5 0.9 collective-permute-start.5
  106.3 2.9 %collective-permute-start.4 = (f32[32,128]{1,0:T(8,128)S(1)}, f32[32,128]{1,0:T(8,128)S(1)}, u32[]{:S(2)}, u32[]{:S(2)}) collective-permute-start(f32[32,128]{1,0:T(8,128)S(1)} %convert_reduce_fusion), channel_id=1, source_target_pairs={{0,80},{16,64},{32,112},{48,96},{64,16},{80,0},{96,48},{112,32},{1... | collective-permute-start | bytes 49160 | tf_op jit(solution)/shard_map/ppermute | solution.py:158
  109.2 0.6 collective-permute-start.3
  109.8 2.8 %collective-permute-start.2 = (f32[32,128]{1,0:T(8,128)S(1)}, f32[32,128]{1,0:T(8,128)S(1)}, u32[]{:S(2)}, u32[]{:S(2)}) collective-permute-start(f32[32,128]{1,0:T(8,128)S(1)} %convert_reduce_fusion), channel_id=1, source_target_pairs={{0,48},{16,32},{32,16},{48,0},{64,112},{80,96},{96,80},{112,64},{1... | collective-permute-start | bytes 49160 | tf_op jit(solution)/shard_map/ppermute | solution.py:158
  112.6 0.0 collective-permute-done.6
  112.6 0.8 collective-permute-start.1
  113.4 0.0 collective-permute-done.5
  113.4 0.5 collective-permute-start
  113.9 0.0 copy-done
  113.9 6.7 %shard_map.78 = (bf16[128,32,128]{2,1,0:T(8,128)(2,1)}, bf16[32,192,128]{2,1,0:T(8,128)(2,1)}) custom-call(bf16[16,672,128]{2,1,0:T(8,128)(2,1)} %copy-done), custom_call_target="tpu_custom_call" | custom-call | flops 1000000000 | bytes 6000000 | tf_op jit(solution)/shard_map/pallas_call | solution.py:199
  120.6 0.0 collective-permute-done.4
  120.6 0.0 collective-permute-done.3
  120.6 0.0 collective-permute-done.2
  120.6 0.0 collective-permute-done.1
  120.6 0.0 collective-permute-done
  120.6 0.6 add_multiply_fusion
  (1 shorter events, 0.0 us)
Async XLA Ops:
  100.3 13.7 %copy-start = (bf16[16,672,128]{2,1,0:T(8,128)(2,1)}, bf16[16,672,128]{2,1,0:T(8,128)(2,1)S(1)}, u32[]{:S(2)}) copy-start(bf16[16,672,128]{2,1,0:T(8,128)(2,1)S(1)} %all_to_all.11.y_ref) | copy-start | bytes 8257540
  100.3 12.3 %collective-permute-start.6 = (f32[32,128]{1,0:T(8,128)S(1)}, f32[32,128]{1,0:T(8,128)S(1)}, u32[]{:S(2)}, u32[]{:S(2)}) collective-permute-start(f32[32,128]{1,0:T(8,128)S(1)} %convert_reduce_fusion), channel_id=1, source_target_pairs={{0,112},{16,96},{32,80},{48,64},{64,48},{80,32},{96,16},{112,0},{1... | collective-permute-start | bytes 49160 | tf_op jit(solution)/shard_map/ppermute | solution.py:158
  105.5 7.9 %collective-permute-start.5 = (f32[32,128]{1,0:T(8,128)S(1)}, f32[32,128]{1,0:T(8,128)S(1)}, u32[]{:S(2)}, u32[]{:S(2)}) collective-permute-start(f32[32,128]{1,0:T(8,128)S(1)} %convert_reduce_fusion), channel_id=1, source_target_pairs={{0,96},{16,112},{32,64},{48,80},{64,32},{80,48},{96,0},{112,16},{1... | collective-permute-start | bytes 49160 | tf_op jit(solution)/shard_map/ppermute | solution.py:158
  106.3 14.3 %collective-permute-start.4 = (f32[32,128]{1,0:T(8,128)S(1)}, f32[32,128]{1,0:T(8,128)S(1)}, u32[]{:S(2)}, u32[]{:S(2)}) collective-permute-start(f32[32,128]{1,0:T(8,128)S(1)} %convert_reduce_fusion), channel_id=1, source_target_pairs={{0,80},{16,64},{32,112},{48,96},{64,16},{80,0},{96,48},{112,32},{1... | collective-permute-start | bytes 49160 | tf_op jit(solution)/shard_map/ppermute | solution.py:158
  109.2 11.4 %collective-permute-start.3 = (f32[32,128]{1,0:T(8,128)S(1)}, f32[32,128]{1,0:T(8,128)S(1)}, u32[]{:S(2)}, u32[]{:S(2)}) collective-permute-start(f32[32,128]{1,0:T(8,128)S(1)} %convert_reduce_fusion), channel_id=1, source_target_pairs={{0,64},{16,80},{32,96},{48,112},{64,0},{80,16},{96,32},{112,48},{1... | collective-permute-start | bytes 49160 | tf_op jit(solution)/shard_map/ppermute | solution.py:158
  109.8 10.8 %collective-permute-start.2 = (f32[32,128]{1,0:T(8,128)S(1)}, f32[32,128]{1,0:T(8,128)S(1)}, u32[]{:S(2)}, u32[]{:S(2)}) collective-permute-start(f32[32,128]{1,0:T(8,128)S(1)} %convert_reduce_fusion), channel_id=1, source_target_pairs={{0,48},{16,32},{32,16},{48,0},{64,112},{80,96},{96,80},{112,64},{1... | collective-permute-start | bytes 49160 | tf_op jit(solution)/shard_map/ppermute | solution.py:158
  112.6 8.0 %collective-permute-start.1 = (f32[32,128]{1,0:T(8,128)S(1)}, f32[32,128]{1,0:T(8,128)S(1)}, u32[]{:S(2)}, u32[]{:S(2)}) collective-permute-start(f32[32,128]{1,0:T(8,128)S(1)} %convert_reduce_fusion), channel_id=1, source_target_pairs={{0,32},{16,48},{32,0},{48,16},{64,96},{80,112},{96,64},{112,80},{1... | collective-permute-start | bytes 49160 | tf_op jit(solution)/shard_map/ppermute | solution.py:158
  113.4 7.2 %collective-permute-start = (f32[32,128]{1,0:T(8,128)S(1)}, f32[32,128]{1,0:T(8,128)S(1)}, u32[]{:S(2)}, u32[]{:S(2)}) collective-permute-start(f32[32,128]{1,0:T(8,128)S(1)} %convert_reduce_fusion), channel_id=1, source_target_pairs={{0,16},{16,0},{32,48},{48,32},{64,80},{80,64},{96,112},{112,96},{1... | collective-permute-start | bytes 49160 | tf_op jit(solution)/shard_map/ppermute | solution.py:158

commit v2 on v0

v2 whole, which is shorter than its diff:
```python
import functools

import jax
import jax.numpy as jnp
from jax import lax
from jax.experimental import pallas as pl
from jax.experimental.pallas import tpu as pltpu
from jax.sharding import PartitionSpec as P

LANES = 128
CHUNKS = 1
TABLE = 16
TURN = (((1,), (1,)), ((), ()))
MIB = 1024 * 1024


def pack_kernel(chunk, emb_ref, cot_ref, *refs):
    *extras, out_ref, turned = refs
    tile, width, samples = emb_ref.shape
    fields = out_ref.shape[0]
    step = samples // CHUNKS
    each = step // fields
    half = tile // 2
    rows = 2 * tile + half
    f32, bf16 = jnp.float32, jnp.bfloat16
    lanes = slice(chunk * step, (chunk + 1) * step)
    for r in range(tile + half):
        if r < tile:
            block = emb_ref[r, :LANES]
        else:
            block = jnp.concatenate([emb_ref[r - tile, LANES:], emb_ref[r - half, LANES:]], axis=0)
        turned[r * step : (r + 1) * step] = block.astype(f32).T[lanes]

    def peer(p, carry):
        for j in range(each):
            number = p * each + j
            both = turned[pl.ds(number, tile + half, stride=step), :].astype(bf16)
            base = j * rows
            out_ref[p, base : base + tile] = both[:tile]
            out_ref[p, base + tile : base + 2 * tile] = cot_ref[number]
            out_ref[p, base + 2 * tile : base + rows] = both[tile:]
        return carry

    lax.fori_loop(0, fields, peer, 0)
    if chunk == 0:
        comp_ref, pairs_ref, counts_ref = extras
        slots = pairs_ref.shape[1]
        number = lax.broadcasted_iota(jnp.int32, (LANES, slots), 0)
        live = lax.broadcasted_iota(jnp.int32, (LANES, slots), 1) < counts_ref[0]
        first = jnp.where((pairs_ref[0:1] == number) & live, 1.0, 0.0).astype(bf16)
        second = jnp.where(pairs_ref[1:2] == number, 1.0, 0.0).astype(bf16)
        table = lax.dot_general(first, second, TURN, preferred_element_type=f32)
        base = each * rows
        for p in range(fields):
            out_ref[p, base : base + tile] = comp_ref[...]
            out_ref[p, base + tile : base + tile + TABLE] = table[:TABLE].astype(bf16)


def pair_mask(x_ref, base, scale, mask, tile):
    fields = x_ref.shape[0]
    f32 = jnp.float32
    table = jnp.zeros((TABLE, LANES), f32)
    for f in range(fields):
        table += x_ref[f, base : base + TABLE].astype(f32)
    square = jnp.concatenate([table, jnp.zeros((LANES - TABLE, LANES), f32)], axis=0)
    on_diag = lax.broadcasted_iota(jnp.int32, square.shape, 0) == lax.broadcasted_iota(
        jnp.int32, square.shape, 1
    )
    mult = (square + square.T - jnp.where(on_diag, square, 0.0)) * scale
    for a in range(fields):
        row = jnp.concatenate(
            [jnp.broadcast_to(mult[a : a + 1, b : b + 1], (1, tile)) for b in range(fields)], axis=1
        )
        mask[a * tile : (a + 1) * tile] = jnp.broadcast_to(row, (tile, row.shape[1]))


def block_kernel(chunk, scale, tile, width, x_ref, *refs):
    fields = x_ref.shape[0]
    half, rest = tile // 2, width - LANES
    rows = 2 * tile + half
    embeds = fields * tile
    f32, bf16 = jnp.float32, jnp.bfloat16
    emb, sides, other = refs[-3:]
    if chunk == 0:
        y_ref, mask, weights, grad = refs[:-3]
        each = (x_ref.shape[1] - tile - TABLE) // rows
        base = each * rows
        pair_mask(x_ref, base + tile, scale, mask, tile)
        weights[...] = x_ref[:, base : base + tile].reshape(embeds, LANES)
        grad[...] = jnp.zeros_like(grad)
    else:
        mask, weights, grad, y_ref = refs[:-3]
        each = x_ref.shape[1] // rows
    sides[:, :LANES] = weights[...]
    other[:, LANES:] = weights[...]

    def sample(j, total):
        start = pl.multiple_of(j * rows, 16)
        emb[:, :LANES] = x_ref[:, pl.ds(start, tile)].reshape(embeds, LANES)
        cot = x_ref[:, pl.ds(start + tile, tile)].reshape(embeds, LANES)
        sides[:, LANES:] = cot
        other[:, :LANES] = cot
        tail = x_ref[:, pl.ds(start + 2 * tile, half)]
        upper = jnp.concatenate([tail[:, :, rest:], tail[:, :, :rest]], axis=2)
        both = jnp.concatenate([tail, upper], axis=1).reshape(embeds, LANES)
        emb[:, LANES:] = both[:, :rest]
        feats = emb[...]
        gram = lax.dot_general(feats, feats, TURN, preferred_element_type=f32)
        masked = (mask[...] * gram).astype(bf16)
        both = jnp.dot(masked, sides[...], preferred_element_type=f32)
        grad[...] += both[:, LANES:]
        y_ref[:, pl.ds(start, tile)] = both[:, :LANES].astype(bf16).reshape(fields, tile, LANES)
        hmat = lax.dot_general(other[...], sides[...], TURN, preferred_element_type=f32)
        sym = (mask[...] * hmat).astype(bf16)
        dfeat = jnp.dot(sym, feats, preferred_element_type=f32).astype(bf16)
        y_ref[:, pl.ds(start + tile, tile)] = dfeat[:, :LANES].reshape(fields, tile, LANES)
        last = dfeat[:, LANES:].reshape(fields, tile, rest)
        y_ref[:, pl.ds(start + 2 * tile, half)] = jnp.concatenate(
            [last[:, :half], last[:, half:]], axis=2
        )
        return total

    lax.fori_loop(0, each, sample, 0)
    if chunk == CHUNKS - 1:
        y_ref[:, each * rows :] = grad[...].astype(bf16).reshape(fields, tile, LANES)


def unpack_kernel(chunk, y_ref, *refs):
    *before, mixed_ref, dfeat_ref, turned = refs
    tile, width, samples = dfeat_ref.shape
    fields = y_ref.shape[0]
    step = samples // CHUNKS
    each = step // fields
    half, rest = tile // 2, width - LANES
    rows = 2 * tile + half
    f32, bf16 = jnp.float32, jnp.bfloat16

    def peer(p, carry):
        for j in range(each):
            number = p * each + j
            base = j * rows
            mixed_ref[number] = y_ref[p, base : base + tile]
            turned[pl.ds(number, tile + half, stride=step), :] = y_ref[
                p, base + tile : base + rows
            ].astype(f32)
        return carry

    lax.fori_loop(0, fields, peer, 0)
    for r in range(tile + half):
        block = turned[r * step : (r + 1) * step].T.astype(bf16)
        pieces = (
            [(r, slice(0, LANES), block)]
            if r < tile
            else [
                (r - tile, slice(LANES, width), block[:rest]),
                (r - half, slice(LANES, width), block[rest:]),
            ]
        )
        for row, part, piece in pieces:
            if chunk > 0:
                piece = jnp.concatenate([before[1][row, part, : chunk * step], piece], axis=1)
            dfeat_ref[row, part, : (chunk + 1) * step] = piece


def dp_sum(x):
    size = lax.axis_size("dp")
    copies = lax.optimization_barrier(jnp.broadcast_to(x, (size,) + x.shape))
    return jnp.sum(lax.all_to_all(copies, "dp", 0, 0), axis=0)


def per_device(emb, comp, cot, pairs, counts):
    samp_rows, tile, width = emb.shape
    fields = lax.axis_size("field")
    embeds = tile * fields
    packed = tile + tile // 2
    rows = packed + tile
    step = samp_rows // CHUNKS
    each = step // fields
    f32, bf16 = jnp.float32, jnp.bfloat16
    params = pltpu.CompilerParams(vmem_limit_bytes=24 * MIB)
    vmem = pl.BlockSpec(memory_space=pltpu.VMEM)
    smem = pl.BlockSpec(memory_space=pltpu.SMEM)
    turned = pltpu.VMEM((packed * step, LANES), f32)
    emb = jnp.transpose(emb, (1, 2, 0))
    whole_emb = pl.BlockSpec(emb.shape, lambda i: (0, 0, 0))

    def part_of(chunk):
        return pl.BlockSpec((step, tile, LANES), lambda i: (chunk, 0, 0))

    def cost(flops, moved):
        return pl.CostEstimate(flops=flops, bytes_accessed=moved, transcendentals=0)

    sent = []
    for chunk in range(CHUNKS):
        first = chunk == 0
        message = (fields, each * rows + (tile + TABLE if first else 0), LANES)
        sent.append(
            pl.pallas_call(
                functools.partial(pack_kernel, chunk),
                grid=(1,),
                out_shape=jax.ShapeDtypeStruct(message, bf16),
                in_specs=[whole_emb, part_of(chunk)] + ([vmem, vmem, smem] if first else []),
                out_specs=pl.BlockSpec(message, lambda i: (0, 0, 0)),
                scratch_shapes=[turned],
                compiler_params=params,
                cost_estimate=cost(10**9, 8 * 10**6),
            )(emb, cot, *([comp, pairs.T, counts] if first else []))
        )
    kept = [
        jax.ShapeDtypeStruct((embeds, embeds), f32),
        jax.ShapeDtypeStruct((embeds, LANES), bf16),
        jax.ShapeDtypeStruct((embeds, LANES), f32),
    ]
    state, back = None, []
    for chunk in range(CHUNKS):
        first, last = chunk == 0, chunk == CHUNKS - 1
        x = lax.all_to_all(sent[chunk], "field", 0, 0)
        message = (fields, each * rows + (tile if last else 0), LANES)
        keep = kept if first and not last else []
        out = pl.pallas_call(
            functools.partial(block_kernel, chunk, width ** (-0.5), tile, width),
            out_shape=[jax.ShapeDtypeStruct(message, bf16)] + keep,
            in_specs=[vmem] + ([] if first else [vmem] * 3),
            out_specs=[vmem] * (1 + len(keep)),
            scratch_shapes=([pltpu.VMEM(k.shape, k.dtype) for k in kept] if first and last else [])
            + [
                pltpu.VMEM((embeds, width), bf16),
                pltpu.VMEM((embeds, 2 * LANES), bf16),
                pltpu.VMEM((embeds, 2 * LANES), bf16),
            ],
            compiler_params=params,
            cost_estimate=cost(4 * 10**9, 6 * 10**6),
        )(x, *([] if first else state))
        if first:
            state = out[1:]
        back.append(lax.all_to_all(out[0], "field", 0, 0))

    grad = dp_sum(jnp.sum(back[-1][:, each * rows :].astype(f32), axis=0))
    weight_grad = grad / (samp_rows * lax.axis_size("dp"))

    result = ()
    for chunk in range(CHUNKS):
        y = back[chunk]
        first = chunk == 0
        result = pl.pallas_call(
            functools.partial(unpack_kernel, chunk),
            grid=(1,),
            out_shape=(
                jax.ShapeDtypeStruct((samp_rows, tile, LANES), bf16),
                jax.ShapeDtypeStruct((tile, width, samp_rows), bf16),
            ),
            in_specs=[pl.BlockSpec(y.shape, lambda i: (0, 0, 0))]
            + ([] if first else [pl.BlockSpec(memory_space=pl.ANY), whole_emb]),
            out_specs=(part_of(chunk), whole_emb),
            input_output_aliases={} if first else {1: 0},
            scratch_shapes=[turned],
            compiler_params=params,
            cost_estimate=cost(10**9, 8 * 10**6),
        )(y, *result)
    mixed, emb_grad = result
    return mixed, jnp.transpose(emb_grad, (2, 0, 1)), weight_grad


def solution(mesh):
    in_specs = (
        P("dp", "field", None),
        P("field", None),
        P("dp", "field", None),
        P("field", None),
        P("field"),
    )
    out_specs = (P("dp", "field", None), P("dp", "field", None), P("field", None))
    return jax.shard_map(
        per_device, mesh=mesh, in_specs=in_specs, out_specs=out_specs, check_vma=False
    )
```

time: 544 us -> 112 us (0.21)
  local copies, waits for them, and re-layouts: 167 us -> 4.64 us
  waiting for transfers between devices: 159 us -> 3.32 us
  matrix products: 105 us -> 0 us
  Pallas kernels: 0 us -> 15.7 us
  blocking collectives: 93.2 us -> 79.3 us
  between operations: 14.5 us -> 1.31 us
  starting transfers between devices: 0.12 us -> 6.64 us
    all_gather x2 -> x0, waiting for transfers between devices: 158 us -> none  [the longest x1 129 us: per_device(): lax.all_gather(emb, 'field', axis=1, tiled=True)]
    dot_general x9 -> x0, matrix products: 105 us -> none  [the longest x1 27.3 us: per_device(): jnp.einsum('brBc,bBcd->bBrd', sym_tiles, feat_tiles, preferred_element_ty...]
    dot_general x2 -> x0, local copies, waits for them, and re-layouts: 96.3 us -> none  [the longest x1 96.3 us: per_device(): jnp.einsum('brBc,bBcd->bBrd', sym_tiles, feat_tiles, preferred_element_ty...]
    all_to_all x0 -> x2, blocking collectives: none -> 79.3 us  [the longest x1 41.9 us: per_device(): x = lax.all_to_all(sent[chunk], 'field', 0, 0)]
    reshape x2 -> x0, local copies, waits for them, and re-layouts: 46.2 us -> none  [the longest x1 23.1 us: per_device(): sym_tiles = sym.reshape(samp_rows, tile, fields, tile)]
    all_gather x2 -> x0, blocking collectives: 43.3 us -> none  [the longest x1 22 us: per_device(): weights = lax.all_gather(comp, 'field', axis=0, tiled=True)]
    psum x1 -> x0, blocking collectives: 41.7 us -> none  [per_device(): weight_grad = lax.psum(own_tile, 'dp') / (samp_rows * lax.axis_size('dp'))]
    convert_element_type x3 -> x0, local copies, waits for them, and re-layouts: 16.1 us -> none  [the longest x1 8.19 us: per_device(): sym = (scale * (hmat_rows + hmat_cols)).astype(jnp.bfloat16)]
  transfers between devices with their start and end apart: 3 -> 1, of which waited for: 2 -> 1; matrix products, arithmetic and copies ran while one was open for 36% -> 0% of each run, Pallas kernels for 0% -> 4%
where the time goes in v2:
time: 112 us
  blocking collectives  79.3 us (71%)
  Pallas kernels  15.7 us (14%)
  starting transfers between devices  6.64 us (6%)
  local copies, waits for them, and re-layouts  4.64 us (4%)
  waiting for transfers between devices  3.32 us (3%)
  between operations  1.31 us (1%)
    all_to_all x1, blocking collectives, per_device(): x = lax.all_to_all(sent[chunk], 'field', 0, 0)  41.9 us
    all_to_all x1, blocking collectives, per_device(): back.append(lax.all_to_all(out[0], 'field', 0, 0))  37.4 us
    pallas_call x1, Pallas kernels, per_device(): pl.pallas_call(functools.partial(block_kernel, chunk, width ** (-0.5), ti...  8.4 us
    all_to_all x1, starting transfers between devices, dp_sum(): return jnp.sum(lax.all_to_all(copies, 'dp', 0, 0), axis=0)  6.64 us
    pallas_call x1, Pallas kernels, per_device(): pl.pallas_call(functools.partial(unpack_kernel, chunk), grid=(1,), out_sh...  4.76 us
    unnamed x8, local copies, waits for them, and re-layouts  4 us
    all_to_all x1, waiting for transfers between devices, dp_sum(): return jnp.sum(lax.all_to_all(copies, 'dp', 0, 0), axis=0)  3.32 us
    pallas_call x1, Pallas kernels, per_device(): pl.pallas_call(functools.partial(pack_kernel, chunk), grid=(1,), out_shap...  2.55 us
  transfers between devices with their start and end apart: 1, of which 1 were waited for; matrix products, arithmetic and copies ran while one was open for 0% of the time, Pallas kernels for 4%

profile of v2, /device:TPU:0, one launch (start us, length us, event | category | flops | bytes accessed | tf_op | source)
XLA Modules:
  0.0 111.6 jit_solution(5432214821867544346)
XLA Ops:
  1.3 0.0 copy-start
  1.3 1.4 %copy-done = bf16[128,32,192]{0,2,1:T(8,128)(2,1)S(1)} copy-done((bf16[128,32,192]{0,2,1:T(8,128)(2,1)S(1)}, bf16[128,32,192]{0,2,1:T(8,128)(2,1)}, u32[]{:S(2)}) %copy-start) | copy-done | bytes 1572888
  2.7 0.0 copy-start.1
  2.7 1.2 %copy-done.1 = bf16[128,32,128]{2,1,0:T(8,128)(2,1)S(1)} copy-done((bf16[128,32,128]{2,1,0:T(8,128)(2,1)S(1)}, bf16[128,32,128]{2,1,0:T(8,128)(2,1)}, u32[]{:S(2)}) %copy-start.1) | copy-done | bytes 1048600
  3.9 0.0 copy-start.2
  3.9 0.7 copy-done.2
  4.6 0.0 copy-start.3
  4.6 0.7 copy-done.3
  5.3 2.5 %shard_map.76 = bf16[16,688,128]{2,1,0:T(8,128)(2,1)S(1)} custom-call(bf16[32,192,128]{2,1,0:T(8,128)(2,1)S(1)} %bitcast.3, bf16[128,32,128]{2,1,0:T(8,128)(2,1)S(1)} %copy-done.1, bf16[32,128]{1,0:T(8,128)(2,1)S(1)} %copy-done.2, s32[2,72]{1,0:T(2,128)S(1)} %bitcast.4, s32[1]{0:T(128)S(6)} %copy.8.refs_2_), custom_call_target="tpu_custom_call" | custom-call | flops 1000000000 | bytes 8000000 | tf_op jit(solution)/shard_map/pallas_call | solution.py:198
  7.8 41.9 %all_to_all.15.x_ref = bf16[16,688,128]{2,1,0:T(8,128)(2,1)S(1)} all-to-all(bf16[16,688,128]{2,1,0:T(8,128)(2,1)S(1)} %shard_map.76), channel_id=1, replica_groups=mesh['dp'=8,'field'=16] {'field'}, dimensions={0} | all-to-all | bytes 5636096 | tf_op jit(solution)/shard_map/all_to_all | solution.py:217
  49.7 8.4 %shard_map.77 = bf16[16,672,128]{2,1,0:T(8,128)(2,1)S(1)} custom-call(bf16[16,688,128]{2,1,0:T(8,128)(2,1)S(1)} %all_to_all.15.x_ref), custom_call_target="tpu_custom_call" | custom-call | flops 4000000000 | bytes 6000000 | tf_op jit(solution)/shard_map/pallas_call | solution.py:220
  58.1 37.4 %all_to_all.16.y_ref = bf16[16,672,128]{2,1,0:T(8,128)(2,1)S(1)} all-to-all(bf16[16,672,128]{2,1,0:T(8,128)(2,1)S(1)} %shard_map.77), channel_id=1, replica_groups=mesh['dp'=8,'field'=16] {'field'}, dimensions={0} | all-to-all | bytes 5505024 | tf_op jit(solution)/shard_map/all_to_all | solution.py:236
  95.6 0.6 broadcast_in_dim.3
  96.2 6.6 %all-to-all-start.2 = ((f32[8,32,128]{2,1,0:T(8,128)}), f32[8,32,128]{2,1,0:T(8,128)S(1)}, u32[]{:S(2)}, u32[]{:S(2)}) async-start(f32[8,32,128]{2,1,0:T(8,128)} %broadcast_in_dim.3), calls=%async_computation.2 | async-start | bytes 262144 | tf_op jit(solution)/shard_map/all_to_all | solution.py:168
  102.9 4.8 %shard_map.78 = (bf16[128,32,128]{2,1,0:T(8,128)(2,1)}, bf16[32,192,128]{2,1,0:T(8,128)(2,1)}) custom-call(bf16[16,672,128]{2,1,0:T(8,128)(2,1)S(1)} %all_to_all.16.y_ref), custom_call_target="tpu_custom_call" | custom-call | flops 1000000000 | bytes 8000000 | tf_op jit(solution)/shard_map/pallas_call | solution.py:245
  107.6 3.3 %all-to-all-done.2 = f32[8,32,128]{2,1,0:T(8,128)S(1)} async-done(((f32[8,32,128]{2,1,0:T(8,128)}), f32[8,32,128]{2,1,0:T(8,128)S(1)}, u32[]{:S(2)}, u32[]{:S(2)}) %all-to-all-start.2) | async-done | bytes 131104 | tf_op jit(solution)/shard_map/all_to_all | solution.py:168
  111.0 0.6 broadcast_multiply_fusion
  (2 shorter events, 0.0 us)
Async XLA Ops:
  1.3 1.4 %copy-start = (bf16[128,32,192]{0,2,1:T(8,128)(2,1)S(1)}, bf16[128,32,192]{0,2,1:T(8,128)(2,1)}, u32[]{:S(2)}) copy-start(bf16[128,32,192]{0,2,1:T(8,128)(2,1)} %param.5) | copy-start | bytes 4718596
  2.7 1.2 %copy-start.1 = (bf16[128,32,128]{2,1,0:T(8,128)(2,1)S(1)}, bf16[128,32,128]{2,1,0:T(8,128)(2,1)}, u32[]{:S(2)}) copy-start(bf16[128,32,128]{2,1,0:T(8,128)(2,1)} %cot_ref.1) | copy-start | bytes 3145732
  3.9 0.7 copy-start.2
  4.6 0.7 copy-start.3
  96.2 14.7 %all-to-all-start.2 = ((f32[8,32,128]{2,1,0:T(8,128)}), f32[8,32,128]{2,1,0:T(8,128)S(1)}, u32[]{:S(2)}, u32[]{:S(2)}) async-start(f32[8,32,128]{2,1,0:T(8,128)} %broadcast_in_dim.3), calls=%async_computation.2 | async-start | bytes 262144 | tf_op jit(solution)/shard_map/all_to_all | solution.py:168

commit v3 on v0

v3 whole, which is shorter than its diff:
```python
import functools

import jax
import jax.numpy as jnp
from jax import lax
from jax.experimental import pallas as pl
from jax.experimental.pallas import tpu as pltpu
from jax.sharding import PartitionSpec as P

LANES = 128
GROUPS = 4
AT_ONCE = 4
HALVES = (1, 8, 2, 6)
BUTTERFLY = (1, 3, 4)
TABLE = 16
TURN = (((1,), (1,)), ((), ()))
MIB = 1024 * 1024


def row_groups(tile):
    size = tile // 2 // GROUPS
    return [(g * size, tile // 2 + g * size, size) for g in range(GROUPS)]


def pack_kernel(
    emb_hbm, cot_hbm, comp_hbm, pairs_hbm, counts_ref, out_hbm, emb, comp, pairs, turned, message, sems
):
    tile, width, samples = emb.shape
    fields = out_hbm.shape[0]
    each = samples // fields
    half = tile // 2
    packed = tile + half
    f32, bf16 = jnp.float32, jnp.bfloat16
    groups = row_groups(tile)
    loads = [
        pltpu.make_async_copy(
            emb_hbm.at[pl.ds(start, size)], emb.at[pl.ds(start, size)], sems.at[2 * g + h]
        )
        for g, (low, high, size) in enumerate(groups)
        for h, start in enumerate((low, high))
    ]
    small = [
        pltpu.make_async_copy(comp_hbm, comp, sems.at[2 * GROUPS]),
        pltpu.make_async_copy(pairs_hbm, pairs, sems.at[2 * GROUPS + 1]),
    ]
    direct = pltpu.make_async_copy(
        cot_hbm, message.at[:, pl.ds(each * packed, each * tile)], sems.at[2 * GROUPS + 2]
    )
    for copy in loads[:2] + small + loads[2:] + [direct]:
        copy.start()
    for copy in small:
        copy.wait()
    slots = pairs.shape[1]
    number = lax.broadcasted_iota(jnp.int32, (LANES, slots), 0)
    live = lax.broadcasted_iota(jnp.int32, (LANES, slots), 1) < counts_ref[0]
    first = jnp.where((pairs[0:1] == number) & live, 1.0, 0.0).astype(bf16)
    second = jnp.where(pairs[1:2] == number, 1.0, 0.0).astype(bf16)
    table = lax.dot_general(first, second, TURN, preferred_element_type=f32)
    base = each * (packed + tile)
    for p in range(fields):
        message[p, base : base + tile] = comp[...]
        message[p, base + tile : base + tile + TABLE] = table[:TABLE].astype(bf16)
    for g, (low, high, size) in enumerate(groups):
        loads[2 * g].wait()
        loads[2 * g + 1].wait()
        for r in range(size):
            blocks = [
                (low + r, emb[low + r, :LANES]),
                (high + r, emb[high + r, :LANES]),
                (
                    tile + low + r,
                    jnp.concatenate([emb[low + r, LANES:], emb[high + r, LANES:]], axis=0),
                ),
            ]
            for place, block in blocks:
                turned[place * samples : (place + 1) * samples] = block.astype(f32).T
    direct.wait()
    stores = []
    for g in range(GROUPS):
        some = fields // GROUPS

        def peer(p, carry):
            for j in range(each):
                both = turned[pl.ds(p * each + j, packed, stride=samples), :]
                message[p, j * packed : (j + 1) * packed] = both.astype(bf16)
            return carry

        lax.fori_loop(g * some, (g + 1) * some, peer, 0)
        here = pl.ds(g * some, some)
        stores.append(
            pltpu.make_async_copy(message.at[here], out_hbm.at[here], sems.at[2 * GROUPS + 3 + g])
        )
        stores[-1].start()
    for copy in stores:
        copy.wait()


def pair_mask(x_ref, base, scale, mask, tile):
    fields = x_ref.shape[0]
    f32 = jnp.float32
    table = jnp.zeros((TABLE, LANES), f32)
    for f in range(fields):
        table += x_ref[f, base : base + TABLE].astype(f32)
    square = jnp.concatenate([table, jnp.zeros((LANES - TABLE, LANES), f32)], axis=0)
    on_diag = lax.broadcasted_iota(jnp.int32, square.shape, 0) == lax.broadcasted_iota(
        jnp.int32, square.shape, 1
    )
    mult = (square + square.T - jnp.where(on_diag, square, 0.0)) * scale
    for a in range(fields):
        row = jnp.concatenate(
            [jnp.broadcast_to(mult[a : a + 1, b : b + 1], (1, tile)) for b in range(fields)], axis=1
        )
        mask[a * tile : (a + 1) * tile] = jnp.broadcast_to(row, (tile, row.shape[1]))


def block_kernel(scale, tile, width, me_ref, x_ref, y_ref, keep_ref, send_ref, mask, grad, *sets):
    fields = x_ref.shape[0]
    half, rest = tile // 2, width - LANES
    packed = tile + half
    rows = packed + tile
    embeds = fields * tile
    f32, bf16 = jnp.float32, jnp.bfloat16
    each = (x_ref.shape[1] - tile - TABLE) // rows
    base = each * rows
    sets = [sets[i : i + 3] for i in range(0, len(sets), 3)]
    pair_mask(x_ref, base + tile, scale, mask, tile)
    weights = x_ref[:, base : base + tile].reshape(embeds, LANES)
    for _, sides, other in sets:
        sides[:, :LANES] = weights
        other[:, LANES:] = weights
    grad[...] = jnp.zeros_like(grad)

    def sample(j, emb, sides, other):
        start = pl.multiple_of(j * packed, 16)
        second = pl.multiple_of(each * packed + j * tile, 16)
        emb[:, :LANES] = x_ref[:, pl.ds(start, tile)].reshape(embeds, LANES)
        cot = x_ref[:, pl.ds(second, tile)].reshape(embeds, LANES)
        sides[:, LANES:] = cot
        other[:, :LANES] = cot
        tail = x_ref[:, pl.ds(start + tile, half)]
        upper = jnp.concatenate([tail[:, :, rest:], tail[:, :, :rest]], axis=2)
        both = jnp.concatenate([tail, upper], axis=1).reshape(embeds, LANES)
        emb[:, LANES:] = both[:, :rest]
        feats = emb[...]
        gram = lax.dot_general(feats, feats, TURN, preferred_element_type=f32)
        hmat = lax.dot_general(other[...], sides[...], TURN, preferred_element_type=f32)
        masked = (mask[...] * gram).astype(bf16)
        sym = (mask[...] * hmat).astype(bf16)
        both = jnp.dot(masked, sides[...], preferred_element_type=f32)
        dfeat = jnp.dot(sym, feats, preferred_element_type=f32).astype(bf16)
        y_ref[:, pl.ds(second, tile)] = both[:, :LANES].astype(bf16).reshape(fields, tile, LANES)
        y_ref[:, pl.ds(start, tile)] = dfeat[:, :LANES].reshape(fields, tile, LANES)
        last = dfeat[:, LANES:].reshape(fields, tile, rest)
        y_ref[:, pl.ds(start + tile, half)] = jnp.concatenate(
            [last[:, :half], last[:, half:]], axis=2
        )
        return both[:, LANES:]

    def some(i, carry):
        terms = [sample(i * len(sets) + u, *refs) for u, refs in enumerate(sets)]
        grad[...] += sum(terms[1:], terms[0])
        return carry

    lax.fori_loop(0, each // len(sets), some, 0)
    for n in range(fields):
        owner = me_ref[0]
        for bit, flip in enumerate(HALVES):
            if n & (fields >> (bit + 1)):
                owner = jnp.bitwise_xor(owner, flip)
        term = grad[pl.ds(pl.multiple_of(owner * tile, tile), tile)]
        if n < fields // 2:
            keep_ref[n] = term
        else:
            send_ref[n - fields // 2] = term


def unpack_kernel(y_ref, mixed_hbm, dfeat_hbm, dfeat, turned, sems):
    tile, width, samples = dfeat.shape
    fields = y_ref.shape[0]
    each = samples // fields
    half, rest = tile // 2, width - LANES
    packed = tile + half
    f32, bf16 = jnp.float32, jnp.bfloat16
    copies = [
        pltpu.make_async_copy(
            y_ref.at[:, pl.ds(each * packed, each * tile)], mixed_hbm, sems.at[2 * GROUPS]
        )
    ]
    copies[0].start()

    def peer(p, carry):
        for j in range(each):
            turned[pl.ds(p * each + j, packed, stride=samples), :] = y_ref[
                p, j * packed : (j + 1) * packed
            ].astype(f32)
        return carry

    lax.fori_loop(0, fields, peer, 0)
    for g, (low, high, size) in enumerate(row_groups(tile)):
        for r in range(size):
            for row in (low + r, high + r):
                dfeat[row, :LANES] = turned[row * samples : (row + 1) * samples].T.astype(bf16)
            place = tile + low + r
            block = turned[place * samples : (place + 1) * samples].T.astype(bf16)
            dfeat[low + r, LANES:] = block[:rest]
            dfeat[high + r, LANES:] = block[rest:]
        for h, start in enumerate((low, high)):
            copy = pltpu.make_async_copy(
                dfeat.at[pl.ds(start, size)], dfeat_hbm.at[pl.ds(start, size)], sems.at[2 * g + h]
            )
            copy.start()
            copies.append(copy)
    for copy in copies:
        copy.wait()


def halve_sum(keep, send):
    size = lax.axis_size("field")
    for flip in HALVES:
        total = keep + lax.ppermute(send, "field", [(i, i ^ flip) for i in range(size)])
        left = total.shape[0] // 2
        keep, send = total[:left], total[left:]
    return total[0]


def dp_sum(total):
    size = lax.axis_size("dp")
    for flip in [f for f in BUTTERFLY if f < size]:
        total = total + lax.ppermute(total, "dp", [(i, i ^ flip) for i in range(size)])
    return total


def per_device(emb, comp, cot, pairs, counts):
    samp_rows, tile, width = emb.shape
    fields = lax.axis_size("field")
    embeds = tile * fields
    packed = tile + tile // 2
    rows = packed + tile
    each = samp_rows // fields
    f32, bf16 = jnp.float32, jnp.bfloat16
    params = pltpu.CompilerParams(vmem_limit_bytes=24 * MIB)
    vmem = pl.BlockSpec(memory_space=pltpu.VMEM)
    smem = pl.BlockSpec(memory_space=pltpu.SMEM)
    hbm = pl.BlockSpec(memory_space=pltpu.HBM)
    turned = pltpu.VMEM((packed * samp_rows, LANES), f32)
    by_row = pltpu.VMEM((tile, width, samp_rows), bf16)

    def cost(flops, moved):
        return pl.CostEstimate(flops=flops, bytes_accessed=moved, transcendentals=0)

    x = pl.pallas_call(
        pack_kernel,
        out_shape=jax.ShapeDtypeStruct((fields, each * rows + tile + TABLE, LANES), bf16),
        in_specs=[hbm, hbm, hbm, hbm, smem],
        out_specs=hbm,
        scratch_shapes=[
            by_row,
            pltpu.VMEM(comp.shape, bf16),
            pltpu.VMEM(pairs.shape[::-1], jnp.int32),
            turned,
            pltpu.VMEM((fields, each * rows + tile + TABLE, LANES), bf16),
            pltpu.SemaphoreType.DMA((3 * GROUPS + 3,)),
        ],
        compiler_params=pltpu.CompilerParams(vmem_limit_bytes=56 * MIB),
        cost_estimate=cost(10**9, 8 * 10**6),
    )(
        jnp.transpose(emb, (1, 2, 0)),
        cot.reshape(fields, each * tile, LANES),
        comp,
        pairs.T,
        counts,
    )
    x = lax.all_to_all(x, "field", 0, 0)
    terms = jax.ShapeDtypeStruct((fields // 2, tile, LANES), f32)
    y, keep, send = pl.pallas_call(
        functools.partial(block_kernel, width ** (-0.5), tile, width),
        out_shape=(jax.ShapeDtypeStruct((fields, each * rows, LANES), bf16), terms, terms),
        in_specs=[smem, vmem],
        out_specs=(vmem, vmem, vmem),
        scratch_shapes=[pltpu.VMEM((embeds, embeds), f32), pltpu.VMEM((embeds, LANES), f32)]
        + [
            pltpu.VMEM((embeds, width), bf16),
            pltpu.VMEM((embeds, 2 * LANES), bf16),
            pltpu.VMEM((embeds, 2 * LANES), bf16),
        ]
        * AT_ONCE,
        compiler_params=params,
        cost_estimate=cost(4 * 10**9, 6 * 10**6),
    )(lax.axis_index("field").astype(jnp.int32).reshape(1), x)
    y = lax.all_to_all(y, "field", 0, 0)
    weight_grad = dp_sum(halve_sum(keep, send)) / (samp_rows * lax.axis_size("dp"))

    mixed, emb_grad = pl.pallas_call(
        unpack_kernel,
        out_shape=(
            jax.ShapeDtypeStruct((fields, each * tile, LANES), bf16),
            jax.ShapeDtypeStruct((tile, width, samp_rows), bf16),
        ),
        in_specs=[vmem],
        out_specs=(hbm, hbm),
        scratch_shapes=[by_row, turned, pltpu.SemaphoreType.DMA((2 * GROUPS + 1,))],
        compiler_params=params,
        cost_estimate=cost(10**9, 8 * 10**6),
    )(y)
    return mixed.reshape(cot.shape), jnp.transpose(emb_grad, (2, 0, 1)), weight_grad


def solution(mesh):
    in_specs = (
        P("dp", "field", None),
        P("field", None),
        P("dp", "field", None),
        P("field", None),
        P("field"),
    )
    out_specs = (P("dp", "field", None), P("dp", "field", None), P("field", None))
    return jax.shard_map(
        per_device, mesh=mesh, in_specs=in_specs, out_specs=out_specs, check_vma=False
    )
```

time: 544 us -> 132 us (0.24)
  local copies, waits for them, and re-layouts: 167 us -> 1.52 us
  matrix products: 105 us -> 0 us
  blocking collectives: 93.2 us -> 0 us
  waiting for transfers between devices: 159 us -> 83.5 us
  starting transfers between devices: 0.12 us -> 29.9 us
  Pallas kernels: 0 us -> 14.9 us
  between operations: 14.5 us -> 1.36 us
    all_gather x2 -> x0, waiting for transfers between devices: 158 us -> none  [the longest x1 129 us: per_device(): lax.all_gather(emb, 'field', axis=1, tiled=True)]
    dot_general x9 -> x0, matrix products: 105 us -> none  [the longest x1 27.3 us: per_device(): jnp.einsum('brBc,bBcd->bBrd', sym_tiles, feat_tiles, preferred_element_ty...]
    dot_general x2 -> x0, local copies, waits for them, and re-layouts: 96.3 us -> none  [the longest x1 96.3 us: per_device(): jnp.einsum('brBc,bBcd->bBrd', sym_tiles, feat_tiles, preferred_element_ty...]
    ppermute x0 -> x7, waiting for transfers between devices: none -> 47 us  [the longest x4 40.2 us: halve_sum(): lax.ppermute(send, 'field', [(i, i ^ flip) for i in range(size)])]
    reshape x2 -> x0, local copies, waits for them, and re-layouts: 46.2 us -> none  [the longest x1 23.1 us: per_device(): sym_tiles = sym.reshape(samp_rows, tile, fields, tile)]
    all_gather x2 -> x0, blocking collectives: 43.3 us -> none  [the longest x1 22 us: per_device(): weights = lax.all_gather(comp, 'field', axis=0, tiled=True)]
    psum x1 -> x0, blocking collectives: 41.7 us -> none  [per_device(): weight_grad = lax.psum(own_tile, 'dp') / (samp_rows * lax.axis_size('dp'))]
    all_to_all x0 -> x2, waiting for transfers between devices: none -> 36.5 us  [the longest x1 36.5 us: per_device(): x = lax.all_to_all(x, 'field', 0, 0)]
  transfers between devices with their start and end apart: 3 -> 9, of which waited for: 2 -> 8; matrix products, arithmetic and copies ran while one was open for 36% -> 1% of each run, Pallas kernels for 0% -> 0%
where the time goes in v3:
time: 132 us
  waiting for transfers between devices  83.5 us (63%)
  starting transfers between devices  29.9 us (23%)
  Pallas kernels  14.9 us (11%)
  local copies, waits for them, and re-layouts  1.52 us (1%)
  between operations  1.36 us (1%)
    ppermute x4, waiting for transfers between devices, halve_sum(): lax.ppermute(send, 'field', [(i, i ^ flip) for i in range(size)])  40.2 us
    all_to_all x1, waiting for transfers between devices, per_device(): x = lax.all_to_all(x, 'field', 0, 0)  36.5 us
    all_to_all x1, starting transfers between devices, per_device(): y = lax.all_to_all(y, 'field', 0, 0)  8.96 us
    ppermute x4, starting transfers between devices, halve_sum(): lax.ppermute(send, 'field', [(i, i ^ flip) for i in range(size)])  7.32 us
    ppermute x3, starting transfers between devices, dp_sum(): lax.ppermute(total, 'dp', [(i, i ^ flip) for i in range(size)])  7.13 us
    ppermute x3, waiting for transfers between devices, dp_sum(): lax.ppermute(total, 'dp', [(i, i ^ flip) for i in range(size)])  6.8 us
    all_to_all x1, starting transfers between devices, per_device(): x = lax.all_to_all(x, 'field', 0, 0)  6.53 us
    pallas_call x1, Pallas kernels, per_device(): pl.pallas_call(functools.partial(block_kernel, width ** (-0.5), tile, wid...  5.72 us
  transfers between devices with their start and end apart: 9, of which 8 were waited for; matrix products, arithmetic and copies ran while one was open for 1% of the time, Pallas kernels for 0%

profile of v3, /device:TPU:0, one launch (start us, length us, event | category | flops | bytes accessed | tf_op | source)
XLA Modules:
  0.0 131.8 jit_solution(15523217422298972133)
XLA Ops:
  1.3 4.7 %shard_map.76 = bf16[16,688,128]{2,1,0:T(8,128)(2,1)} custom-call(bf16[32,192,128]{2,1,0:T(8,128)(2,1)} %bitcast.8, bf16[16,256,128]{2,1,0:T(8,128)(2,1)} %bitcast.9, bf16[32,128]{1,0:T(8,128)(2,1)} %comp_hbm.1, s32[2,72]{1,0:T(2,128)} %bitcast.10, s32[1]{0:T(128)S(6)} %copy.8.counts_ref), custom_call_target="tpu_custom_call" | custom-call | flops 1000000000 | bytes 8000000 | tf_op jit(solution)/shard_map/pallas_call | solution.py:251
  6.0 6.5 %all-to-all-start = ((bf16[16,688,128]{2,1,0:T(8,128)(2,1)}), bf16[16,688,128]{2,1,0:T(8,128)(2,1)S(1)}, u32[]{:S(2)}, u32[]{:S(2)}) async-start(bf16[16,688,128]{2,1,0:T(8,128)(2,1)} %shard_map.76), calls=%async_computation | async-start | bytes 5636096 | tf_op jit(solution)/shard_map/all_to_all | solution.py:273
  12.6 36.5 %all-to-all-done.x_ref = bf16[16,688,128]{2,1,0:T(8,128)(2,1)S(1)} async-done(((bf16[16,688,128]{2,1,0:T(8,128)(2,1)}), bf16[16,688,128]{2,1,0:T(8,128)(2,1)S(1)}, u32[]{:S(2)}, u32[]{:S(2)}) %all-to-all-start) | async-done | bytes 2818080 | tf_op jit(solution)/shard_map/all_to_all | solution.py:273
  49.0 5.7 %shard_map.77 = (bf16[16,640,128]{2,1,0:T(8,128)(2,1)S(1)}, f32[8,32,128]{2,1,0:T(8,128)S(1)}, f32[8,32,128]{2,1,0:T(8,128)S(1)}) custom-call(s32[1]{0:T(128)} %bitcast.me_ref, bf16[16,688,128]{2,1,0:T(8,128)(2,1)S(1)} %all-to-all-done.x_ref), custom_call_target="tpu_custom_call" | custom-call | flops 4000000000 | bytes 6000000 | tf_op jit(solution)/shard_map/pallas_call | solution.py:275
  54.8 0.0 copy-start
  54.8 1.5 %copy-done = bf16[16,640,128]{2,1,0:T(8,128)(2,1)} copy-done((bf16[16,640,128]{2,1,0:T(8,128)(2,1)}, bf16[16,640,128]{2,1,0:T(8,128)(2,1)S(1)}, u32[]{:S(2)}) %copy-start) | copy-done | bytes 2621464
  56.3 9.0 %all-to-all-start.1 = ((bf16[16,640,128]{2,1,0:T(8,128)(2,1)}), bf16[16,640,128]{2,1,0:T(8,128)(2,1)S(1)}, u32[]{:S(2)}, u32[]{:S(2)}) async-start(bf16[16,640,128]{2,1,0:T(8,128)(2,1)} %copy-done), calls=%async_computation.1 | async-start | bytes 5242880 | tf_op jit(solution)/shard_map/all_to_all | solution.py:290
  65.3 0.4 collective-permute-start
  65.7 1.1 collective-permute-done
  66.8 1.9 %collective-permute-start.1 = (f32[4,32,128]{2,1,0:T(8,128)S(1)}, f32[4,32,128]{2,1,0:T(8,128)S(1)}, u32[]{:S(2)}, u32[]{:S(2)}) collective-permute-start(f32[4,32,128]{2,1,0:T(8,128)S(1)} %slice.25), channel_id=1, source_target_pairs={{0,8},{1,9},{2,10},{3,11},{4,12},{5,13},{6,14},{7,15},{8,0},{9,1},... | collective-permute-start | bytes 196616 | tf_op jit(solution)/shard_map/ppermute | solution.py:220
  68.7 32.3 %collective-permute-done.1 = f32[4,32,128]{2,1,0:T(8,128)S(1)} collective-permute-done((f32[4,32,128]{2,1,0:T(8,128)S(1)}, f32[4,32,128]{2,1,0:T(8,128)S(1)}, u32[]{:S(2)}, u32[]{:S(2)}) %collective-permute-start.1) | collective-permute-done | bytes 65568 | tf_op jit(solution)/shard_map/ppermute | solution.py:220
  101.0 4.9 %collective-permute-start.2 = (f32[2,32,128]{2,1,0:T(8,128)S(1)}, f32[2,32,128]{2,1,0:T(8,128)S(1)}, u32[]{:S(2)}, u32[]{:S(2)}) collective-permute-start(f32[2,32,128]{2,1,0:T(8,128)S(1)} %slice.27), channel_id=1, source_target_pairs={{0,2},{1,3},{2,0},{3,1},{4,6},{5,7},{6,4},{7,5},{8,10},{9,11},{10,... | collective-permute-start | bytes 98312 | tf_op jit(solution)/shard_map/ppermute | solution.py:220
  105.9 1.9 %collective-permute-done.2 = f32[2,32,128]{2,1,0:T(8,128)S(1)} collective-permute-done((f32[2,32,128]{2,1,0:T(8,128)S(1)}, f32[2,32,128]{2,1,0:T(8,128)S(1)}, u32[]{:S(2)}, u32[]{:S(2)}) %collective-permute-start.2) | collective-permute-done | bytes 32800 | tf_op jit(solution)/shard_map/ppermute | solution.py:220
  107.8 0.1 collective-permute-start.3
  107.9 4.9 %collective-permute-done.3 = f32[1,32,128]{2,1,0:T(8,128)S(1)} collective-permute-done((f32[1,32,128]{2,1,0:T(8,128)S(1)}, f32[1,32,128]{2,1,0:T(8,128)S(1)}, u32[]{:S(2)}, u32[]{:S(2)}) %collective-permute-start.3) | collective-permute-done | bytes 16416 | tf_op jit(solution)/shard_map/ppermute | solution.py:220
  112.8 1.5 %collective-permute-start.4 = (f32[32,128]{1,0:T(8,128)S(1)}, f32[32,128]{1,0:T(8,128)S(1)}, u32[]{:S(2)}, u32[]{:S(2)}) collective-permute-start(f32[32,128]{1,0:T(8,128)S(1)} %fusion), channel_id=1, source_target_pairs={{0,16},{16,0},{32,48},{48,32},{64,80},{80,64},{96,112},{112,96},{1... | collective-permute-start | bytes 49160 | tf_op jit(solution)/shard_map/ppermute | solution.py:229
  114.3 2.3 %collective-permute-done.4 = f32[32,128]{1,0:T(8,128)S(1)} collective-permute-done((f32[32,128]{1,0:T(8,128)S(1)}, f32[32,128]{1,0:T(8,128)S(1)}, u32[]{:S(2)}, u32[]{:S(2)}) %collective-permute-start.4) | collective-permute-done | bytes 16416 | tf_op jit(solution)/shard_map/ppermute | solution.py:229
  116.6 2.8 %collective-permute-start.5 = (f32[32,128]{1,0:T(8,128)S(1)}, f32[32,128]{1,0:T(8,128)S(1)}, u32[]{:S(2)}, u32[]{:S(2)}) collective-permute-start(f32[32,128]{1,0:T(8,128)S(1)} %add.25), channel_id=1, source_target_pairs={{0,48},{16,32},{32,16},{48,0},{64,112},{80,96},{96,80},{112,64},{1... | collective-permute-start | bytes 49160 | tf_op jit(solution)/shard_map/ppermute | solution.py:229
  119.3 2.2 %collective-permute-done.5 = f32[32,128]{1,0:T(8,128)S(1)} collective-permute-done((f32[32,128]{1,0:T(8,128)S(1)}, f32[32,128]{1,0:T(8,128)S(1)}, u32[]{:S(2)}, u32[]{:S(2)}) %collective-permute-start.5) | collective-permute-done | bytes 16416 | tf_op jit(solution)/shard_map/ppermute | solution.py:229
  121.5 2.9 %collective-permute-start.6 = (f32[32,128]{1,0:T(8,128)S(1)}, f32[32,128]{1,0:T(8,128)S(1)}, u32[]{:S(2)}, u32[]{:S(2)}) collective-permute-start(f32[32,128]{1,0:T(8,128)S(1)} %add.26), channel_id=1, source_target_pairs={{0,64},{16,80},{32,96},{48,112},{64,0},{80,16},{96,32},{112,48},{1... | collective-permute-start | bytes 49160 | tf_op jit(solution)/shard_map/ppermute | solution.py:229
  124.4 2.3 %collective-permute-done.6 = f32[32,128]{1,0:T(8,128)S(1)} collective-permute-done((f32[32,128]{1,0:T(8,128)S(1)}, f32[32,128]{1,0:T(8,128)S(1)}, u32[]{:S(2)}, u32[]{:S(2)}) %collective-permute-start.6) | collective-permute-done | bytes 16416 | tf_op jit(solution)/shard_map/ppermute | solution.py:229
  126.8 0.6 add_multiply_fusion
  127.4 0.0 all-to-all-done.1.y_ref
  127.4 4.4 %shard_map.78 = (bf16[16,256,128]{2,1,0:T(8,128)(2,1)}, bf16[32,192,128]{2,1,0:T(8,128)(2,1)}) custom-call(bf16[16,640,128]{2,1,0:T(8,128)(2,1)S(1)} %all-to-all-done.1.y_ref), custom_call_target="tpu_custom_call" | custom-call | flops 1000000000 | bytes 8000000 | tf_op jit(solution)/shard_map/pallas_call | solution.py:293
  (9 shorter events, 0.1 us)
Async XLA Ops:
  6.0 43.0 %all-to-all-start = ((bf16[16,688,128]{2,1,0:T(8,128)(2,1)}), bf16[16,688,128]{2,1,0:T(8,128)(2,1)S(1)}, u32[]{:S(2)}, u32[]{:S(2)}) async-start(bf16[16,688,128]{2,1,0:T(8,128)(2,1)} %shard_map.76), calls=%async_computation | async-start | bytes 5636096 | tf_op jit(solution)/shard_map/all_to_all | solution.py:273
  54.8 1.5 %copy-start = (bf16[16,640,128]{2,1,0:T(8,128)(2,1)}, bf16[16,640,128]{2,1,0:T(8,128)(2,1)S(1)}, u32[]{:S(2)}) copy-start(bf16[16,640,128]{2,1,0:T(8,128)(2,1)S(1)} %get-tuple-element.8) | copy-start | bytes 7864324
  56.3 71.1 %all-to-all-start.1 = ((bf16[16,640,128]{2,1,0:T(8,128)(2,1)}), bf16[16,640,128]{2,1,0:T(8,128)(2,1)S(1)}, u32[]{:S(2)}, u32[]{:S(2)}) async-start(bf16[16,640,128]{2,1,0:T(8,128)(2,1)} %copy-done), calls=%async_computation.1 | async-start | bytes 5242880 | tf_op jit(solution)/shard_map/all_to_all | solution.py:290
  65.3 1.5 %collective-permute-start = (f32[8,32,128]{2,1,0:T(8,128)S(1)}, f32[8,32,128]{2,1,0:T(8,128)S(1)}, u32[]{:S(2)}, u32[]{:S(2)}) collective-permute-start(f32[8,32,128]{2,1,0:T(8,128)S(1)} %get-tuple-element.12), channel_id=1, source_target_pairs={{0,1},{1,0},{2,3},{3,2},{4,5},{5,4},{6,7},{7,6},{8,9},{9,8},{10,11... | collective-permute-start | bytes 393224 | tf_op jit(solution)/shard_map/ppermute | solution.py:220
  66.8 34.1 %collective-permute-start.1 = (f32[4,32,128]{2,1,0:T(8,128)S(1)}, f32[4,32,128]{2,1,0:T(8,128)S(1)}, u32[]{:S(2)}, u32[]{:S(2)}) collective-permute-start(f32[4,32,128]{2,1,0:T(8,128)S(1)} %slice.25), channel_id=1, source_target_pairs={{0,8},{1,9},{2,10},{3,11},{4,12},{5,13},{6,14},{7,15},{8,0},{9,1},... | collective-permute-start | bytes 196616 | tf_op jit(solution)/shard_map/ppermute | solution.py:220
  101.0 6.8 %collective-permute-start.2 = (f32[2,32,128]{2,1,0:T(8,128)S(1)}, f32[2,32,128]{2,1,0:T(8,128)S(1)}, u32[]{:S(2)}, u32[]{:S(2)}) collective-permute-start(f32[2,32,128]{2,1,0:T(8,128)S(1)} %slice.27), channel_id=1, source_target_pairs={{0,2},{1,3},{2,0},{3,1},{4,6},{5,7},{6,4},{7,5},{8,10},{9,11},{10,... | collective-permute-start | bytes 98312 | tf_op jit(solution)/shard_map/ppermute | solution.py:220
  107.8 5.0 %collective-permute-start.3 = (f32[1,32,128]{2,1,0:T(8,128)S(1)}, f32[1,32,128]{2,1,0:T(8,128)S(1)}, u32[]{:S(2)}, u32[]{:S(2)}) collective-permute-start(f32[1,32,128]{2,1,0:T(8,128)S(1)} %slice.29), channel_id=1, source_target_pairs={{0,6},{1,7},{2,4},{3,5},{4,2},{5,3},{6,0},{7,1},{8,14},{9,15},{10,... | collective-permute-start | bytes 49160 | tf_op jit(solution)/shard_map/ppermute | solution.py:220
  112.8 3.7 %collective-permute-start.4 = (f32[32,128]{1,0:T(8,128)S(1)}, f32[32,128]{1,0:T(8,128)S(1)}, u32[]{:S(2)}, u32[]{:S(2)}) collective-permute-start(f32[32,128]{1,0:T(8,128)S(1)} %fusion), channel_id=1, source_target_pairs={{0,16},{16,0},{32,48},{48,32},{64,80},{80,64},{96,112},{112,96},{1... | collective-permute-start | bytes 49160 | tf_op jit(solution)/shard_map/ppermute | solution.py:229
  116.6 4.9 %collective-permute-start.5 = (f32[32,128]{1,0:T(8,128)S(1)}, f32[32,128]{1,0:T(8,128)S(1)}, u32[]{:S(2)}, u32[]{:S(2)}) collective-permute-start(f32[32,128]{1,0:T(8,128)S(1)} %add.25), channel_id=1, source_target_pairs={{0,48},{16,32},{32,16},{48,0},{64,112},{80,96},{96,80},{112,64},{1... | collective-permute-start | bytes 49160 | tf_op jit(solution)/shard_map/ppermute | solution.py:229
  121.5 5.2 %collective-permute-start.6 = (f32[32,128]{1,0:T(8,128)S(1)}, f32[32,128]{1,0:T(8,128)S(1)}, u32[]{:S(2)}, u32[]{:S(2)}) collective-permute-start(f32[32,128]{1,0:T(8,128)S(1)} %add.26), channel_id=1, source_target_pairs={{0,64},{16,80},{32,96},{48,112},{64,0},{80,16},{96,32},{112,48},{1... | collective-permute-start | bytes 49160 | tf_op jit(solution)/shard_map/ppermute | solution.py:229

commit v4 on v3

--- a/solution.py
+++ b/solution.py
@@ -10,7 +10,6 @@
 LANES = 128
 GROUPS = 4
 AT_ONCE = 4
-HALVES = (1, 8, 2, 6)
 BUTTERFLY = (1, 3, 4)
 TABLE = 16
 TURN = (((1,), (1,)), ((), ()))
@@ -113,7 +112,7 @@
         mask[a * tile : (a + 1) * tile] = jnp.broadcast_to(row, (tile, row.shape[1]))
 
 
-def block_kernel(scale, tile, width, me_ref, x_ref, y_ref, keep_ref, send_ref, mask, grad, *sets):
+def block_kernel(scale, tile, width, x_ref, y_ref, mask, grad, *sets):
     fields = x_ref.shape[0]
     half, rest = tile // 2, width - LANES
     packed = tile + half
@@ -162,46 +161,42 @@
         return carry
 
     lax.fori_loop(0, each // len(sets), some, 0)
-    for n in range(fields):
-        owner = me_ref[0]
-        for bit, flip in enumerate(HALVES):
-            if n & (fields >> (bit + 1)):
-                owner = jnp.bitwise_xor(owner, flip)
-        term = grad[pl.ds(pl.multiple_of(owner * tile, tile), tile)]
-        if n < fields // 2:
-            keep_ref[n] = term
-        else:
-            send_ref[n - fields // 2] = term
-
-
-def unpack_kernel(y_ref, mixed_hbm, dfeat_hbm, dfeat, turned, sems):
-    tile, width, samples = dfeat.shape
-    fields = y_ref.shape[0]
+    y_ref[:, base:] = grad[...].astype(bf16).reshape(fields, tile, LANES)
+
+
+def regroup_kernel(samples, y_ref, mixed_hbm, turned, sem):
+    fields, rows = y_ref.shape[0], turned.shape[0] // samples
     each = samples // fields
-    half, rest = tile // 2, width - LANES
-    packed = tile + half
-    f32, bf16 = jnp.float32, jnp.bfloat16
-    copies = [
-        pltpu.make_async_copy(
-            y_ref.at[:, pl.ds(each * packed, each * tile)], mixed_hbm, sems.at[2 * GROUPS]
-        )
-    ]
-    copies[0].start()
+    copy = pltpu.make_async_copy(
+        y_ref.at[:, pl.ds(each * rows, mixed_hbm.shape[1])], mixed_hbm, sem
+    )
+    copy.start()
 
     def peer(p, carry):
         for j in range(each):
-            turned[pl.ds(p * each + j, packed, stride=samples), :] = y_ref[
-                p, j * packed : (j + 1) * packed
-            ].astype(f32)
+            turned[pl.ds(p * each + j, rows, stride=samples), :] = y_ref[
+                p, j * rows : (j + 1) * rows
+            ].astype(jnp.float32)
         return carry
 
     lax.fori_loop(0, fields, peer, 0)
-    for g, (low, high, size) in enumerate(row_groups(tile)):
+    copy.wait()
+
+
+def turn_kernel(part, turned, *refs):
+    dfeat_hbm, dfeat, sems = refs[-3:]
+    tile, width, samples = dfeat.shape
+    rest = width - LANES
+    groups = row_groups(tile)
+    share = len(groups) // 2
+    copies = []
+    for g, (low, high, size) in enumerate(groups[part * share : (part + 1) * share]):
         for r in range(size):
             for row in (low + r, high + r):
-                dfeat[row, :LANES] = turned[row * samples : (row + 1) * samples].T.astype(bf16)
+                block = turned[row * samples : (row + 1) * samples].T
+                dfeat[row, :LANES] = block.astype(jnp.bfloat16)
             place = tile + low + r
-            block = turned[place * samples : (place + 1) * samples].T.astype(bf16)
+            block = turned[place * samples : (place + 1) * samples].T.astype(jnp.bfloat16)
             dfeat[low + r, LANES:] = block[:rest]
             dfeat[high + r, LANES:] = block[rest:]
         for h, start in enumerate((low, high)):
@@ -212,15 +207,6 @@
             copies.append(copy)
     for copy in copies:
         copy.wait()
-
-
-def halve_sum(keep, send):
-    size = lax.axis_size("field")
-    for flip in HALVES:
-        total = keep + lax.ppermute(send, "field", [(i, i ^ flip) for i in range(size)])
-        left = total.shape[0] // 2
-        keep, send = total[:left], total[left:]
-    return total[0]
 
 
 def dp_sum(total):
@@ -271,12 +257,11 @@
         counts,
     )
     x = lax.all_to_all(x, "field", 0, 0)
-    terms = jax.ShapeDtypeStruct((fields // 2, tile, LANES), f32)
-    y, keep, send = pl.pallas_call(
+    y = pl.pallas_call(
         functools.partial(block_kernel, width ** (-0.5), tile, width),
-        out_shape=(jax.ShapeDtypeStruct((fields, each * rows, LANES), bf16), terms, terms),
-        in_specs=[smem, vmem],
-        out_specs=(vmem, vmem, vmem),
+        out_shape=jax.ShapeDtypeStruct((fields, each * rows + tile, LANES), bf16),
+        in_specs=[vmem],
+        out_specs=vmem,
         scratch_shapes=[pltpu.VMEM((embeds, embeds), f32), pltpu.VMEM((embeds, LANES), f32)]
         + [
             pltpu.VMEM((embeds, width), bf16),
@@ -286,22 +271,36 @@
         * AT_ONCE,
         compiler_params=params,
         cost_estimate=cost(4 * 10**9, 6 * 10**6),
-    )(lax.axis_index("field").astype(jnp.int32).reshape(1), x)
+    )(x)
     y = lax.all_to_all(y, "field", 0, 0)
-    weight_grad = dp_sum(halve_sum(keep, send)) / (samp_rows * lax.axis_size("dp"))
-
-    mixed, emb_grad = pl.pallas_call(
-        unpack_kernel,
+    grad = dp_sum(jnp.sum(y[:, each * rows :].astype(f32), axis=0))
+    weight_grad = grad / (samp_rows * lax.axis_size("dp"))
+
+    mixed, sorted_rows = pl.pallas_call(
+        functools.partial(regroup_kernel, samp_rows),
         out_shape=(
             jax.ShapeDtypeStruct((fields, each * tile, LANES), bf16),
-            jax.ShapeDtypeStruct((tile, width, samp_rows), bf16),
+            jax.ShapeDtypeStruct((packed * samp_rows, LANES), f32),
         ),
         in_specs=[vmem],
-        out_specs=(hbm, hbm),
-        scratch_shapes=[by_row, turned, pltpu.SemaphoreType.DMA((2 * GROUPS + 1,))],
+        out_specs=(hbm, vmem),
+        scratch_shapes=[pltpu.SemaphoreType.DMA],
         compiler_params=params,
         cost_estimate=cost(10**9, 8 * 10**6),
     )(y)
+    emb_grad = ()
+    for part in range(2):
+        emb_grad = pl.pallas_call(
+            functools.partial(turn_kernel, part),
+            out_shape=(jax.ShapeDtypeStruct((tile, width, samp_rows), bf16),),
+            in_specs=[vmem] + [hbm] * part,
+            out_specs=(hbm,),
+            input_output_aliases={1: 0} if part else {},
+            scratch_shapes=[by_row, pltpu.SemaphoreType.DMA((GROUPS,))],
+            compiler_params=params,
+            cost_estimate=cost(10**9, 8 * 10**6),
+        )(sorted_rows, *emb_grad)
+    (emb_grad,) = emb_grad
     return mixed.reshape(cot.shape), jnp.transpose(emb_grad, (2, 0, 1)), weight_grad
 
 

time: 132 us -> 107 us (0.81)
  waiting for transfers between devices: 83.5 us -> 3.02 us
  blocking collectives: 0 us -> 79.4 us
  starting transfers between devices: 29.9 us -> 6.65 us
  local copies, waits for them, and re-layouts: 1.52 us -> 0 us
    all_to_all x0 -> x2, blocking collectives: none -> 79.4 us  [the longest x1 42 us: per_device(): x = lax.all_to_all(x, 'field', 0, 0)]
    ppermute x4 -> x0, waiting for transfers between devices: 40.2 us -> none  [halve_sum(): lax.ppermute(send, 'field', [(i, i ^ flip) for i in range(size)])]
    all_to_all x2 -> x0, waiting for transfers between devices: 36.5 us -> none  [the longest x1 36.5 us: per_device(): x = lax.all_to_all(x, 'field', 0, 0)]
    all_to_all x2 -> x0, starting transfers between devices: 15.5 us -> none  [the longest x1 8.96 us: per_device(): y = lax.all_to_all(y, 'field', 0, 0)]
    ppermute x4 -> x0, starting transfers between devices: 7.32 us -> none  [halve_sum(): lax.ppermute(send, 'field', [(i, i ^ flip) for i in range(size)])]
    ppermute x3, waiting for transfers between devices: 6.8 us -> 3.02 us  [dp_sum(): lax.ppermute(total, 'dp', [(i, i ^ flip) for i in range(size)])]
    unnamed x2 -> x0, local copies, waits for them, and re-layouts: 1.5 us -> none
    pallas_call x1 -> x3, Pallas kernels: 4.44 us -> 5.22 us  [the longest x1 3.07 us: per_device(): pl.pallas_call(functools.partial(regroup_kernel, samp_rows), out_shape=(j...]
  transfers between devices with their start and end apart: 9 -> 3, of which waited for: 8 -> 2; matrix products, arithmetic and copies ran while one was open for 1% -> 0% of each run, Pallas kernels for 0% -> 5%
where the time goes in v4:
time: 107 us
  blocking collectives  79.4 us (74%)
  Pallas kernels  15.7 us (15%)
  starting transfers between devices  6.65 us (6%)
  waiting for transfers between devices  3.02 us (3%)
  between operations  1.34 us (1%)
    all_to_all x1, blocking collectives, per_device(): x = lax.all_to_all(x, 'field', 0, 0)  42 us
    all_to_all x1, blocking collectives, per_device(): y = lax.all_to_all(y, 'field', 0, 0)  37.4 us
    ppermute x3, starting transfers between devices, dp_sum(): lax.ppermute(total, 'dp', [(i, i ^ flip) for i in range(size)])  6.65 us
    pallas_call x1, Pallas kernels, per_device(): pl.pallas_call(functools.partial(block_kernel, width ** (-0.5), tile, wid...  5.71 us
    pallas_call x1, Pallas kernels, per_device(): pl.pallas_call(pack_kernel, out_shape=jax.ShapeDtypeStruct((fields, each...  4.76 us
    pallas_call x1, Pallas kernels, per_device(): pl.pallas_call(functools.partial(regroup_kernel, samp_rows), out_shape=(j...  3.07 us
    ppermute x3, waiting for transfers between devices, dp_sum(): lax.ppermute(total, 'dp', [(i, i ^ flip) for i in range(size)])  3.02 us
    pallas_call x2, Pallas kernels, per_device(): pl.pallas_call(functools.partial(turn_kernel, part), out_shape=(jax.Shape...  2.15 us
  transfers between devices with their start and end apart: 3, of which 2 were waited for; matrix products, arithmetic and copies ran while one was open for 0% of the time, Pallas kernels for 5%

profile of v4, /device:TPU:0, one launch (start us, length us, event | category | flops | bytes accessed | tf_op | source)
XLA Modules:
  0.0 106.8 jit_solution(12326930739925345313)
XLA Ops:
  1.3 4.8 %shard_map.76 = bf16[16,688,128]{2,1,0:T(8,128)(2,1)} custom-call(bf16[32,192,128]{2,1,0:T(8,128)(2,1)} %bitcast.6, bf16[16,256,128]{2,1,0:T(8,128)(2,1)} %bitcast.7, bf16[32,128]{1,0:T(8,128)(2,1)} %comp_hbm.1, s32[2,72]{1,0:T(2,128)} %bitcast.8, s32[1]{0:T(128)S(6)} %copy.10.counts_ref), custom_call_target="tpu_custom_call" | custom-call | flops 1000000000 | bytes 8000000 | tf_op jit(solution)/shard_map/pallas_call | solution.py:237
  6.0 42.0 %all_to_all.10.x_ref = bf16[16,688,128]{2,1,0:T(8,128)(2,1)S(1)} all-to-all(bf16[16,688,128]{2,1,0:T(8,128)(2,1)} %shard_map.76), channel_id=1, replica_groups=mesh['dp'=8,'field'=16] {'field'}, dimensions={0} | all-to-all | bytes 5636096 | tf_op jit(solution)/shard_map/all_to_all | solution.py:259
  48.0 5.7 %shard_map.77 = bf16[16,672,128]{2,1,0:T(8,128)(2,1)S(1)} custom-call(bf16[16,688,128]{2,1,0:T(8,128)(2,1)S(1)} %all_to_all.10.x_ref), custom_call_target="tpu_custom_call" | custom-call | flops 4000000000 | bytes 6000000 | tf_op jit(solution)/shard_map/pallas_call | solution.py:260
  53.8 37.4 %all_to_all.11.y_ref = bf16[16,672,128]{2,1,0:T(8,128)(2,1)S(1)} all-to-all(bf16[16,672,128]{2,1,0:T(8,128)(2,1)S(1)} %shard_map.77), channel_id=1, replica_groups=mesh['dp'=8,'field'=16] {'field'}, dimensions={0} | all-to-all | bytes 5505024 | tf_op jit(solution)/shard_map/all_to_all | solution.py:275
  91.2 1.6 %collective-permute-start = (f32[32,128]{1,0:T(8,128)S(1)}, f32[32,128]{1,0:T(8,128)S(1)}, u32[]{:S(2)}, u32[]{:S(2)}) collective-permute-start(f32[32,128]{1,0:T(8,128)S(1)} %convert_reduce_fusion), channel_id=1, source_target_pairs={{0,16},{16,0},{32,48},{48,32},{64,80},{80,64},{96,112},{112,96},{1... | collective-permute-start | bytes 49160 | tf_op jit(solution)/shard_map/ppermute | solution.py:215
  92.8 3.1 %shard_map.78 = (bf16[16,256,128]{2,1,0:T(8,128)(2,1)}, f32[6144,128]{1,0:T(8,128)S(1)}) custom-call(bf16[16,672,128]{2,1,0:T(8,128)(2,1)S(1)} %all_to_all.11.y_ref), custom_call_target="tpu_custom_call" | custom-call | flops 1000000000 | bytes 8000000 | tf_op jit(solution)/shard_map/pallas_call | solution.py:279
  95.9 0.0 collective-permute-done
  95.9 2.2 %collective-permute-start.1 = (f32[32,128]{1,0:T(8,128)S(1)}, f32[32,128]{1,0:T(8,128)S(1)}, u32[]{:S(2)}, u32[]{:S(2)}) collective-permute-start(f32[32,128]{1,0:T(8,128)S(1)} %add.9), channel_id=1, source_target_pairs={{0,48},{16,32},{32,16},{48,0},{64,112},{80,96},{96,80},{112,64},{1... | collective-permute-start | bytes 49160 | tf_op jit(solution)/shard_map/ppermute | solution.py:215
  98.1 1.1 %shard_map.79.refs_0_ = bf16[32,192,128]{2,1,0:T(8,128)(2,1)} custom-call(f32[6144,128]{1,0:T(8,128)S(1)} %get-tuple-element.6.turned), custom_call_target="tpu_custom_call" | custom-call | flops 1000000000 | bytes 8000000 | tf_op jit(solution)/shard_map/pallas_call | solution.py:293
  99.1 1.8 %collective-permute-done.1 = f32[32,128]{1,0:T(8,128)S(1)} collective-permute-done((f32[32,128]{1,0:T(8,128)S(1)}, f32[32,128]{1,0:T(8,128)S(1)}, u32[]{:S(2)}, u32[]{:S(2)}) %collective-permute-start.1) | collective-permute-done | bytes 16416 | tf_op jit(solution)/shard_map/ppermute | solution.py:215
  100.9 2.9 %collective-permute-start.2 = (f32[32,128]{1,0:T(8,128)S(1)}, f32[32,128]{1,0:T(8,128)S(1)}, u32[]{:S(2)}, u32[]{:S(2)}) collective-permute-start(f32[32,128]{1,0:T(8,128)S(1)} %add.10), channel_id=1, source_target_pairs={{0,64},{16,80},{32,96},{48,112},{64,0},{80,16},{96,32},{112,48},{1... | collective-permute-start | bytes 49160 | tf_op jit(solution)/shard_map/ppermute | solution.py:215
  103.8 1.1 %shard_map.80 = bf16[32,192,128]{2,1,0:T(8,128)(2,1)} custom-call(f32[6144,128]{1,0:T(8,128)S(1)} %get-tuple-element.6.turned, bf16[32,192,128]{2,1,0:T(8,128)(2,1)} %shard_map.79.refs_0_), custom_call_target="tpu_custom_call", output_to_operand_aliasing={{}: (1, {})} | custom-call | flops 1000000000 | bytes 8000000 | tf_op jit(solution)/shard_map/pallas_call | solution.py:293
  104.9 1.3 %collective-permute-done.2 = f32[32,128]{1,0:T(8,128)S(1)} collective-permute-done((f32[32,128]{1,0:T(8,128)S(1)}, f32[32,128]{1,0:T(8,128)S(1)}, u32[]{:S(2)}, u32[]{:S(2)}) %collective-permute-start.2) | collective-permute-done | bytes 16416 | tf_op jit(solution)/shard_map/ppermute | solution.py:215
  106.2 0.6 add_multiply_fusion
  (3 shorter events, 0.0 us)
Async XLA Ops:
  91.2 4.6 %collective-permute-start = (f32[32,128]{1,0:T(8,128)S(1)}, f32[32,128]{1,0:T(8,128)S(1)}, u32[]{:S(2)}, u32[]{:S(2)}) collective-permute-start(f32[32,128]{1,0:T(8,128)S(1)} %convert_reduce_fusion), channel_id=1, source_target_pairs={{0,16},{16,0},{32,48},{48,32},{64,80},{80,64},{96,112},{112,96},{1... | collective-permute-start | bytes 49160 | tf_op jit(solution)/shard_map/ppermute | solution.py:215
  95.9 5.0 %collective-permute-start.1 = (f32[32,128]{1,0:T(8,128)S(1)}, f32[32,128]{1,0:T(8,128)S(1)}, u32[]{:S(2)}, u32[]{:S(2)}) collective-permute-start(f32[32,128]{1,0:T(8,128)S(1)} %add.9), channel_id=1, source_target_pairs={{0,48},{16,32},{32,16},{48,0},{64,112},{80,96},{96,80},{112,64},{1... | collective-permute-start | bytes 49160 | tf_op jit(solution)/shard_map/ppermute | solution.py:215
  100.9 5.2 %collective-permute-start.2 = (f32[32,128]{1,0:T(8,128)S(1)}, f32[32,128]{1,0:T(8,128)S(1)}, u32[]{:S(2)}, u32[]{:S(2)}) collective-permute-start(f32[32,128]{1,0:T(8,128)S(1)} %add.10), channel_id=1, source_target_pairs={{0,64},{16,80},{32,96},{48,112},{64,0},{80,16},{96,32},{112,48},{1... | collective-permute-start | bytes 49160 | tf_op jit(solution)/shard_map/ppermute | solution.py:215

commit v5 on v4

--- a/solution.py
+++ b/solution.py
@@ -9,8 +9,8 @@
 
 LANES = 128
 GROUPS = 4
-AT_ONCE = 4
-BUTTERFLY = (1, 3, 4)
+AT_ONCE = 8
+ALONG_X = 4
 TABLE = 16
 TURN = (((1,), (1,)), ((), ()))
 MIB = 1024 * 1024
@@ -164,56 +164,62 @@
     y_ref[:, base:] = grad[...].astype(bf16).reshape(fields, tile, LANES)
 
 
-def regroup_kernel(samples, y_ref, mixed_hbm, turned, sem):
-    fields, rows = y_ref.shape[0], turned.shape[0] // samples
-    each = samples // fields
-    copy = pltpu.make_async_copy(
-        y_ref.at[:, pl.ds(each * rows, mixed_hbm.shape[1])], mixed_hbm, sem
-    )
-    copy.start()
-
-    def peer(p, carry):
-        for j in range(each):
-            turned[pl.ds(p * each + j, rows, stride=samples), :] = y_ref[
-                p, j * rows : (j + 1) * rows
-            ].astype(jnp.float32)
-        return carry
-
-    lax.fori_loop(0, fields, peer, 0)
-    copy.wait()
-
-
-def turn_kernel(part, turned, *refs):
-    dfeat_hbm, dfeat, sems = refs[-3:]
+def turn(part, sorted_rows, dfeat_hbm, dfeat, sems):
     tile, width, samples = dfeat.shape
     rest = width - LANES
+    packed = tile + tile // 2
     groups = row_groups(tile)
     share = len(groups) // 2
+
+    def block(row):
+        rows = sorted_rows[pl.ds(row, samples, stride=packed), :]
+        return rows.T.astype(jnp.bfloat16)
+
     copies = []
     for g, (low, high, size) in enumerate(groups[part * share : (part + 1) * share]):
         for r in range(size):
             for row in (low + r, high + r):
-                block = turned[row * samples : (row + 1) * samples].T
-                dfeat[row, :LANES] = block.astype(jnp.bfloat16)
-            place = tile + low + r
-            block = turned[place * samples : (place + 1) * samples].T.astype(jnp.bfloat16)
-            dfeat[low + r, LANES:] = block[:rest]
-            dfeat[high + r, LANES:] = block[rest:]
+                dfeat[row, :LANES] = block(row)
+            both = block(tile + low + r)
+            dfeat[low + r, LANES:] = both[:rest]
+            dfeat[high + r, LANES:] = both[rest:]
         for h, start in enumerate((low, high)):
             copy = pltpu.make_async_copy(
                 dfeat.at[pl.ds(start, size)], dfeat_hbm.at[pl.ds(start, size)], sems.at[2 * g + h]
             )
             copy.start()
             copies.append(copy)
-    for copy in copies:
+    return copies
+
+
+def unpack_kernel(y_ref, mixed_hbm, dfeat_hbm, sorted_rows, dfeat, sems):
+    fields, length = mixed_hbm.shape[:2]
+    share = sorted_rows.shape[0] // fields
+    mixed = pltpu.make_async_copy(
+        y_ref.at[:, pl.ds(share, length)], mixed_hbm, sems.at[GROUPS]
+    )
+    mixed.start()
+    for p in range(fields):
+        sorted_rows[p * share : (p + 1) * share] = y_ref[p, :share].astype(jnp.float32)
+    for copy in turn(0, sorted_rows, dfeat_hbm, dfeat, sems) + [mixed]:
         copy.wait()
 
 
-def dp_sum(total):
+def finish_kernel(sorted_rows, _, dfeat_hbm, dfeat, sems):
+    for copy in turn(1, sorted_rows, dfeat_hbm, dfeat, sems):
+        copy.wait()
+
+
+def dp_sum(own):
     size = lax.axis_size("dp")
-    for flip in [f for f in BUTTERFLY if f < size]:
-        total = total + lax.ppermute(total, "dp", [(i, i ^ flip) for i in range(size)])
-    return total
+
+    def partner(value, flip):
+        return lax.ppermute(value, "dp", [(i, i ^ flip) for i in range(size)])
+
+    if size != 2 * ALONG_X:
+        return lax.psum(own, "dp")
+    total = (own + partner(own, 1)) + (partner(own, 2) + partner(own, 3))
+    return total + partner(total, ALONG_X)
 
 
 def per_device(emb, comp, cot, pairs, counts):
@@ -276,31 +282,30 @@
     grad = dp_sum(jnp.sum(y[:, each * rows :].astype(f32), axis=0))
     weight_grad = grad / (samp_rows * lax.axis_size("dp"))
 
-    mixed, sorted_rows = pl.pallas_call(
-        functools.partial(regroup_kernel, samp_rows),
+    by_row_out = jax.ShapeDtypeStruct((tile, width, samp_rows), bf16)
+    mixed, emb_grad, sorted_rows = pl.pallas_call(
+        unpack_kernel,
         out_shape=(
             jax.ShapeDtypeStruct((fields, each * tile, LANES), bf16),
+            by_row_out,
             jax.ShapeDtypeStruct((packed * samp_rows, LANES), f32),
         ),
         in_specs=[vmem],
-        out_specs=(hbm, vmem),
-        scratch_shapes=[pltpu.SemaphoreType.DMA],
+        out_specs=(hbm, hbm, vmem),
+        scratch_shapes=[by_row, pltpu.SemaphoreType.DMA((GROUPS + 1,))],
         compiler_params=params,
         cost_estimate=cost(10**9, 8 * 10**6),
     )(y)
-    emb_grad = ()
-    for part in range(2):
-        emb_grad = pl.pallas_call(
-            functools.partial(turn_kernel, part),
-            out_shape=(jax.ShapeDtypeStruct((tile, width, samp_rows), bf16),),
-            in_specs=[vmem] + [hbm] * part,
-            out_specs=(hbm,),
-            input_output_aliases={1: 0} if part else {},
-            scratch_shapes=[by_row, pltpu.SemaphoreType.DMA((GROUPS,))],
-            compiler_params=params,
-            cost_estimate=cost(10**9, 8 * 10**6),
-        )(sorted_rows, *emb_grad)
-    (emb_grad,) = emb_grad
+    (emb_grad,) = pl.pallas_call(
+        finish_kernel,
+        out_shape=(by_row_out,),
+        in_specs=[vmem, hbm],
+        out_specs=(hbm,),
+        input_output_aliases={1: 0},
+        scratch_shapes=[by_row, pltpu.SemaphoreType.DMA((GROUPS,))],
+        compiler_params=params,
+        cost_estimate=cost(10**9, 8 * 10**6),
+    )(sorted_rows, emb_grad)
     return mixed.reshape(cot.shape), jnp.transpose(emb_grad, (2, 0, 1)), weight_grad
 
 

time: 107 us -> 105 us (0.981)
  Pallas kernels: 15.7 us -> 13 us
    pallas_call x3 -> x2, Pallas kernels: 5.22 us -> 3.25 us  [the longest x1 1.88 us: per_device(): pl.pallas_call(unpack_kernel, out_shape=(jax.ShapeDtypeStruct((fields, ea...]
    ppermute x3 -> x4, starting transfers between devices: 6.65 us -> 7.15 us  [partner(): return lax.ppermute(value, 'dp', [(i, i ^ flip) for i in range(size)])]
    ppermute x3 -> x4, waiting for transfers between devices: 3.02 us -> 2.98 us  [partner(): return lax.ppermute(value, 'dp', [(i, i ^ flip) for i in range(size)])]
  transfers between devices with their start and end apart: 3 -> 4, of which waited for: 2 -> 2; matrix products, arithmetic and copies ran while one was open for 0% -> 0% of each run, Pallas kernels for 5% -> 3%
where the time goes in v5:
time: 105 us
  blocking collectives  79.4 us (76%)
  Pallas kernels  13 us (12%)
  starting transfers between devices  7.15 us (7%)
  waiting for transfers between devices  2.98 us (3%)
  between operations  1.32 us (1%)
    all_to_all x1, blocking collectives, per_device(): x = lax.all_to_all(x, 'field', 0, 0)  42 us
    all_to_all x1, blocking collectives, per_device(): y = lax.all_to_all(y, 'field', 0, 0)  37.4 us
    ppermute x4, starting transfers between devices, partner(): return lax.ppermute(value, 'dp', [(i, i ^ flip) for i in range(size)])  7.15 us
    pallas_call x1, Pallas kernels, per_device(): pl.pallas_call(functools.partial(block_kernel, width ** (-0.5), tile, wid...  5.04 us
    pallas_call x1, Pallas kernels, per_device(): pl.pallas_call(pack_kernel, out_shape=jax.ShapeDtypeStruct((fields, each...  4.75 us
    ppermute x4, waiting for transfers between devices, partner(): return lax.ppermute(value, 'dp', [(i, i ^ flip) for i in range(size)])  2.98 us
  transfers between devices with their start and end apart: 4, of which 2 were waited for; matrix products, arithmetic and copies ran while one was open for 0% of the time, Pallas kernels for 3%

profile of v5, /device:TPU:0, one launch (start us, length us, event | category | flops | bytes accessed | tf_op | source)
XLA Modules:
  0.0 104.6 jit_solution(14637119442370352791)
XLA Ops:
  1.3 4.8 %shard_map.76 = bf16[16,688,128]{2,1,0:T(8,128)(2,1)} custom-call(bf16[32,192,128]{2,1,0:T(8,128)(2,1)} %bitcast.5, bf16[16,256,128]{2,1,0:T(8,128)(2,1)} %bitcast.7, bf16[32,128]{1,0:T(8,128)(2,1)} %comp_hbm.1, s32[2,72]{1,0:T(2,128)} %bitcast.8, s32[1]{0:T(128)S(6)} %copy.10.counts_ref), custom_call_target="tpu_custom_call" | custom-call | flops 1000000000 | bytes 8000000 | tf_op jit(solution)/shard_map/pallas_call | solution.py:243
  6.0 42.0 %all_to_all.10.x_ref = bf16[16,688,128]{2,1,0:T(8,128)(2,1)S(1)} all-to-all(bf16[16,688,128]{2,1,0:T(8,128)(2,1)} %shard_map.76), channel_id=1, replica_groups=mesh['dp'=8,'field'=16] {'field'}, dimensions={0} | all-to-all | bytes 5636096 | tf_op jit(solution)/shard_map/all_to_all | solution.py:265
  48.0 5.0 %shard_map.77 = bf16[16,672,128]{2,1,0:T(8,128)(2,1)S(1)} custom-call(bf16[16,688,128]{2,1,0:T(8,128)(2,1)S(1)} %all_to_all.10.x_ref), custom_call_target="tpu_custom_call" | custom-call | flops 4000000000 | bytes 6000000 | tf_op jit(solution)/shard_map/pallas_call | solution.py:266
  53.1 37.4 %all_to_all.11.y_ref = bf16[16,672,128]{2,1,0:T(8,128)(2,1)S(1)} all-to-all(bf16[16,672,128]{2,1,0:T(8,128)(2,1)S(1)} %shard_map.77), channel_id=1, replica_groups=mesh['dp'=8,'field'=16] {'field'}, dimensions={0} | all-to-all | bytes 5505024 | tf_op jit(solution)/shard_map/all_to_all | solution.py:281
  90.5 2.8 %collective-permute-start.2 = (f32[32,128]{1,0:T(8,128)S(1)}, f32[32,128]{1,0:T(8,128)S(1)}, u32[]{:S(2)}, u32[]{:S(2)}) collective-permute-start(f32[32,128]{1,0:T(8,128)S(1)} %convert_reduce_fusion), channel_id=1, source_target_pairs={{0,48},{16,32},{32,16},{48,0},{64,112},{80,96},{96,80},{112,64},{1... | collective-permute-start | bytes 49160 | tf_op jit(solution)/shard_map/ppermute | solution.py:217
  93.4 0.8 collective-permute-start.1
  94.2 0.5 collective-permute-start
  94.7 1.9 %shard_map.78 = (bf16[16,256,128]{2,1,0:T(8,128)(2,1)}, bf16[32,192,128]{2,1,0:T(8,128)(2,1)}, f32[6144,128]{1,0:T(8,128)S(1)}) custom-call(bf16[16,672,128]{2,1,0:T(8,128)(2,1)S(1)} %all_to_all.11.y_ref), custom_call_target="tpu_custom_call" | custom-call | flops 1000000000 | bytes 8000000 | tf_op jit(solution)/shard_map/pallas_call | solution.py:286
  96.6 0.0 collective-permute-done.2
  96.6 2.0 %collective-permute-done.1 = f32[32,128]{1,0:T(8,128)S(1)} collective-permute-done((f32[32,128]{1,0:T(8,128)S(1)}, f32[32,128]{1,0:T(8,128)S(1)}, u32[]{:S(2)}, u32[]{:S(2)}) %collective-permute-start.1) | collective-permute-done | bytes 16416 | tf_op jit(solution)/shard_map/ppermute | solution.py:217
  98.6 0.0 collective-permute-done
  98.6 3.0 %collective-permute-start.3 = (f32[32,128]{1,0:T(8,128)S(1)}, f32[32,128]{1,0:T(8,128)S(1)}, u32[]{:S(2)}, u32[]{:S(2)}) collective-permute-start(f32[32,128]{1,0:T(8,128)S(1)} %add_add_fusion), channel_id=1, source_target_pairs={{0,64},{16,80},{32,96},{48,112},{64,0},{80,16},{96,32},{112,48},{1... | collective-permute-start | bytes 49160 | tf_op jit(solution)/shard_map/ppermute | solution.py:217
  101.6 1.4 %shard_map.79 = bf16[32,192,128]{2,1,0:T(8,128)(2,1)} custom-call(f32[6144,128]{1,0:T(8,128)S(1)} %get-tuple-element.7.sorted_rows, bf16[32,192,128]{2,1,0:T(8,128)(2,1)} %get-tuple-element.8._), custom_call_target="tpu_custom_call", output_to_operand_aliasing={{}: (1, {})} | custom-call | flops 1000000000 | bytes 8000000 | tf_op jit(solution)/shard_map/pallas_call | solution.py:299
  103.0 1.0 collective-permute-done.3
  103.9 0.6 add_multiply_fusion
  (2 shorter events, 0.0 us)
Async XLA Ops:
  90.5 6.1 %collective-permute-start.2 = (f32[32,128]{1,0:T(8,128)S(1)}, f32[32,128]{1,0:T(8,128)S(1)}, u32[]{:S(2)}, u32[]{:S(2)}) collective-permute-start(f32[32,128]{1,0:T(8,128)S(1)} %convert_reduce_fusion), channel_id=1, source_target_pairs={{0,48},{16,32},{32,16},{48,0},{64,112},{80,96},{96,80},{112,64},{1... | collective-permute-start | bytes 49160 | tf_op jit(solution)/shard_map/ppermute | solution.py:217
  93.4 5.2 %collective-permute-start.1 = (f32[32,128]{1,0:T(8,128)S(1)}, f32[32,128]{1,0:T(8,128)S(1)}, u32[]{:S(2)}, u32[]{:S(2)}) collective-permute-start(f32[32,128]{1,0:T(8,128)S(1)} %convert_reduce_fusion), channel_id=1, source_target_pairs={{0,32},{16,48},{32,0},{48,16},{64,96},{80,112},{96,64},{112,80},{1... | collective-permute-start | bytes 49160 | tf_op jit(solution)/shard_map/ppermute | solution.py:217
  94.2 4.4 %collective-permute-start = (f32[32,128]{1,0:T(8,128)S(1)}, f32[32,128]{1,0:T(8,128)S(1)}, u32[]{:S(2)}, u32[]{:S(2)}) collective-permute-start(f32[32,128]{1,0:T(8,128)S(1)} %convert_reduce_fusion), channel_id=1, source_target_pairs={{0,16},{16,0},{32,48},{48,32},{64,80},{80,64},{96,112},{112,96},{1... | collective-permute-start | bytes 49160 | tf_op jit(solution)/shard_map/ppermute | solution.py:217
  98.6 5.3 %collective-permute-start.3 = (f32[32,128]{1,0:T(8,128)S(1)}, f32[32,128]{1,0:T(8,128)S(1)}, u32[]{:S(2)}, u32[]{:S(2)}) collective-permute-start(f32[32,128]{1,0:T(8,128)S(1)} %add_add_fusion), channel_id=1, source_target_pairs={{0,64},{16,80},{32,96},{48,112},{64,0},{80,16},{96,32},{112,48},{1... | collective-permute-start | bytes 49160 | tf_op jit(solution)/shard_map/ppermute | solution.py:217

commit v6 on v5

--- a/solution.py
+++ b/solution.py
@@ -72,7 +72,7 @@
                 ),
             ]
             for place, block in blocks:
-                turned[place * samples : (place + 1) * samples] = block.astype(f32).T
+                turned[place * samples : (place + 1) * samples] = block.T.astype(f32)
     direct.wait()
     stores = []
     for g in range(GROUPS):
@@ -173,7 +173,7 @@
 
     def block(row):
         rows = sorted_rows[pl.ds(row, samples, stride=packed), :]
-        return rows.T.astype(jnp.bfloat16)
+        return rows.astype(jnp.bfloat16).T
 
     copies = []
     for g, (low, high, size) in enumerate(groups[part * share : (part + 1) * share]):
@@ -218,8 +218,8 @@
 
     if size != 2 * ALONG_X:
         return lax.psum(own, "dp")
-    total = (own + partner(own, 1)) + (partner(own, 2) + partner(own, 3))
-    return total + partner(total, ALONG_X)
+    total = own + partner(own, ALONG_X)
+    return (total + partner(total, 1)) + (partner(total, 2) + partner(total, 3))
 
 
 def per_device(emb, comp, cot, pairs, counts):

time: 105 us -> 105 us (level)
  no operation moved by 1% of the time
where the time goes in v6:
time: 105 us; the launch traced here: 104 us
  blocking collectives  79.4 us (76%)
  Pallas kernels  12.9 us (12%)
  starting transfers between devices  7.07 us (7%)
  waiting for transfers between devices  3.1 us (3%)
  between operations  1.32 us (1%)
    all_to_all x1, blocking collectives, per_device(): x = lax.all_to_all(x, 'field', 0, 0)  42 us
    all_to_all x1, blocking collectives, per_device(): y = lax.all_to_all(y, 'field', 0, 0)  37.4 us
    ppermute x4, starting transfers between devices, partner(): return lax.ppermute(value, 'dp', [(i, i ^ flip) for i in range(size)])  7.07 us
    pallas_call x1, Pallas kernels, per_device(): pl.pallas_call(functools.partial(block_kernel, width ** (-0.5), tile, wid...  5.04 us
    pallas_call x1, Pallas kernels, per_device(): pl.pallas_call(pack_kernel, out_shape=jax.ShapeDtypeStruct((fields, each...  4.75 us
    ppermute x4, waiting for transfers between devices, partner(): return lax.ppermute(value, 'dp', [(i, i ^ flip) for i in range(size)])  3.1 us
  transfers between devices with their start and end apart: 4, of which 2 were waited for; matrix products, arithmetic and copies ran while one was open for 0% of the time, Pallas kernels for 3%

profile of v6, /device:TPU:0, one launch (start us, length us, event | category | flops | bytes accessed | tf_op | source)
XLA Modules:
  0.0 104.5 jit_solution(5418380077037688084)
XLA Ops:
  1.3 4.8 %shard_map.76 = bf16[16,688,128]{2,1,0:T(8,128)(2,1)} custom-call(bf16[32,192,128]{2,1,0:T(8,128)(2,1)} %bitcast.5, bf16[16,256,128]{2,1,0:T(8,128)(2,1)} %bitcast.7, bf16[32,128]{1,0:T(8,128)(2,1)} %comp_hbm.1, s32[2,72]{1,0:T(2,128)} %bitcast.8, s32[1]{0:T(128)S(6)} %copy.10.counts_ref), custom_call_target="tpu_custom_call" | custom-call | flops 1000000000 | bytes 8000000 | tf_op jit(solution)/shard_map/pallas_call | solution.py:243
  6.0 42.0 %all_to_all.10.x_ref = bf16[16,688,128]{2,1,0:T(8,128)(2,1)S(1)} all-to-all(bf16[16,688,128]{2,1,0:T(8,128)(2,1)} %shard_map.76), channel_id=1, replica_groups=mesh['dp'=8,'field'=16] {'field'}, dimensions={0} | all-to-all | bytes 5636096 | tf_op jit(solution)/shard_map/all_to_all | solution.py:265
  48.0 5.0 %shard_map.77 = bf16[16,672,128]{2,1,0:T(8,128)(2,1)S(1)} custom-call(bf16[16,688,128]{2,1,0:T(8,128)(2,1)S(1)} %all_to_all.10.x_ref), custom_call_target="tpu_custom_call" | custom-call | flops 4000000000 | bytes 6000000 | tf_op jit(solution)/shard_map/pallas_call | solution.py:266
  53.1 37.4 %all_to_all.11.y_ref = bf16[16,672,128]{2,1,0:T(8,128)(2,1)S(1)} all-to-all(bf16[16,672,128]{2,1,0:T(8,128)(2,1)S(1)} %shard_map.77), channel_id=1, replica_groups=mesh['dp'=8,'field'=16] {'field'}, dimensions={0} | all-to-all | bytes 5505024 | tf_op jit(solution)/shard_map/all_to_all | solution.py:281
  90.5 3.0 %collective-permute-start = (f32[32,128]{1,0:T(8,128)S(1)}, f32[32,128]{1,0:T(8,128)S(1)}, u32[]{:S(2)}, u32[]{:S(2)}) collective-permute-start(f32[32,128]{1,0:T(8,128)S(1)} %convert_reduce_fusion), channel_id=1, source_target_pairs={{0,64},{16,80},{32,96},{48,112},{64,0},{80,16},{96,32},{112,48},{1... | collective-permute-start | bytes 49160 | tf_op jit(solution)/shard_map/ppermute | solution.py:217
  93.5 1.7 %shard_map.78 = (bf16[16,256,128]{2,1,0:T(8,128)(2,1)}, bf16[32,192,128]{2,1,0:T(8,128)(2,1)}, f32[6144,128]{1,0:T(8,128)S(1)}) custom-call(bf16[16,672,128]{2,1,0:T(8,128)(2,1)S(1)} %all_to_all.11.y_ref), custom_call_target="tpu_custom_call" | custom-call | flops 1000000000 | bytes 8000000 | tf_op jit(solution)/shard_map/pallas_call | solution.py:286
  95.2 0.7 collective-permute-done
  95.9 2.8 %collective-permute-start.3 = (f32[32,128]{1,0:T(8,128)S(1)}, f32[32,128]{1,0:T(8,128)S(1)}, u32[]{:S(2)}, u32[]{:S(2)}) collective-permute-start(f32[32,128]{1,0:T(8,128)S(1)} %add.12), channel_id=1, source_target_pairs={{0,48},{16,32},{32,16},{48,0},{64,112},{80,96},{96,80},{112,64},{1... | collective-permute-start | bytes 49160 | tf_op jit(solution)/shard_map/ppermute | solution.py:217
  98.6 0.8 collective-permute-start.2
  99.4 0.5 collective-permute-start.1
  99.9 1.5 %shard_map.79 = bf16[32,192,128]{2,1,0:T(8,128)(2,1)} custom-call(f32[6144,128]{1,0:T(8,128)S(1)} %get-tuple-element.7.sorted_rows, bf16[32,192,128]{2,1,0:T(8,128)(2,1)} %get-tuple-element.8._), custom_call_target="tpu_custom_call", output_to_operand_aliasing={{}: (1, {})} | custom-call | flops 1000000000 | bytes 8000000 | tf_op jit(solution)/shard_map/pallas_call | solution.py:299
  101.4 0.0 collective-permute-done.3
  101.4 2.4 %collective-permute-done.2 = f32[32,128]{1,0:T(8,128)S(1)} collective-permute-done((f32[32,128]{1,0:T(8,128)S(1)}, f32[32,128]{1,0:T(8,128)S(1)}, u32[]{:S(2)}, u32[]{:S(2)}) %collective-permute-start.2) | collective-permute-done | bytes 16416 | tf_op jit(solution)/shard_map/ppermute | solution.py:217
  103.9 0.0 collective-permute-done.1
  103.9 0.6 add_multiply_fusion
  (2 shorter events, 0.0 us)
Async XLA Ops:
  90.5 5.3 %collective-permute-start = (f32[32,128]{1,0:T(8,128)S(1)}, f32[32,128]{1,0:T(8,128)S(1)}, u32[]{:S(2)}, u32[]{:S(2)}) collective-permute-start(f32[32,128]{1,0:T(8,128)S(1)} %convert_reduce_fusion), channel_id=1, source_target_pairs={{0,64},{16,80},{32,96},{48,112},{64,0},{80,16},{96,32},{112,48},{1... | collective-permute-start | bytes 49160 | tf_op jit(solution)/shard_map/ppermute | solution.py:217
  95.9 5.6 %collective-permute-start.3 = (f32[32,128]{1,0:T(8,128)S(1)}, f32[32,128]{1,0:T(8,128)S(1)}, u32[]{:S(2)}, u32[]{:S(2)}) collective-permute-start(f32[32,128]{1,0:T(8,128)S(1)} %add.12), channel_id=1, source_target_pairs={{0,48},{16,32},{32,16},{48,0},{64,112},{80,96},{96,80},{112,64},{1... | collective-permute-start | bytes 49160 | tf_op jit(solution)/shard_map/ppermute | solution.py:217
  98.6 5.2 %collective-permute-start.2 = (f32[32,128]{1,0:T(8,128)S(1)}, f32[32,128]{1,0:T(8,128)S(1)}, u32[]{:S(2)}, u32[]{:S(2)}) collective-permute-start(f32[32,128]{1,0:T(8,128)S(1)} %add.12), channel_id=1, source_target_pairs={{0,32},{16,48},{32,0},{48,16},{64,96},{80,112},{96,64},{112,80},{1... | collective-permute-start | bytes 49160 | tf_op jit(solution)/shard_map/ppermute | solution.py:217
  99.4 4.4 %collective-permute-start.1 = (f32[32,128]{1,0:T(8,128)S(1)}, f32[32,128]{1,0:T(8,128)S(1)}, u32[]{:S(2)}, u32[]{:S(2)}) collective-permute-start(f32[32,128]{1,0:T(8,128)S(1)} %add.12), channel_id=1, source_target_pairs={{0,16},{16,0},{32,48},{48,32},{64,80},{80,64},{96,112},{112,96},{1... | collective-permute-start | bytes 49160 | tf_op jit(solution)/shard_map/ppermute | solution.py:217

commit v7 on v6

--- a/solution.py
+++ b/solution.py
@@ -8,9 +8,8 @@
 from jax.sharding import PartitionSpec as P
 
 LANES = 128
-GROUPS = 4
+GROUPS = 8
 AT_ONCE = 8
-ALONG_X = 4
 TABLE = 16
 TURN = (((1,), (1,)), ((), ()))
 MIB = 1024 * 1024
@@ -212,14 +211,8 @@
 
 def dp_sum(own):
     size = lax.axis_size("dp")
-
-    def partner(value, flip):
-        return lax.ppermute(value, "dp", [(i, i ^ flip) for i in range(size)])
-
-    if size != 2 * ALONG_X:
-        return lax.psum(own, "dp")
-    total = own + partner(own, ALONG_X)
-    return (total + partner(total, 1)) + (partner(total, 2) + partner(total, 3))
+    copies = lax.optimization_barrier(jnp.broadcast_to(own, (size,) + own.shape))
+    return jnp.sum(lax.all_to_all(copies, "dp", 0, 0), axis=0)
 
 
 def per_device(emb, comp, cot, pairs, counts):
@@ -281,6 +274,7 @@
     y = lax.all_to_all(y, "field", 0, 0)
     grad = dp_sum(jnp.sum(y[:, each * rows :].astype(f32), axis=0))
     weight_grad = grad / (samp_rows * lax.axis_size("dp"))
+    y, weight_grad = lax.optimization_barrier((y, weight_grad))
 
     by_row_out = jax.ShapeDtypeStruct((tile, width, samp_rows), bf16)
     mixed, emb_grad, sorted_rows = pl.pallas_call(

time: 105 us -> 109 us (1.038)
  blocking collectives: 79.4 us -> 93.9 us
  starting transfers between devices: 7.07 us -> 0 us
  waiting for transfers between devices: 3.1 us -> 0 us
    all_to_all x0 -> x1, blocking collectives: none -> 14.5 us  [dp_sum(): return jnp.sum(lax.all_to_all(copies, 'dp', 0, 0), axis=0)]
    ppermute x4 -> x0, starting transfers between devices: 7.07 us -> none  [partner(): return lax.ppermute(value, 'dp', [(i, i ^ flip) for i in range(size)])]
    ppermute x4 -> x0, waiting for transfers between devices: 3.1 us -> none  [partner(): return lax.ppermute(value, 'dp', [(i, i ^ flip) for i in range(size)])]
  transfers between devices with their start and end apart: 4 -> 0, of which waited for: 2 -> 0; matrix products, arithmetic and copies ran while one was open for 0% -> 0% of each run, Pallas kernels for 3% -> 0%
where the time goes in v7:
time: 109 us
  blocking collectives  93.9 us (86%)
  Pallas kernels  12.9 us (12%)
  between operations  1.31 us (1%)
    all_to_all x1, blocking collectives, per_device(): x = lax.all_to_all(x, 'field', 0, 0)  42 us
    all_to_all x1, blocking collectives, per_device(): y = lax.all_to_all(y, 'field', 0, 0)  37.4 us
    all_to_all x1, blocking collectives, dp_sum(): return jnp.sum(lax.all_to_all(copies, 'dp', 0, 0), axis=0)  14.5 us
    pallas_call x1, Pallas kernels, per_device(): pl.pallas_call(functools.partial(block_kernel, width ** (-0.5), tile, wid...  5.04 us
    pallas_call x1, Pallas kernels, per_device(): pl.pallas_call(pack_kernel, out_shape=jax.ShapeDtypeStruct((fields, each...  4.73 us

profile of v7, /device:TPU:0, one launch (start us, length us, event | category | flops | bytes accessed | tf_op | source)
XLA Modules:
  0.0 108.8 jit_solution(17869433607738322070)
XLA Ops:
  1.3 4.7 %shard_map.76 = bf16[16,688,128]{2,1,0:T(8,128)(2,1)} custom-call(bf16[32,192,128]{2,1,0:T(8,128)(2,1)} %bitcast.5, bf16[16,256,128]{2,1,0:T(8,128)(2,1)} %bitcast.7, bf16[32,128]{1,0:T(8,128)(2,1)} %comp_hbm.1, s32[2,72]{1,0:T(2,128)} %bitcast.8, s32[1]{0:T(128)S(6)} %copy.10.counts_ref), custom_call_target="tpu_custom_call" | custom-call | flops 1000000000 | bytes 8000000 | tf_op jit(solution)/shard_map/pallas_call | solution.py:236
  6.0 42.0 %all_to_all.15.x_ref = bf16[16,688,128]{2,1,0:T(8,128)(2,1)S(1)} all-to-all(bf16[16,688,128]{2,1,0:T(8,128)(2,1)} %shard_map.76), channel_id=1, replica_groups=mesh['dp'=8,'field'=16] {'field'}, dimensions={0} | all-to-all | bytes 5636096 | tf_op jit(solution)/shard_map/all_to_all | solution.py:258
  48.0 5.0 %shard_map.77 = bf16[16,672,128]{2,1,0:T(8,128)(2,1)S(1)} custom-call(bf16[16,688,128]{2,1,0:T(8,128)(2,1)S(1)} %all_to_all.15.x_ref), custom_call_target="tpu_custom_call" | custom-call | flops 4000000000 | bytes 6000000 | tf_op jit(solution)/shard_map/pallas_call | solution.py:259
  53.0 37.4 %all_to_all.16.y_ref = bf16[16,672,128]{2,1,0:T(8,128)(2,1)S(1)} all-to-all(bf16[16,672,128]{2,1,0:T(8,128)(2,1)S(1)} %shard_map.77), channel_id=1, replica_groups=mesh['dp'=8,'field'=16] {'field'}, dimensions={0} | all-to-all | bytes 5505024 | tf_op jit(solution)/shard_map/all_to_all | solution.py:274
  90.5 14.5 %all_to_all.17 = f32[8,32,128]{2,1,0:T(8,128)S(1)} all-to-all(f32[8,32,128]{2,1,0:T(8,128)S(1)} %broadcast_in_dim.3), channel_id=1, replica_groups=mesh['dp'=8,'field'=16] {'dp'}, dimensions={0} | all-to-all | bytes 262144 | tf_op jit(solution)/shard_map/all_to_all | solution.py:215
  105.1 0.6 broadcast_multiply_fusion
  105.7 1.7 %shard_map.78 = (bf16[16,256,128]{2,1,0:T(8,128)(2,1)}, bf16[32,192,128]{2,1,0:T(8,128)(2,1)}, f32[6144,128]{1,0:T(8,128)S(1)}) custom-call(bf16[16,672,128]{2,1,0:T(8,128)(2,1)S(1)} %all_to_all.16.y_ref), custom_call_target="tpu_custom_call" | custom-call | flops 1000000000 | bytes 8000000 | tf_op jit(solution)/shard_map/pallas_call | solution.py:280
  107.4 1.4 %shard_map.79 = bf16[32,192,128]{2,1,0:T(8,128)(2,1)} custom-call(f32[6144,128]{1,0:T(8,128)S(1)} %get-tuple-element.10.sorted_rows, bf16[32,192,128]{2,1,0:T(8,128)(2,1)} %get-tuple-element.11._), custom_call_target="tpu_custom_call", output_to_operand_aliasing={{}: (1, {})} | custom-call | flops 1000000000 | bytes 8000000 | tf_op jit(solution)/shard_map/pallas_call | solution.py:293
  (3 shorter events, 0.0 us)

commit v8 on v6

--- a/solution.py
+++ b/solution.py
@@ -45,7 +45,7 @@
     direct = pltpu.make_async_copy(
         cot_hbm, message.at[:, pl.ds(each * packed, each * tile)], sems.at[2 * GROUPS + 2]
     )
-    for copy in loads[:2] + small + loads[2:] + [direct]:
+    for copy in small + loads[:2] + [direct] + loads[2:]:
         copy.start()
     for copy in small:
         copy.wait()
@@ -59,7 +59,17 @@
     for p in range(fields):
         message[p, base : base + tile] = comp[...]
         message[p, base + tile : base + tile + TABLE] = table[:TABLE].astype(bf16)
+    stores = []
     for g, (low, high, size) in enumerate(groups):
+        if g == 1:
+            direct.wait()
+            later = pl.ds(each * packed, each * tile + tile + TABLE)
+            stores.append(
+                pltpu.make_async_copy(
+                    message.at[:, later], out_hbm.at[:, later], sems.at[3 * GROUPS + 3]
+                )
+            )
+            stores[-1].start()
         loads[2 * g].wait()
         loads[2 * g + 1].wait()
         for r in range(size):
@@ -73,8 +83,6 @@
             ]
             for place, block in blocks:
                 turned[place * samples : (place + 1) * samples] = block.T.astype(f32)
-    direct.wait()
-    stores = []
     for g in range(GROUPS):
         some = fields // GROUPS
 
@@ -85,7 +93,7 @@
             return carry
 
         lax.fori_loop(g * some, (g + 1) * some, peer, 0)
-        here = pl.ds(g * some, some)
+        here = (pl.ds(g * some, some), pl.ds(0, each * packed))
         stores.append(
             pltpu.make_async_copy(message.at[here], out_hbm.at[here], sems.at[2 * GROUPS + 3 + g])
         )
@@ -219,7 +227,9 @@
     if size != 2 * ALONG_X:
         return lax.psum(own, "dp")
     total = own + partner(own, ALONG_X)
-    return (total + partner(total, 1)) + (partner(total, 2) + partner(total, 3))
+    first, third = partner(total, 1), partner(total, 3)
+    second = partner(total, 2)
+    return (first + third) + (total + second)
 
 
 def per_device(emb, comp, cot, pairs, counts):
@@ -251,7 +261,7 @@
             pltpu.VMEM(pairs.shape[::-1], jnp.int32),
             turned,
             pltpu.VMEM((fields, each * rows + tile + TABLE, LANES), bf16),
-            pltpu.SemaphoreType.DMA((3 * GROUPS + 3,)),
+            pltpu.SemaphoreType.DMA((3 * GROUPS + 4,)),
         ],
         compiler_params=pltpu.CompilerParams(vmem_limit_bytes=56 * MIB),
         cost_estimate=cost(10**9, 8 * 10**6),

time: 105 us -> 105 us (level)
  no operation moved by 1% of the time
where the time goes in v8:
time: 105 us; the launch traced here: 104 us
  blocking collectives  79.4 us (76%)
  Pallas kernels  13 us (12%)
  starting transfers between devices  7.15 us (7%)
  waiting for transfers between devices  3 us (3%)
  between operations  1.32 us (1%)
    all_to_all x1, blocking collectives, per_device(): x = lax.all_to_all(x, 'field', 0, 0)  42 us
    all_to_all x1, blocking collectives, per_device(): y = lax.all_to_all(y, 'field', 0, 0)  37.4 us
    ppermute x4, starting transfers between devices, partner(): return lax.ppermute(value, 'dp', [(i, i ^ flip) for i in range(size)])  7.15 us
    pallas_call x1, Pallas kernels, per_device(): pl.pallas_call(functools.partial(block_kernel, width ** (-0.5), tile, wid...  5.04 us
    pallas_call x1, Pallas kernels, per_device(): pl.pallas_call(pack_kernel, out_shape=jax.ShapeDtypeStruct((fields, each...  4.79 us
    ppermute x4, waiting for transfers between devices, partner(): return lax.ppermute(value, 'dp', [(i, i ^ flip) for i in range(size)])  3 us
  transfers between devices with their start and end apart: 4, of which 2 were waited for; matrix products, arithmetic and copies ran while one was open for 0% of the time, Pallas kernels for 3%

profile of v8, /device:TPU:0, one launch (start us, length us, event | category | flops | bytes accessed | tf_op | source)
XLA Modules:
  0.0 104.5 jit_solution(11648009381431171965)
XLA Ops:
  1.3 4.8 %shard_map.76 = bf16[16,688,128]{2,1,0:T(8,128)(2,1)} custom-call(bf16[32,192,128]{2,1,0:T(8,128)(2,1)} %bitcast.5, bf16[16,256,128]{2,1,0:T(8,128)(2,1)} %bitcast.7, bf16[32,128]{1,0:T(8,128)(2,1)} %comp_hbm.1, s32[2,72]{1,0:T(2,128)} %bitcast.8, s32[1]{0:T(128)S(6)} %copy.10.counts_ref), custom_call_target="tpu_custom_call" | custom-call | flops 1000000000 | bytes 8000000 | tf_op jit(solution)/shard_map/pallas_call | solution.py:253
  6.1 42.0 %all_to_all.10.x_ref = bf16[16,688,128]{2,1,0:T(8,128)(2,1)S(1)} all-to-all(bf16[16,688,128]{2,1,0:T(8,128)(2,1)} %shard_map.76), channel_id=1, replica_groups=mesh['dp'=8,'field'=16] {'field'}, dimensions={0} | all-to-all | bytes 5636096 | tf_op jit(solution)/shard_map/all_to_all | solution.py:275
  48.1 5.0 %shard_map.77 = bf16[16,672,128]{2,1,0:T(8,128)(2,1)S(1)} custom-call(bf16[16,688,128]{2,1,0:T(8,128)(2,1)S(1)} %all_to_all.10.x_ref), custom_call_target="tpu_custom_call" | custom-call | flops 4000000000 | bytes 6000000 | tf_op jit(solution)/shard_map/pallas_call | solution.py:276
  53.1 37.4 %all_to_all.11.y_ref = bf16[16,672,128]{2,1,0:T(8,128)(2,1)S(1)} all-to-all(bf16[16,672,128]{2,1,0:T(8,128)(2,1)S(1)} %shard_map.77), channel_id=1, replica_groups=mesh['dp'=8,'field'=16] {'field'}, dimensions={0} | all-to-all | bytes 5505024 | tf_op jit(solution)/shard_map/all_to_all | solution.py:291
  90.6 3.0 %collective-permute-start = (f32[32,128]{1,0:T(8,128)S(1)}, f32[32,128]{1,0:T(8,128)S(1)}, u32[]{:S(2)}, u32[]{:S(2)}) collective-permute-start(f32[32,128]{1,0:T(8,128)S(1)} %convert_reduce_fusion), channel_id=1, source_target_pairs={{0,64},{16,80},{32,96},{48,112},{64,0},{80,16},{96,32},{112,48},{1... | collective-permute-start | bytes 49160 | tf_op jit(solution)/shard_map/ppermute | solution.py:225
  93.5 1.7 %shard_map.78 = (bf16[16,256,128]{2,1,0:T(8,128)(2,1)}, bf16[32,192,128]{2,1,0:T(8,128)(2,1)}, f32[6144,128]{1,0:T(8,128)S(1)}) custom-call(bf16[16,672,128]{2,1,0:T(8,128)(2,1)S(1)} %all_to_all.11.y_ref), custom_call_target="tpu_custom_call" | custom-call | flops 1000000000 | bytes 8000000 | tf_op jit(solution)/shard_map/pallas_call | solution.py:296
  95.2 0.7 collective-permute-done
  95.9 3.0 %collective-permute-start.3 = (f32[32,128]{1,0:T(8,128)S(1)}, f32[32,128]{1,0:T(8,128)S(1)}, u32[]{:S(2)}, u32[]{:S(2)}) collective-permute-start(f32[32,128]{1,0:T(8,128)S(1)} %add.12), channel_id=1, source_target_pairs={{0,32},{16,48},{32,0},{48,16},{64,96},{80,112},{96,64},{112,80},{1... | collective-permute-start | bytes 49160 | tf_op jit(solution)/shard_map/ppermute | solution.py:225
  98.9 1.1 %collective-permute-start.2 = (f32[32,128]{1,0:T(8,128)S(1)}, f32[32,128]{1,0:T(8,128)S(1)}, u32[]{:S(2)}, u32[]{:S(2)}) collective-permute-start(f32[32,128]{1,0:T(8,128)S(1)} %add.12), channel_id=1, source_target_pairs={{0,48},{16,32},{32,16},{48,0},{64,112},{80,96},{96,80},{112,64},{1... | collective-permute-start | bytes 49160 | tf_op jit(solution)/shard_map/ppermute | solution.py:225
  100.0 0.0 collective-permute-start.1
  100.1 1.5 %shard_map.79 = bf16[32,192,128]{2,1,0:T(8,128)(2,1)} custom-call(f32[6144,128]{1,0:T(8,128)S(1)} %get-tuple-element.7.sorted_rows, bf16[32,192,128]{2,1,0:T(8,128)(2,1)} %get-tuple-element.8._), custom_call_target="tpu_custom_call", output_to_operand_aliasing={{}: (1, {})} | custom-call | flops 1000000000 | bytes 8000000 | tf_op jit(solution)/shard_map/pallas_call | solution.py:309
  101.5 0.0 collective-permute-done.3
  101.5 2.3 %collective-permute-done.2 = f32[32,128]{1,0:T(8,128)S(1)} collective-permute-done((f32[32,128]{1,0:T(8,128)S(1)}, f32[32,128]{1,0:T(8,128)S(1)}, u32[]{:S(2)}, u32[]{:S(2)}) %collective-permute-start.2) | collective-permute-done | bytes 16416 | tf_op jit(solution)/shard_map/ppermute | solution.py:225
  103.9 0.0 collective-permute-done.1
  103.9 0.6 add_multiply_fusion
  (2 shorter events, 0.0 us)
Async XLA Ops:
  90.6 5.3 %collective-permute-start = (f32[32,128]{1,0:T(8,128)S(1)}, f32[32,128]{1,0:T(8,128)S(1)}, u32[]{:S(2)}, u32[]{:S(2)}) collective-permute-start(f32[32,128]{1,0:T(8,128)S(1)} %convert_reduce_fusion), channel_id=1, source_target_pairs={{0,64},{16,80},{32,96},{48,112},{64,0},{80,16},{96,32},{112,48},{1... | collective-permute-start | bytes 49160 | tf_op jit(solution)/shard_map/ppermute | solution.py:225
  95.9 5.6 %collective-permute-start.3 = (f32[32,128]{1,0:T(8,128)S(1)}, f32[32,128]{1,0:T(8,128)S(1)}, u32[]{:S(2)}, u32[]{:S(2)}) collective-permute-start(f32[32,128]{1,0:T(8,128)S(1)} %add.12), channel_id=1, source_target_pairs={{0,32},{16,48},{32,0},{48,16},{64,96},{80,112},{96,64},{112,80},{1... | collective-permute-start | bytes 49160 | tf_op jit(solution)/shard_map/ppermute | solution.py:225
  98.9 4.9 %collective-permute-start.2 = (f32[32,128]{1,0:T(8,128)S(1)}, f32[32,128]{1,0:T(8,128)S(1)}, u32[]{:S(2)}, u32[]{:S(2)}) collective-permute-start(f32[32,128]{1,0:T(8,128)S(1)} %add.12), channel_id=1, source_target_pairs={{0,48},{16,32},{32,16},{48,0},{64,112},{80,96},{96,80},{112,64},{1... | collective-permute-start | bytes 49160 | tf_op jit(solution)/shard_map/ppermute | solution.py:225
  100.0 3.8 %collective-permute-start.1 = (f32[32,128]{1,0:T(8,128)S(1)}, f32[32,128]{1,0:T(8,128)S(1)}, u32[]{:S(2)}, u32[]{:S(2)}) collective-permute-start(f32[32,128]{1,0:T(8,128)S(1)} %add.12), channel_id=1, source_target_pairs={{0,16},{16,0},{32,48},{48,32},{64,80},{80,64},{96,112},{112,96},{1... | collective-permute-start | bytes 49160 | tf_op jit(solution)/shard_map/ppermute | solution.py:225

commit v9 on v6

--- a/solution.py
+++ b/solution.py
@@ -21,14 +21,11 @@
     return [(g * size, tile // 2 + g * size, size) for g in range(GROUPS)]
 
 
-def pack_kernel(
-    emb_hbm, cot_hbm, comp_hbm, pairs_hbm, counts_ref, out_hbm, emb, comp, pairs, turned, message, sems
-):
+def pack_kernel(emb_hbm, cot_hbm, comp_hbm, pairs_hbm, counts_ref, out_ref, emb, comp, pairs, turned, sems):
     tile, width, samples = emb.shape
-    fields = out_hbm.shape[0]
+    fields = out_ref.shape[0]
     each = samples // fields
-    half = tile // 2
-    packed = tile + half
+    packed = tile + tile // 2
     f32, bf16 = jnp.float32, jnp.bfloat16
     groups = row_groups(tile)
     loads = [
@@ -38,27 +35,15 @@
         for g, (low, high, size) in enumerate(groups)
         for h, start in enumerate((low, high))
     ]
-    small = [
+    others = [
         pltpu.make_async_copy(comp_hbm, comp, sems.at[2 * GROUPS]),
         pltpu.make_async_copy(pairs_hbm, pairs, sems.at[2 * GROUPS + 1]),
+        pltpu.make_async_copy(
+            cot_hbm, out_ref.at[:, pl.ds(each * packed, each * tile)], sems.at[2 * GROUPS + 2]
+        ),
     ]
-    direct = pltpu.make_async_copy(
-        cot_hbm, message.at[:, pl.ds(each * packed, each * tile)], sems.at[2 * GROUPS + 2]
-    )
-    for copy in loads[:2] + small + loads[2:] + [direct]:
+    for copy in loads + others:
         copy.start()
-    for copy in small:
-        copy.wait()
-    slots = pairs.shape[1]
-    number = lax.broadcasted_iota(jnp.int32, (LANES, slots), 0)
-    live = lax.broadcasted_iota(jnp.int32, (LANES, slots), 1) < counts_ref[0]
-    first = jnp.where((pairs[0:1] == number) & live, 1.0, 0.0).astype(bf16)
-    second = jnp.where(pairs[1:2] == number, 1.0, 0.0).astype(bf16)
-    table = lax.dot_general(first, second, TURN, preferred_element_type=f32)
-    base = each * (packed + tile)
-    for p in range(fields):
-        message[p, base : base + tile] = comp[...]
-        message[p, base + tile : base + tile + TABLE] = table[:TABLE].astype(bf16)
     for g, (low, high, size) in enumerate(groups):
         loads[2 * g].wait()
         loads[2 * g + 1].wait()
@@ -73,25 +58,26 @@
             ]
             for place, block in blocks:
                 turned[place * samples : (place + 1) * samples] = block.T.astype(f32)
-    direct.wait()
-    stores = []
-    for g in range(GROUPS):
-        some = fields // GROUPS
-
-        def peer(p, carry):
-            for j in range(each):
-                both = turned[pl.ds(p * each + j, packed, stride=samples), :]
-                message[p, j * packed : (j + 1) * packed] = both.astype(bf16)
-            return carry
-
-        lax.fori_loop(g * some, (g + 1) * some, peer, 0)
-        here = pl.ds(g * some, some)
-        stores.append(
-            pltpu.make_async_copy(message.at[here], out_hbm.at[here], sems.at[2 * GROUPS + 3 + g])
-        )
-        stores[-1].start()
-    for copy in stores:
+
+    def peer(p, carry):
+        for j in range(each):
+            both = turned[pl.ds(p * each + j, packed, stride=samples), :]
+            out_ref[p, j * packed : (j + 1) * packed] = both.astype(bf16)
+        return carry
+
+    lax.fori_loop(0, fields, peer, 0)
+    for copy in others:
         copy.wait()
+    slots = pairs.shape[1]
+    number = lax.broadcasted_iota(jnp.int32, (LANES, slots), 0)
+    live = lax.broadcasted_iota(jnp.int32, (LANES, slots), 1) < counts_ref[0]
+    first = jnp.where((pairs[0:1] == number) & live, 1.0, 0.0).astype(bf16)
+    second = jnp.where(pairs[1:2] == number, 1.0, 0.0).astype(bf16)
+    table = lax.dot_general(first, second, TURN, preferred_element_type=f32)
+    base = each * (packed + tile)
+    for p in range(fields):
+        out_ref[p, base : base + tile] = comp[...]
+        out_ref[p, base + tile : base + tile + TABLE] = table[:TABLE].astype(bf16)
 
 
 def pair_mask(x_ref, base, scale, mask, tile):
@@ -237,6 +223,9 @@
     turned = pltpu.VMEM((packed * samp_rows, LANES), f32)
     by_row = pltpu.VMEM((tile, width, samp_rows), bf16)
 
+    def stay(array):
+        return pltpu.with_memory_space_constraint(array, pltpu.HBM)
+
     def cost(flops, moved):
         return pl.CostEstimate(flops=flops, bytes_accessed=moved, transcendentals=0)
 
@@ -244,22 +233,21 @@
         pack_kernel,
         out_shape=jax.ShapeDtypeStruct((fields, each * rows + tile + TABLE, LANES), bf16),
         in_specs=[hbm, hbm, hbm, hbm, smem],
-        out_specs=hbm,
+        out_specs=vmem,
         scratch_shapes=[
             by_row,
             pltpu.VMEM(comp.shape, bf16),
             pltpu.VMEM(pairs.shape[::-1], jnp.int32),
             turned,
-            pltpu.VMEM((fields, each * rows + tile + TABLE, LANES), bf16),
-            pltpu.SemaphoreType.DMA((3 * GROUPS + 3,)),
+            pltpu.SemaphoreType.DMA((2 * GROUPS + 3,)),
         ],
-        compiler_params=pltpu.CompilerParams(vmem_limit_bytes=56 * MIB),
+        compiler_params=pltpu.CompilerParams(vmem_limit_bytes=24 * MIB),
         cost_estimate=cost(10**9, 8 * 10**6),
     )(
-        jnp.transpose(emb, (1, 2, 0)),
-        cot.reshape(fields, each * tile, LANES),
-        comp,
-        pairs.T,
+        stay(jnp.transpose(emb, (1, 2, 0))),
+        stay(cot.reshape(fields, each * tile, LANES)),
+        stay(comp),
+        stay(pairs.T),
         counts,
     )
     x = lax.all_to_all(x, "field", 0, 0)

time: 105 us -> 104 us (level)
  no operation moved by 1% of the time
where the time goes in v9:
time: 104 us; the launch traced here: 103 us
  blocking collectives  79.2 us (76%)
  Pallas kernels  12 us (12%)
  starting transfers between devices  7.07 us (7%)
  waiting for transfers between devices  3.1 us (3%)
  between operations  1.32 us (1%)
    all_to_all x1, blocking collectives, per_device(): x = lax.all_to_all(x, 'field', 0, 0)  41.8 us
    all_to_all x1, blocking collectives, per_device(): y = lax.all_to_all(y, 'field', 0, 0)  37.4 us
    ppermute x4, starting transfers between devices, partner(): return lax.ppermute(value, 'dp', [(i, i ^ flip) for i in range(size)])  7.07 us
    pallas_call x1, Pallas kernels, per_device(): pl.pallas_call(functools.partial(block_kernel, width ** (-0.5), tile, wid...  5.04 us
    pallas_call x1, Pallas kernels, per_device(): pl.pallas_call(pack_kernel, out_shape=jax.ShapeDtypeStruct((fields, each...  3.86 us
    ppermute x4, waiting for transfers between devices, partner(): return lax.ppermute(value, 'dp', [(i, i ^ flip) for i in range(size)])  3.1 us
  transfers between devices with their start and end apart: 4, of which 2 were waited for; matrix products, arithmetic and copies ran while one was open for 0% of the time, Pallas kernels for 3%

profile of v9, /device:TPU:0, one launch (start us, length us, event | category | flops | bytes accessed | tf_op | source)
XLA Modules:
  0.0 103.4 jit_solution(7918758504966166559)
XLA Ops:
  1.3 3.9 %shard_map.76 = bf16[16,688,128]{2,1,0:T(8,128)(2,1)S(1)} custom-call(bf16[32,192,128]{2,1,0:T(8,128)(2,1)} %bitcast.5, bf16[16,256,128]{2,1,0:T(8,128)(2,1)} %bitcast.7, bf16[32,128]{1,0:T(8,128)(2,1)} %comp_hbm.1, s32[2,72]{1,0:T(2,128)} %bitcast.8, s32[1]{0:T(128)S(6)} %copy.10.counts_ref), custom_call_target="tpu_custom_call" | custom-call | flops 1000000000 | bytes 8000000 | tf_op jit(solution)/shard_map/pallas_call | solution.py:232
  5.1 41.8 %all_to_all.10.x_ref = bf16[16,688,128]{2,1,0:T(8,128)(2,1)S(1)} all-to-all(bf16[16,688,128]{2,1,0:T(8,128)(2,1)S(1)} %shard_map.76), channel_id=1, replica_groups=mesh['dp'=8,'field'=16] {'field'}, dimensions={0} | all-to-all | bytes 5636096 | tf_op jit(solution)/shard_map/all_to_all | solution.py:253
  46.9 5.0 %shard_map.77 = bf16[16,672,128]{2,1,0:T(8,128)(2,1)S(1)} custom-call(bf16[16,688,128]{2,1,0:T(8,128)(2,1)S(1)} %all_to_all.10.x_ref), custom_call_target="tpu_custom_call" | custom-call | flops 4000000000 | bytes 6000000 | tf_op jit(solution)/shard_map/pallas_call | solution.py:254
  52.0 37.4 %all_to_all.11.y_ref = bf16[16,672,128]{2,1,0:T(8,128)(2,1)S(1)} all-to-all(bf16[16,672,128]{2,1,0:T(8,128)(2,1)S(1)} %shard_map.77), channel_id=1, replica_groups=mesh['dp'=8,'field'=16] {'field'}, dimensions={0} | all-to-all | bytes 5505024 | tf_op jit(solution)/shard_map/all_to_all | solution.py:269
  89.4 3.0 %collective-permute-start = (f32[32,128]{1,0:T(8,128)S(1)}, f32[32,128]{1,0:T(8,128)S(1)}, u32[]{:S(2)}, u32[]{:S(2)}) collective-permute-start(f32[32,128]{1,0:T(8,128)S(1)} %convert_reduce_fusion), channel_id=1, source_target_pairs={{0,64},{16,80},{32,96},{48,112},{64,0},{80,16},{96,32},{112,48},{1... | collective-permute-start | bytes 49160 | tf_op jit(solution)/shard_map/ppermute | solution.py:203
  92.4 1.7 %shard_map.78 = (bf16[16,256,128]{2,1,0:T(8,128)(2,1)}, bf16[32,192,128]{2,1,0:T(8,128)(2,1)}, f32[6144,128]{1,0:T(8,128)S(1)}) custom-call(bf16[16,672,128]{2,1,0:T(8,128)(2,1)S(1)} %all_to_all.11.y_ref), custom_call_target="tpu_custom_call" | custom-call | flops 1000000000 | bytes 8000000 | tf_op jit(solution)/shard_map/pallas_call | solution.py:274
  94.1 0.7 collective-permute-done
  94.7 2.8 %collective-permute-start.3 = (f32[32,128]{1,0:T(8,128)S(1)}, f32[32,128]{1,0:T(8,128)S(1)}, u32[]{:S(2)}, u32[]{:S(2)}) collective-permute-start(f32[32,128]{1,0:T(8,128)S(1)} %add.12), channel_id=1, source_target_pairs={{0,48},{16,32},{32,16},{48,0},{64,112},{80,96},{96,80},{112,64},{1... | collective-permute-start | bytes 49160 | tf_op jit(solution)/shard_map/ppermute | solution.py:203
  97.5 0.8 collective-permute-start.2
  98.3 0.5 collective-permute-start.1
  98.8 1.5 %shard_map.79 = bf16[32,192,128]{2,1,0:T(8,128)(2,1)} custom-call(f32[6144,128]{1,0:T(8,128)S(1)} %get-tuple-element.7.sorted_rows, bf16[32,192,128]{2,1,0:T(8,128)(2,1)} %get-tuple-element.8._), custom_call_target="tpu_custom_call", output_to_operand_aliasing={{}: (1, {})} | custom-call | flops 1000000000 | bytes 8000000 | tf_op jit(solution)/shard_map/pallas_call | solution.py:287
  100.3 0.0 collective-permute-done.3
  100.3 2.4 %collective-permute-done.2 = f32[32,128]{1,0:T(8,128)S(1)} collective-permute-done((f32[32,128]{1,0:T(8,128)S(1)}, f32[32,128]{1,0:T(8,128)S(1)}, u32[]{:S(2)}, u32[]{:S(2)}) %collective-permute-start.2) | collective-permute-done | bytes 16416 | tf_op jit(solution)/shard_map/ppermute | solution.py:203
  102.8 0.0 collective-permute-done.1
  102.8 0.6 add_multiply_fusion
  (2 shorter events, 0.0 us)
Async XLA Ops:
  89.4 5.3 %collective-permute-start = (f32[32,128]{1,0:T(8,128)S(1)}, f32[32,128]{1,0:T(8,128)S(1)}, u32[]{:S(2)}, u32[]{:S(2)}) collective-permute-start(f32[32,128]{1,0:T(8,128)S(1)} %convert_reduce_fusion), channel_id=1, source_target_pairs={{0,64},{16,80},{32,96},{48,112},{64,0},{80,16},{96,32},{112,48},{1... | collective-permute-start | bytes 49160 | tf_op jit(solution)/shard_map/ppermute | solution.py:203
  94.7 5.6 %collective-permute-start.3 = (f32[32,128]{1,0:T(8,128)S(1)}, f32[32,128]{1,0:T(8,128)S(1)}, u32[]{:S(2)}, u32[]{:S(2)}) collective-permute-start(f32[32,128]{1,0:T(8,128)S(1)} %add.12), channel_id=1, source_target_pairs={{0,48},{16,32},{32,16},{48,0},{64,112},{80,96},{96,80},{112,64},{1... | collective-permute-start | bytes 49160 | tf_op jit(solution)/shard_map/ppermute | solution.py:203
  97.5 5.2 %collective-permute-start.2 = (f32[32,128]{1,0:T(8,128)S(1)}, f32[32,128]{1,0:T(8,128)S(1)}, u32[]{:S(2)}, u32[]{:S(2)}) collective-permute-start(f32[32,128]{1,0:T(8,128)S(1)} %add.12), channel_id=1, source_target_pairs={{0,32},{16,48},{32,0},{48,16},{64,96},{80,112},{96,64},{112,80},{1... | collective-permute-start | bytes 49160 | tf_op jit(solution)/shard_map/ppermute | solution.py:203
  98.3 4.4 %collective-permute-start.1 = (f32[32,128]{1,0:T(8,128)S(1)}, f32[32,128]{1,0:T(8,128)S(1)}, u32[]{:S(2)}, u32[]{:S(2)}) collective-permute-start(f32[32,128]{1,0:T(8,128)S(1)} %add.12), channel_id=1, source_target_pairs={{0,16},{16,0},{32,48},{48,32},{64,80},{80,64},{96,112},{112,96},{1... | collective-permute-start | bytes 49160 | tf_op jit(solution)/shard_map/ppermute | solution.py:203

commit v10 on v9

--- a/solution.py
+++ b/solution.py
@@ -8,7 +8,7 @@
 from jax.sharding import PartitionSpec as P
 
 LANES = 128
-GROUPS = 4
+GROUPS = 8
 AT_ONCE = 8
 ALONG_X = 4
 TABLE = 16
@@ -205,7 +205,9 @@
     if size != 2 * ALONG_X:
         return lax.psum(own, "dp")
     total = own + partner(own, ALONG_X)
-    return (total + partner(total, 1)) + (partner(total, 2) + partner(total, 3))
+    first, third = partner(total, 1), partner(total, 3)
+    second = partner(total, 2)
+    return (total + second) + (third + first)
 
 
 def per_device(emb, comp, cot, pairs, counts):

time: 104 us -> 105 us (level)
  transfers between devices with their start and end apart: 4 -> 4, of which waited for: 2 -> 3; matrix products, arithmetic and copies ran while one was open for 0% -> 0% of each run, Pallas kernels for 3% -> 3%
where the time goes in v10:
time: 105 us; the launch traced here: 104 us
  blocking collectives  79.2 us (75%)
  Pallas kernels  12.2 us (12%)
  starting transfers between devices  7.2 us (7%)
  waiting for transfers between devices  3.78 us (4%)
  between operations  1.32 us (1%)
    all_to_all x1, blocking collectives, per_device(): x = lax.all_to_all(x, 'field', 0, 0)  41.8 us
    all_to_all x1, blocking collectives, per_device(): y = lax.all_to_all(y, 'field', 0, 0)  37.4 us
    ppermute x4, starting transfers between devices, partner(): return lax.ppermute(value, 'dp', [(i, i ^ flip) for i in range(size)])  7.2 us
    pallas_call x1, Pallas kernels, per_device(): pl.pallas_call(functools.partial(block_kernel, width ** (-0.5), tile, wid...  5.04 us
    pallas_call x1, Pallas kernels, per_device(): pl.pallas_call(pack_kernel, out_shape=jax.ShapeDtypeStruct((fields, each...  4.04 us
    ppermute x4, waiting for transfers between devices, partner(): return lax.ppermute(value, 'dp', [(i, i ^ flip) for i in range(size)])  3.78 us
  transfers between devices with their start and end apart: 4, of which 3 were waited for; matrix products, arithmetic and copies ran while one was open for 0% of the time, Pallas kernels for 3%

profile of v10, /device:TPU:0, one launch (start us, length us, event | category | flops | bytes accessed | tf_op | source)
XLA Modules:
  0.0 104.4 jit_solution(10956689789115933101)
XLA Ops:
  1.3 4.0 %shard_map.76 = bf16[16,688,128]{2,1,0:T(8,128)(2,1)S(1)} custom-call(bf16[32,192,128]{2,1,0:T(8,128)(2,1)} %bitcast.5, bf16[16,256,128]{2,1,0:T(8,128)(2,1)} %bitcast.7, bf16[32,128]{1,0:T(8,128)(2,1)} %comp_hbm.1, s32[2,72]{1,0:T(2,128)} %bitcast.8, s32[1]{0:T(128)S(6)} %copy.10.counts_ref), custom_call_target="tpu_custom_call" | custom-call | flops 1000000000 | bytes 8000000 | tf_op jit(solution)/shard_map/pallas_call | solution.py:234
  5.3 41.8 %all_to_all.10.x_ref = bf16[16,688,128]{2,1,0:T(8,128)(2,1)S(1)} all-to-all(bf16[16,688,128]{2,1,0:T(8,128)(2,1)S(1)} %shard_map.76), channel_id=1, replica_groups=mesh['dp'=8,'field'=16] {'field'}, dimensions={0} | all-to-all | bytes 5636096 | tf_op jit(solution)/shard_map/all_to_all | solution.py:255
  47.1 5.0 %shard_map.77 = bf16[16,672,128]{2,1,0:T(8,128)(2,1)S(1)} custom-call(bf16[16,688,128]{2,1,0:T(8,128)(2,1)S(1)} %all_to_all.10.x_ref), custom_call_target="tpu_custom_call" | custom-call | flops 4000000000 | bytes 6000000 | tf_op jit(solution)/shard_map/pallas_call | solution.py:256
  52.1 37.4 %all_to_all.11.y_ref = bf16[16,672,128]{2,1,0:T(8,128)(2,1)S(1)} all-to-all(bf16[16,672,128]{2,1,0:T(8,128)(2,1)S(1)} %shard_map.77), channel_id=1, replica_groups=mesh['dp'=8,'field'=16] {'field'}, dimensions={0} | all-to-all | bytes 5505024 | tf_op jit(solution)/shard_map/all_to_all | solution.py:271
  89.6 3.0 %collective-permute-start = (f32[32,128]{1,0:T(8,128)S(1)}, f32[32,128]{1,0:T(8,128)S(1)}, u32[]{:S(2)}, u32[]{:S(2)}) collective-permute-start(f32[32,128]{1,0:T(8,128)S(1)} %convert_reduce_fusion), channel_id=1, source_target_pairs={{0,64},{16,80},{32,96},{48,112},{64,0},{80,16},{96,32},{112,48},{1... | collective-permute-start | bytes 49160 | tf_op jit(solution)/shard_map/ppermute | solution.py:203
  92.6 1.7 %shard_map.78 = (bf16[16,256,128]{2,1,0:T(8,128)(2,1)}, bf16[32,192,128]{2,1,0:T(8,128)(2,1)}, f32[6144,128]{1,0:T(8,128)S(1)}) custom-call(bf16[16,672,128]{2,1,0:T(8,128)(2,1)S(1)} %all_to_all.11.y_ref), custom_call_target="tpu_custom_call" | custom-call | flops 1000000000 | bytes 8000000 | tf_op jit(solution)/shard_map/pallas_call | solution.py:276
  94.3 0.6 collective-permute-done
  94.9 1.5 %collective-permute-start.3 = (f32[32,128]{1,0:T(8,128)S(1)}, f32[32,128]{1,0:T(8,128)S(1)}, u32[]{:S(2)}, u32[]{:S(2)}) collective-permute-start(f32[32,128]{1,0:T(8,128)S(1)} %add.12), channel_id=1, source_target_pairs={{0,16},{16,0},{32,48},{48,32},{64,80},{80,64},{96,112},{112,96},{1... | collective-permute-start | bytes 49160 | tf_op jit(solution)/shard_map/ppermute | solution.py:203
  96.4 2.1 %collective-permute-start.2 = (f32[32,128]{1,0:T(8,128)S(1)}, f32[32,128]{1,0:T(8,128)S(1)}, u32[]{:S(2)}, u32[]{:S(2)}) collective-permute-start(f32[32,128]{1,0:T(8,128)S(1)} %add.12), channel_id=1, source_target_pairs={{0,48},{16,32},{32,16},{48,0},{64,112},{80,96},{96,80},{112,64},{1... | collective-permute-start | bytes 49160 | tf_op jit(solution)/shard_map/ppermute | solution.py:203
  98.5 0.6 collective-permute-start.1
  99.2 1.4 %shard_map.79 = bf16[32,192,128]{2,1,0:T(8,128)(2,1)} custom-call(f32[6144,128]{1,0:T(8,128)S(1)} %get-tuple-element.7.sorted_rows, bf16[32,192,128]{2,1,0:T(8,128)(2,1)} %get-tuple-element.8._), custom_call_target="tpu_custom_call", output_to_operand_aliasing={{}: (1, {})} | custom-call | flops 1000000000 | bytes 8000000 | tf_op jit(solution)/shard_map/pallas_call | solution.py:289
  100.6 0.0 collective-permute-done.3
  100.6 0.8 collective-permute-done.2
  101.4 2.3 %collective-permute-done.1 = f32[32,128]{1,0:T(8,128)S(1)} collective-permute-done((f32[32,128]{1,0:T(8,128)S(1)}, f32[32,128]{1,0:T(8,128)S(1)}, u32[]{:S(2)}, u32[]{:S(2)}) %collective-permute-start.1) | collective-permute-done | bytes 16416 | tf_op jit(solution)/shard_map/ppermute | solution.py:203
  103.8 0.6 add_multiply_fusion
  (2 shorter events, 0.0 us)
Async XLA Ops:
  89.6 5.3 %collective-permute-start = (f32[32,128]{1,0:T(8,128)S(1)}, f32[32,128]{1,0:T(8,128)S(1)}, u32[]{:S(2)}, u32[]{:S(2)}) collective-permute-start(f32[32,128]{1,0:T(8,128)S(1)} %convert_reduce_fusion), channel_id=1, source_target_pairs={{0,64},{16,80},{32,96},{48,112},{64,0},{80,16},{96,32},{112,48},{1... | collective-permute-start | bytes 49160 | tf_op jit(solution)/shard_map/ppermute | solution.py:203
  94.9 5.7 %collective-permute-start.3 = (f32[32,128]{1,0:T(8,128)S(1)}, f32[32,128]{1,0:T(8,128)S(1)}, u32[]{:S(2)}, u32[]{:S(2)}) collective-permute-start(f32[32,128]{1,0:T(8,128)S(1)} %add.12), channel_id=1, source_target_pairs={{0,16},{16,0},{32,48},{48,32},{64,80},{80,64},{96,112},{112,96},{1... | collective-permute-start | bytes 49160 | tf_op jit(solution)/shard_map/ppermute | solution.py:203
  96.4 5.0 %collective-permute-start.2 = (f32[32,128]{1,0:T(8,128)S(1)}, f32[32,128]{1,0:T(8,128)S(1)}, u32[]{:S(2)}, u32[]{:S(2)}) collective-permute-start(f32[32,128]{1,0:T(8,128)S(1)} %add.12), channel_id=1, source_target_pairs={{0,48},{16,32},{32,16},{48,0},{64,112},{80,96},{96,80},{112,64},{1... | collective-permute-start | bytes 49160 | tf_op jit(solution)/shard_map/ppermute | solution.py:203
  98.5 5.2 %collective-permute-start.1 = (f32[32,128]{1,0:T(8,128)S(1)}, f32[32,128]{1,0:T(8,128)S(1)}, u32[]{:S(2)}, u32[]{:S(2)}) collective-permute-start(f32[32,128]{1,0:T(8,128)S(1)} %add.12), channel_id=1, source_target_pairs={{0,32},{16,48},{32,0},{48,16},{64,96},{80,112},{96,64},{112,80},{1... | collective-permute-start | bytes 49160 | tf_op jit(solution)/shard_map/ppermute | solution.py:203

commit v11 on v9

--- a/solution.py
+++ b/solution.py
@@ -10,6 +10,7 @@
 LANES = 128
 GROUPS = 4
 AT_ONCE = 8
+SETS = 4
 ALONG_X = 4
 TABLE = 16
 TURN = (((1,), (1,)), ((), ()))
@@ -42,8 +43,20 @@
             cot_hbm, out_ref.at[:, pl.ds(each * packed, each * tile)], sems.at[2 * GROUPS + 2]
         ),
     ]
-    for copy in loads + others:
+    for copy in others[:2] + loads + others[2:]:
         copy.start()
+    for copy in others[:2]:
+        copy.wait()
+    slots = pairs.shape[1]
+    number = lax.broadcasted_iota(jnp.int32, (LANES, slots), 0)
+    live = lax.broadcasted_iota(jnp.int32, (LANES, slots), 1) < counts_ref[0]
+    first = jnp.where((pairs[0:1] == number) & live, 1.0, 0.0).astype(bf16)
+    second = jnp.where(pairs[1:2] == number, 1.0, 0.0).astype(bf16)
+    table = lax.dot_general(first, second, TURN, preferred_element_type=f32)
+    base = each * (packed + tile)
+    for p in range(fields):
+        out_ref[p, base : base + tile] = comp[...]
+        out_ref[p, base + tile : base + tile + TABLE] = table[:TABLE].astype(bf16)
     for g, (low, high, size) in enumerate(groups):
         loads[2 * g].wait()
         loads[2 * g + 1].wait()
@@ -66,18 +79,7 @@
         return carry
 
     lax.fori_loop(0, fields, peer, 0)
-    for copy in others:
-        copy.wait()
-    slots = pairs.shape[1]
-    number = lax.broadcasted_iota(jnp.int32, (LANES, slots), 0)
-    live = lax.broadcasted_iota(jnp.int32, (LANES, slots), 1) < counts_ref[0]
-    first = jnp.where((pairs[0:1] == number) & live, 1.0, 0.0).astype(bf16)
-    second = jnp.where(pairs[1:2] == number, 1.0, 0.0).astype(bf16)
-    table = lax.dot_general(first, second, TURN, preferred_element_type=f32)
-    base = each * (packed + tile)
-    for p in range(fields):
-        out_ref[p, base : base + tile] = comp[...]
-        out_ref[p, base + tile : base + tile + TABLE] = table[:TABLE].astype(bf16)
+    others[2].wait()
 
 
 def pair_mask(x_ref, base, scale, mask, tile):
@@ -142,11 +144,11 @@
         return both[:, LANES:]
 
     def some(i, carry):
-        terms = [sample(i * len(sets) + u, *refs) for u, refs in enumerate(sets)]
+        terms = [sample(i * AT_ONCE + u, *sets[u % SETS]) for u in range(AT_ONCE)]
         grad[...] += sum(terms[1:], terms[0])
         return carry
 
-    lax.fori_loop(0, each // len(sets), some, 0)
+    lax.fori_loop(0, each // AT_ONCE, some, 0)
     y_ref[:, base:] = grad[...].astype(bf16).reshape(fields, tile, LANES)
 
 
@@ -262,7 +264,7 @@
             pltpu.VMEM((embeds, 2 * LANES), bf16),
             pltpu.VMEM((embeds, 2 * LANES), bf16),
         ]
-        * AT_ONCE,
+        * SETS,
         compiler_params=params,
         cost_estimate=cost(4 * 10**9, 6 * 10**6),
     )(x)

time: 104 us -> 104 us (level)
  no operation moved by 1% of the time
where the time goes in v11:
time: 104 us; the launch traced here: 103 us
  blocking collectives  79.2 us (76%)
  Pallas kernels  12 us (12%)
  starting transfers between devices  7.07 us (7%)
  waiting for transfers between devices  3.1 us (3%)
  between operations  1.32 us (1%)
    all_to_all x1, blocking collectives, per_device(): x = lax.all_to_all(x, 'field', 0, 0)  41.8 us
    all_to_all x1, blocking collectives, per_device(): y = lax.all_to_all(y, 'field', 0, 0)  37.4 us
    ppermute x4, starting transfers between devices, partner(): return lax.ppermute(value, 'dp', [(i, i ^ flip) for i in range(size)])  7.07 us
    pallas_call x1, Pallas kernels, per_device(): pl.pallas_call(functools.partial(block_kernel, width ** (-0.5), tile, wid...  5.15 us
    pallas_call x1, Pallas kernels, per_device(): pl.pallas_call(pack_kernel, out_shape=jax.ShapeDtypeStruct((fields, each...  3.72 us
    ppermute x4, waiting for transfers between devices, partner(): return lax.ppermute(value, 'dp', [(i, i ^ flip) for i in range(size)])  3.1 us
  transfers between devices with their start and end apart: 4, of which 2 were waited for; matrix products, arithmetic and copies ran while one was open for 0% of the time, Pallas kernels for 3%

profile of v11, /device:TPU:0, one launch (start us, length us, event | category | flops | bytes accessed | tf_op | source)
XLA Modules:
  0.0 103.3 jit_solution(8607092418114711812)
XLA Ops:
  1.3 3.7 %shard_map.76 = bf16[16,688,128]{2,1,0:T(8,128)(2,1)S(1)} custom-call(bf16[32,192,128]{2,1,0:T(8,128)(2,1)} %bitcast.5, bf16[16,256,128]{2,1,0:T(8,128)(2,1)} %bitcast.7, bf16[32,128]{1,0:T(8,128)(2,1)} %comp_hbm.1, s32[2,72]{1,0:T(2,128)} %bitcast.8, s32[1]{0:T(128)S(6)} %copy.10.counts_ref), custom_call_target="tpu_custom_call" | custom-call | flops 1000000000 | bytes 8000000 | tf_op jit(solution)/shard_map/pallas_call | solution.py:234
  5.0 41.8 %all_to_all.10.x_ref = bf16[16,688,128]{2,1,0:T(8,128)(2,1)S(1)} all-to-all(bf16[16,688,128]{2,1,0:T(8,128)(2,1)S(1)} %shard_map.76), channel_id=1, replica_groups=mesh['dp'=8,'field'=16] {'field'}, dimensions={0} | all-to-all | bytes 5636096 | tf_op jit(solution)/shard_map/all_to_all | solution.py:255
  46.8 5.2 %shard_map.77 = bf16[16,672,128]{2,1,0:T(8,128)(2,1)S(1)} custom-call(bf16[16,688,128]{2,1,0:T(8,128)(2,1)S(1)} %all_to_all.10.x_ref), custom_call_target="tpu_custom_call" | custom-call | flops 4000000000 | bytes 6000000 | tf_op jit(solution)/shard_map/pallas_call | solution.py:256
  51.9 37.4 %all_to_all.11.y_ref = bf16[16,672,128]{2,1,0:T(8,128)(2,1)S(1)} all-to-all(bf16[16,672,128]{2,1,0:T(8,128)(2,1)S(1)} %shard_map.77), channel_id=1, replica_groups=mesh['dp'=8,'field'=16] {'field'}, dimensions={0} | all-to-all | bytes 5505024 | tf_op jit(solution)/shard_map/all_to_all | solution.py:271
  89.4 3.0 %collective-permute-start = (f32[32,128]{1,0:T(8,128)S(1)}, f32[32,128]{1,0:T(8,128)S(1)}, u32[]{:S(2)}, u32[]{:S(2)}) collective-permute-start(f32[32,128]{1,0:T(8,128)S(1)} %convert_reduce_fusion), channel_id=1, source_target_pairs={{0,64},{16,80},{32,96},{48,112},{64,0},{80,16},{96,32},{112,48},{1... | collective-permute-start | bytes 49160 | tf_op jit(solution)/shard_map/ppermute | solution.py:205
  92.4 1.7 %shard_map.78 = (bf16[16,256,128]{2,1,0:T(8,128)(2,1)}, bf16[32,192,128]{2,1,0:T(8,128)(2,1)}, f32[6144,128]{1,0:T(8,128)S(1)}) custom-call(bf16[16,672,128]{2,1,0:T(8,128)(2,1)S(1)} %all_to_all.11.y_ref), custom_call_target="tpu_custom_call" | custom-call | flops 1000000000 | bytes 8000000 | tf_op jit(solution)/shard_map/pallas_call | solution.py:276
  94.0 0.7 collective-permute-done
  94.7 2.8 %collective-permute-start.3 = (f32[32,128]{1,0:T(8,128)S(1)}, f32[32,128]{1,0:T(8,128)S(1)}, u32[]{:S(2)}, u32[]{:S(2)}) collective-permute-start(f32[32,128]{1,0:T(8,128)S(1)} %add.12), channel_id=1, source_target_pairs={{0,48},{16,32},{32,16},{48,0},{64,112},{80,96},{96,80},{112,64},{1... | collective-permute-start | bytes 49160 | tf_op jit(solution)/shard_map/ppermute | solution.py:205
  97.5 0.8 collective-permute-start.2
  98.3 0.5 collective-permute-start.1
  98.8 1.5 %shard_map.79 = bf16[32,192,128]{2,1,0:T(8,128)(2,1)} custom-call(f32[6144,128]{1,0:T(8,128)S(1)} %get-tuple-element.7.sorted_rows, bf16[32,192,128]{2,1,0:T(8,128)(2,1)} %get-tuple-element.8._), custom_call_target="tpu_custom_call", output_to_operand_aliasing={{}: (1, {})} | custom-call | flops 1000000000 | bytes 8000000 | tf_op jit(solution)/shard_map/pallas_call | solution.py:289
  100.3 0.0 collective-permute-done.3
  100.3 2.4 %collective-permute-done.2 = f32[32,128]{1,0:T(8,128)S(1)} collective-permute-done((f32[32,128]{1,0:T(8,128)S(1)}, f32[32,128]{1,0:T(8,128)S(1)}, u32[]{:S(2)}, u32[]{:S(2)}) %collective-permute-start.2) | collective-permute-done | bytes 16416 | tf_op jit(solution)/shard_map/ppermute | solution.py:205
  102.7 0.0 collective-permute-done.1
  102.7 0.6 add_multiply_fusion
  (2 shorter events, 0.0 us)
Async XLA Ops:
  89.4 5.3 %collective-permute-start = (f32[32,128]{1,0:T(8,128)S(1)}, f32[32,128]{1,0:T(8,128)S(1)}, u32[]{:S(2)}, u32[]{:S(2)}) collective-permute-start(f32[32,128]{1,0:T(8,128)S(1)} %convert_reduce_fusion), channel_id=1, source_target_pairs={{0,64},{16,80},{32,96},{48,112},{64,0},{80,16},{96,32},{112,48},{1... | collective-permute-start | bytes 49160 | tf_op jit(solution)/shard_map/ppermute | solution.py:205
  94.7 5.6 %collective-permute-start.3 = (f32[32,128]{1,0:T(8,128)S(1)}, f32[32,128]{1,0:T(8,128)S(1)}, u32[]{:S(2)}, u32[]{:S(2)}) collective-permute-start(f32[32,128]{1,0:T(8,128)S(1)} %add.12), channel_id=1, source_target_pairs={{0,48},{16,32},{32,16},{48,0},{64,112},{80,96},{96,80},{112,64},{1... | collective-permute-start | bytes 49160 | tf_op jit(solution)/shard_map/ppermute | solution.py:205
  97.5 5.2 %collective-permute-start.2 = (f32[32,128]{1,0:T(8,128)S(1)}, f32[32,128]{1,0:T(8,128)S(1)}, u32[]{:S(2)}, u32[]{:S(2)}) collective-permute-start(f32[32,128]{1,0:T(8,128)S(1)} %add.12), channel_id=1, source_target_pairs={{0,32},{16,48},{32,0},{48,16},{64,96},{80,112},{96,64},{112,80},{1... | collective-permute-start | bytes 49160 | tf_op jit(solution)/shard_map/ppermute | solution.py:205
  98.3 4.5 %collective-permute-start.1 = (f32[32,128]{1,0:T(8,128)S(1)}, f32[32,128]{1,0:T(8,128)S(1)}, u32[]{:S(2)}, u32[]{:S(2)}) collective-permute-start(f32[32,128]{1,0:T(8,128)S(1)} %add.12), channel_id=1, source_target_pairs={{0,16},{16,0},{32,48},{48,32},{64,80},{80,64},{96,112},{112,96},{1... | collective-permute-start | bytes 49160 | tf_op jit(solution)/shard_map/ppermute | solution.py:205

commit v12 on v11

--- a/solution.py
+++ b/solution.py
@@ -9,7 +9,7 @@
 
 LANES = 128
 GROUPS = 4
-AT_ONCE = 8
+HALVES = 2
 SETS = 4
 ALONG_X = 4
 TABLE = 16
@@ -36,12 +36,17 @@
         for g, (low, high, size) in enumerate(groups)
         for h, start in enumerate((low, high))
     ]
+    length = each // HALVES * tile
     others = [
         pltpu.make_async_copy(comp_hbm, comp, sems.at[2 * GROUPS]),
         pltpu.make_async_copy(pairs_hbm, pairs, sems.at[2 * GROUPS + 1]),
+    ] + [
         pltpu.make_async_copy(
-            cot_hbm, out_ref.at[:, pl.ds(each * packed, each * tile)], sems.at[2 * GROUPS + 2]
-        ),
+            cot_hbm.at[h],
+            out_ref.at[:, pl.ds(each * packed + h * length, length)],
+            sems.at[2 * GROUPS + 2 + h],
+        )
+        for h in range(HALVES)
     ]
     for copy in others[:2] + loads + others[2:]:
         copy.start()
@@ -74,12 +79,15 @@
 
     def peer(p, carry):
         for j in range(each):
-            both = turned[pl.ds(p * each + j, packed, stride=samples), :]
+            half, rank = divmod(j, each // HALVES)
+            number = half * (samples // HALVES) + p * (each // HALVES) + rank
+            both = turned[pl.ds(number, packed, stride=samples), :]
             out_ref[p, j * packed : (j + 1) * packed] = both.astype(bf16)
         return carry
 
     lax.fori_loop(0, fields, peer, 0)
-    others[2].wait()
+    for copy in others[2:]:
+        copy.wait()
 
 
 def pair_mask(x_ref, base, scale, mask, tile):
@@ -100,7 +108,7 @@
         mask[a * tile : (a + 1) * tile] = jnp.broadcast_to(row, (tile, row.shape[1]))
 
 
-def block_kernel(scale, tile, width, x_ref, y_ref, mask, grad, *sets):
+def block_kernel(scale, tile, width, x_ref, *refs):
     fields = x_ref.shape[0]
     half, rest = tile // 2, width - LANES
     packed = tile + half
@@ -109,6 +117,7 @@
     f32, bf16 = jnp.float32, jnp.bfloat16
     each = (x_ref.shape[1] - tile - TABLE) // rows
     base = each * rows
+    y_refs, (mask, grad), sets = refs[:HALVES], refs[HALVES : HALVES + 2], refs[HALVES + 2 :]
     sets = [sets[i : i + 3] for i in range(0, len(sets), 3)]
     pair_mask(x_ref, base + tile, scale, mask, tile)
     weights = x_ref[:, base : base + tile].reshape(embeds, LANES)
@@ -118,8 +127,7 @@
     grad[...] = jnp.zeros_like(grad)
 
     def sample(j, emb, sides, other):
-        start = pl.multiple_of(j * packed, 16)
-        second = pl.multiple_of(each * packed + j * tile, 16)
+        start, second = j * packed, each * packed + j * tile
         emb[:, :LANES] = x_ref[:, pl.ds(start, tile)].reshape(embeds, LANES)
         cot = x_ref[:, pl.ds(second, tile)].reshape(embeds, LANES)
         sides[:, LANES:] = cot
@@ -135,36 +143,57 @@
         sym = (mask[...] * hmat).astype(bf16)
         both = jnp.dot(masked, sides[...], preferred_element_type=f32)
         dfeat = jnp.dot(sym, feats, preferred_element_type=f32).astype(bf16)
+        share = each // HALVES
+        y_ref = y_refs[j // share]
+        start, second = j % share * packed, share * packed + j % share * tile
         y_ref[:, pl.ds(second, tile)] = both[:, :LANES].astype(bf16).reshape(fields, tile, LANES)
         y_ref[:, pl.ds(start, tile)] = dfeat[:, :LANES].reshape(fields, tile, LANES)
         last = dfeat[:, LANES:].reshape(fields, tile, rest)
-        y_ref[:, pl.ds(start + tile, half)] = jnp.concatenate(
-            [last[:, :half], last[:, half:]], axis=2
-        )
+        y_ref[:, pl.ds(start + tile, half)] = jnp.concatenate([last[:, :half], last[:, half:]], axis=2)
         return both[:, LANES:]
 
-    def some(i, carry):
-        terms = [sample(i * AT_ONCE + u, *sets[u % SETS]) for u in range(AT_ONCE)]
-        grad[...] += sum(terms[1:], terms[0])
-        return carry
-
-    lax.fori_loop(0, each // AT_ONCE, some, 0)
-    y_ref[:, base:] = grad[...].astype(bf16).reshape(fields, tile, LANES)
-
-
-def turn(part, sorted_rows, dfeat_hbm, dfeat, sems):
+    for j in range(each):
+        grad[...] += sample(j, *sets[j % SETS])
+    y_refs[0][:, base // HALVES :] = grad[...].astype(bf16).reshape(fields, tile, LANES)
+
+
+def cast_rows(y_ref, rows_ref):
+    fields = y_ref.shape[0]
+    share = rows_ref.shape[0] // fields
+    for p in range(fields):
+        rows_ref[p * share : (p + 1) * share] = y_ref[p, :share].astype(jnp.float32)
+
+
+def early_kernel(y_ref, mixed_hbm, rows_ref, sem):
+    fields, length = mixed_hbm.shape[1:3]
+    share = rows_ref.shape[0] // fields
+    copy = pltpu.make_async_copy(y_ref.at[:, pl.ds(share, length)], mixed_hbm.at[0], sem)
+    copy.start()
+    cast_rows(y_ref, rows_ref)
+    copy.wait()
+
+
+def late_kernel(y_ref, rows_ref, _, mixed_hbm, dfeat_hbm, more, dfeat, sems):
     tile, width, samples = dfeat.shape
     rest = width - LANES
     packed = tile + tile // 2
-    groups = row_groups(tile)
-    share = len(groups) // 2
+    fields, length = mixed_hbm.shape[1:3]
+    share = rows_ref.shape[0] // fields
+    copies = [
+        pltpu.make_async_copy(
+            y_ref.at[:, pl.ds(share, length)], mixed_hbm.at[1], sems.at[2 * GROUPS]
+        )
+    ]
+    copies[0].start()
+    cast_rows(y_ref, more)
 
     def block(row):
-        rows = sorted_rows[pl.ds(row, samples, stride=packed), :]
-        return rows.astype(jnp.bfloat16).T
-
-    copies = []
-    for g, (low, high, size) in enumerate(groups[part * share : (part + 1) * share]):
+        halves = [
+            ref[pl.ds(row, samples // HALVES, stride=packed), :] for ref in (rows_ref, more)
+        ]
+        return jnp.concatenate(halves, axis=0).astype(jnp.bfloat16).T
+
+    for g, (low, high, size) in enumerate(row_groups(tile)):
         for r in range(size):
             for row in (low + r, high + r):
                 dfeat[row, :LANES] = block(row)
@@ -177,24 +206,7 @@
             )
             copy.start()
             copies.append(copy)
-    return copies
-
-
-def unpack_kernel(y_ref, mixed_hbm, dfeat_hbm, sorted_rows, dfeat, sems):
-    fields, length = mixed_hbm.shape[:2]
-    share = sorted_rows.shape[0] // fields
-    mixed = pltpu.make_async_copy(
-        y_ref.at[:, pl.ds(share, length)], mixed_hbm, sems.at[GROUPS]
-    )
-    mixed.start()
-    for p in range(fields):
-        sorted_rows[p * share : (p + 1) * share] = y_ref[p, :share].astype(jnp.float32)
-    for copy in turn(0, sorted_rows, dfeat_hbm, dfeat, sems) + [mixed]:
-        copy.wait()
-
-
-def finish_kernel(sorted_rows, _, dfeat_hbm, dfeat, sems):
-    for copy in turn(1, sorted_rows, dfeat_hbm, dfeat, sems):
+    for copy in copies:
         copy.wait()
 
 
@@ -206,8 +218,8 @@
 
     if size != 2 * ALONG_X:
         return lax.psum(own, "dp")
-    total = own + partner(own, ALONG_X)
-    return (total + partner(total, 1)) + (partner(total, 2) + partner(total, 3))
+    total = (own + partner(own, 1)) + (partner(own, 2) + partner(own, 3))
+    return total + partner(total, ALONG_X)
 
 
 def per_device(emb, comp, cot, pairs, counts):
@@ -241,23 +253,26 @@
             pltpu.VMEM(comp.shape, bf16),
             pltpu.VMEM(pairs.shape[::-1], jnp.int32),
             turned,
-            pltpu.SemaphoreType.DMA((2 * GROUPS + 3,)),
+            pltpu.SemaphoreType.DMA((2 * GROUPS + 2 + HALVES,)),
         ],
         compiler_params=pltpu.CompilerParams(vmem_limit_bytes=24 * MIB),
         cost_estimate=cost(10**9, 8 * 10**6),
     )(
         stay(jnp.transpose(emb, (1, 2, 0))),
-        stay(cot.reshape(fields, each * tile, LANES)),
+        stay(cot.reshape(HALVES, fields, each // HALVES * tile, LANES)),
         stay(comp),
         stay(pairs.T),
         counts,
     )
     x = lax.all_to_all(x, "field", 0, 0)
-    y = pl.pallas_call(
+    y, z = pl.pallas_call(
         functools.partial(block_kernel, width ** (-0.5), tile, width),
-        out_shape=jax.ShapeDtypeStruct((fields, each * rows + tile, LANES), bf16),
+        out_shape=(
+            jax.ShapeDtypeStruct((fields, each // HALVES * rows + tile, LANES), bf16),
+            jax.ShapeDtypeStruct((fields, each // HALVES * rows, LANES), bf16),
+        ),
         in_specs=[vmem],
-        out_specs=vmem,
+        out_specs=(vmem, vmem),
         scratch_shapes=[pltpu.VMEM((embeds, embeds), f32), pltpu.VMEM((embeds, LANES), f32)]
         + [
             pltpu.VMEM((embeds, width), bf16),
@@ -269,33 +284,36 @@
         cost_estimate=cost(4 * 10**9, 6 * 10**6),
     )(x)
     y = lax.all_to_all(y, "field", 0, 0)
-    grad = dp_sum(jnp.sum(y[:, each * rows :].astype(f32), axis=0))
+    y, z = lax.optimization_barrier((y, z))
+    z = lax.all_to_all(z, "field", 0, 0)
+    grad = dp_sum(jnp.sum(y[:, each // HALVES * rows :].astype(f32), axis=0))
     weight_grad = grad / (samp_rows * lax.axis_size("dp"))
 
-    by_row_out = jax.ShapeDtypeStruct((tile, width, samp_rows), bf16)
-    mixed, emb_grad, sorted_rows = pl.pallas_call(
-        unpack_kernel,
-        out_shape=(
-            jax.ShapeDtypeStruct((fields, each * tile, LANES), bf16),
-            by_row_out,
-            jax.ShapeDtypeStruct((packed * samp_rows, LANES), f32),
-        ),
+    mixed_out = jax.ShapeDtypeStruct((HALVES, fields, each // HALVES * tile, LANES), bf16)
+    half_rows = (packed * samp_rows // HALVES, LANES)
+    mixed, sorted_rows = pl.pallas_call(
+        early_kernel,
+        out_shape=(mixed_out, jax.ShapeDtypeStruct(half_rows, f32)),
         in_specs=[vmem],
-        out_specs=(hbm, hbm, vmem),
-        scratch_shapes=[by_row, pltpu.SemaphoreType.DMA((GROUPS + 1,))],
+        out_specs=(hbm, vmem),
+        scratch_shapes=[pltpu.SemaphoreType.DMA],
+        compiler_params=params,
+        cost_estimate=cost(10**8, 4 * 10**6),
+    )(y)
+    mixed, emb_grad = pl.pallas_call(
+        late_kernel,
+        out_shape=(mixed_out, jax.ShapeDtypeStruct((tile, width, samp_rows), bf16)),
+        in_specs=[vmem, vmem, hbm],
+        out_specs=(hbm, hbm),
+        input_output_aliases={2: 0},
+        scratch_shapes=[
+            pltpu.VMEM(half_rows, f32),
+            by_row,
+            pltpu.SemaphoreType.DMA((2 * GROUPS + 1,)),
+        ],
         compiler_params=params,
         cost_estimate=cost(10**9, 8 * 10**6),
-    )(y)
-    (emb_grad,) = pl.pallas_call(
-        finish_kernel,
-        out_shape=(by_row_out,),
-        in_specs=[vmem, hbm],
-        out_specs=(hbm,),
-        input_output_aliases={1: 0},
-        scratch_shapes=[by_row, pltpu.SemaphoreType.DMA((GROUPS,))],
-        compiler_params=params,
-        cost_estimate=cost(10**9, 8 * 10**6),
-    )(sorted_rows, emb_grad)
+    )(z, sorted_rows, mixed)
     return mixed.reshape(cot.shape), jnp.transpose(emb_grad, (2, 0, 1)), weight_grad
 
 

time: 104 us -> 103 us (level)
  blocking collectives: 79.2 us -> 65.1 us
  waiting for transfers between devices: 3.1 us -> 9.82 us
  starting transfers between devices: 7.07 us -> 10.9 us
  local copies, waits for them, and re-layouts: 0 us -> 2.55 us
    all_to_all x1, blocking collectives: 37.4 us -> 23.3 us  [per_device(): y = lax.all_to_all(y, 'field', 0, 0)]
    ppermute x4, waiting for transfers between devices: 3.1 us -> 9.57 us  [partner(): return lax.ppermute(value, 'dp', [(i, i ^ flip) for i in range(size)])]
    all_to_all x0 -> x1, starting transfers between devices: none -> 3.7 us  [per_device(): z = lax.all_to_all(z, 'field', 0, 0)]
    unnamed x0 -> x6, local copies, waits for them, and re-layouts: none -> 2.55 us
  transfers between devices with their start and end apart: 4 -> 5, of which waited for: 2 -> 4; matrix products, arithmetic and copies ran while one was open for 0% -> 1% of each run, Pallas kernels for 3% -> 1%
where the time goes in v12:
time: 103 us; the launch traced here: 102 us
  blocking collectives  65.1 us (63%)
  Pallas kernels  11.9 us (12%)
  starting transfers between devices  10.9 us (11%)
  waiting for transfers between devices  9.82 us (10%)
  local copies, waits for them, and re-layouts  2.55 us (2%)
  between operations  1.33 us (1%)
    all_to_all x1, blocking collectives, per_device(): x = lax.all_to_all(x, 'field', 0, 0)  41.8 us
    all_to_all x1, blocking collectives, per_device(): y = lax.all_to_all(y, 'field', 0, 0)  23.3 us
    ppermute x4, waiting for transfers between devices, partner(): return lax.ppermute(value, 'dp', [(i, i ^ flip) for i in range(size)])  9.57 us
    ppermute x4, starting transfers between devices, partner(): return lax.ppermute(value, 'dp', [(i, i ^ flip) for i in range(size)])  7.16 us
    pallas_call x1, Pallas kernels, per_device(): pl.pallas_call(functools.partial(block_kernel, width ** (-0.5), tile, wid...  5.14 us
    pallas_call x1, Pallas kernels, per_device(): pl.pallas_call(pack_kernel, out_shape=jax.ShapeDtypeStruct((fields, each...  3.73 us
    all_to_all x1, starting transfers between devices, per_device(): z = lax.all_to_all(z, 'field', 0, 0)  3.7 us
    unnamed x6, local copies, waits for them, and re-layouts  2.55 us
  transfers between devices with their start and end apart: 5, of which 4 were waited for; matrix products, arithmetic and copies ran while one was open for 1% of the time, Pallas kernels for 1%

profile of v12, /device:TPU:0, one launch (start us, length us, event | category | flops | bytes accessed | tf_op | source)
XLA Modules:
  0.0 102.2 jit_solution(11435273769117184144)
XLA Ops:
  1.3 3.7 %shard_map.76 = bf16[16,688,128]{2,1,0:T(8,128)(2,1)S(1)} custom-call(bf16[32,192,128]{2,1,0:T(8,128)(2,1)} %bitcast.5, bf16[2,16,128,128]{3,2,1,0:T(8,128)(2,1)} %bitcast.6, bf16[32,128]{1,0:T(8,128)(2,1)} %comp_hbm.1, s32[2,72]{1,0:T(2,128)} %bitcast.8, s32[1]{0:T(128)S(6)} %copy.10.counts_ref), custom_call_target="tpu_custom_call" | custom-call | flops 1000000000 | bytes 8000000 | tf_op jit(solution)/shard_map/pallas_call | solution.py:246
  5.0 41.8 %all_to_all.15.x_ref = bf16[16,688,128]{2,1,0:T(8,128)(2,1)S(1)} all-to-all(bf16[16,688,128]{2,1,0:T(8,128)(2,1)S(1)} %shard_map.76), channel_id=1, replica_groups=mesh['dp'=8,'field'=16] {'field'}, dimensions={0} | all-to-all | bytes 5636096 | tf_op jit(solution)/shard_map/all_to_all | solution.py:267
  46.8 5.1 %shard_map.77 = (bf16[16,352,128]{2,1,0:T(8,128)(2,1)S(1)}, bf16[16,320,128]{2,1,0:T(8,128)(2,1)S(1)}) custom-call(bf16[16,688,128]{2,1,0:T(8,128)(2,1)S(1)} %all_to_all.15.x_ref), custom_call_target="tpu_custom_call" | custom-call | flops 4000000000 | bytes 6000000 | tf_op jit(solution)/shard_map/pallas_call | solution.py:268
  51.9 0.0 copy-start.2
  51.9 23.3 %all_to_all.16.y_ref = bf16[16,352,128]{2,1,0:T(8,128)(2,1)S(1)} all-to-all(bf16[16,352,128]{2,1,0:T(8,128)(2,1)S(1)} %get-tuple-element.11), channel_id=1, replica_groups=mesh['dp'=8,'field'=16] {'field'}, dimensions={0} | all-to-all | bytes 2883584 | tf_op jit(solution)/shard_map/all_to_all | solution.py:286
  75.3 0.0 copy-done.2
  75.3 3.7 %all-to-all-start.2 = ((bf16[16,320,128]{2,1,0:T(8,128)(2,1)}), bf16[16,320,128]{2,1,0:T(8,128)(2,1)S(1)}, u32[]{:S(2)}, u32[]{:S(2)}) async-start(bf16[16,320,128]{2,1,0:T(8,128)(2,1)} %copy-done.2), calls=%async_computation.2 | async-start | bytes 2621440 | tf_op jit(solution)/shard_map/all_to_all | solution.py:288
  79.0 2.8 %collective-permute-start.2 = (f32[32,128]{1,0:T(8,128)S(1)}, f32[32,128]{1,0:T(8,128)S(1)}, u32[]{:S(2)}, u32[]{:S(2)}) collective-permute-start(f32[32,128]{1,0:T(8,128)S(1)} %convert_reduce_fusion), channel_id=1, source_target_pairs={{0,48},{16,32},{32,16},{48,0},{64,112},{80,96},{96,80},{112,64},{1... | collective-permute-start | bytes 49160 | tf_op jit(solution)/shard_map/ppermute | solution.py:217
  81.8 0.8 collective-permute-start.1
  82.6 0.5 collective-permute-start
  83.2 0.9 collective-permute-done.2
  84.0 3.1 %collective-permute-done.1 = f32[32,128]{1,0:T(8,128)S(1)} collective-permute-done((f32[32,128]{1,0:T(8,128)S(1)}, f32[32,128]{1,0:T(8,128)S(1)}, u32[]{:S(2)}, u32[]{:S(2)}) %collective-permute-start.1) | collective-permute-done | bytes 16416 | tf_op jit(solution)/shard_map/ppermute | solution.py:217
  87.1 0.0 collective-permute-done
  87.1 3.0 %collective-permute-start.3 = (f32[32,128]{1,0:T(8,128)S(1)}, f32[32,128]{1,0:T(8,128)S(1)}, u32[]{:S(2)}, u32[]{:S(2)}) collective-permute-start(f32[32,128]{1,0:T(8,128)S(1)} %add_add_fusion), channel_id=1, source_target_pairs={{0,64},{16,80},{32,96},{48,112},{64,0},{80,16},{96,32},{112,48},{1... | collective-permute-start | bytes 49160 | tf_op jit(solution)/shard_map/ppermute | solution.py:217
  90.1 0.8 shard_map.78
  90.9 0.0 copy-start
  90.9 1.1 %copy-done = f32[3072,128]{1,0:T(8,128)} copy-done((f32[3072,128]{1,0:T(8,128)}, f32[3072,128]{1,0:T(8,128)S(1)}, u32[]{:S(2)}) %copy-start) | copy-done | bytes 1572888
  92.0 5.7 %collective-permute-done.3 = f32[32,128]{1,0:T(8,128)S(1)} collective-permute-done((f32[32,128]{1,0:T(8,128)S(1)}, f32[32,128]{1,0:T(8,128)S(1)}, u32[]{:S(2)}, u32[]{:S(2)}) %collective-permute-start.3) | collective-permute-done | bytes 16416 | tf_op jit(solution)/shard_map/ppermute | solution.py:217
  97.7 0.6 add_multiply_fusion
  98.3 0.2 all-to-all-done.2.y_ref
  98.6 0.0 copy-start.1
  98.6 1.4 %copy-done.1 = f32[3072,128]{1,0:T(8,128)S(1)} copy-done((f32[3072,128]{1,0:T(8,128)S(1)}, f32[3072,128]{1,0:T(8,128)}, u32[]{:S(2)}) %copy-start.1) | copy-done | bytes 1572888
  100.0 2.3 %shard_map.79 = (bf16[2,16,128,128]{3,2,1,0:T(8,128)(2,1)}, bf16[32,192,128]{2,1,0:T(8,128)(2,1)}) custom-call(bf16[16,320,128]{2,1,0:T(8,128)(2,1)S(1)} %all-to-all-done.2.y_ref, f32[3072,128]{1,0:T(8,128)S(1)} %copy-done.1, bf16[2,16,128,128]{3,2,1,0:T(8,128)(2,1)} %get-tuple-element.16._), custom_call_target="tpu_custom_call", output_to_operand_aliasing={{0}: (2, {})} | custom-call | flops 1000000000 | bytes 8000000 | tf_op jit(solution)/shard_map/pallas_call | solution.py:303
  (2 shorter events, 0.0 us)
Async XLA Ops:
  51.9 23.3 %copy-start.2 = (bf16[16,320,128]{2,1,0:T(8,128)(2,1)}, bf16[16,320,128]{2,1,0:T(8,128)(2,1)S(1)}, u32[]{:S(2)}) copy-start(bf16[16,320,128]{2,1,0:T(8,128)(2,1)S(1)} %get-tuple-element.13) | copy-start | bytes 3932164
  75.3 23.3 %all-to-all-start.2 = ((bf16[16,320,128]{2,1,0:T(8,128)(2,1)}), bf16[16,320,128]{2,1,0:T(8,128)(2,1)S(1)}, u32[]{:S(2)}, u32[]{:S(2)}) async-start(bf16[16,320,128]{2,1,0:T(8,128)(2,1)} %copy-done.2), calls=%async_computation.2 | async-start | bytes 2621440 | tf_op jit(solution)/shard_map/all_to_all | solution.py:288
  79.0 5.0 %collective-permute-start.2 = (f32[32,128]{1,0:T(8,128)S(1)}, f32[32,128]{1,0:T(8,128)S(1)}, u32[]{:S(2)}, u32[]{:S(2)}) collective-permute-start(f32[32,128]{1,0:T(8,128)S(1)} %convert_reduce_fusion), channel_id=1, source_target_pairs={{0,48},{16,32},{32,16},{48,0},{64,112},{80,96},{96,80},{112,64},{1... | collective-permute-start | bytes 49160 | tf_op jit(solution)/shard_map/ppermute | solution.py:217
  81.8 5.2 %collective-permute-start.1 = (f32[32,128]{1,0:T(8,128)S(1)}, f32[32,128]{1,0:T(8,128)S(1)}, u32[]{:S(2)}, u32[]{:S(2)}) collective-permute-start(f32[32,128]{1,0:T(8,128)S(1)} %convert_reduce_fusion), channel_id=1, source_target_pairs={{0,32},{16,48},{32,0},{48,16},{64,96},{80,112},{96,64},{112,80},{1... | collective-permute-start | bytes 49160 | tf_op jit(solution)/shard_map/ppermute | solution.py:217
  82.6 4.5 %collective-permute-start = (f32[32,128]{1,0:T(8,128)S(1)}, f32[32,128]{1,0:T(8,128)S(1)}, u32[]{:S(2)}, u32[]{:S(2)}) collective-permute-start(f32[32,128]{1,0:T(8,128)S(1)} %convert_reduce_fusion), channel_id=1, source_target_pairs={{0,16},{16,0},{32,48},{48,32},{64,80},{80,64},{96,112},{112,96},{1... | collective-permute-start | bytes 49160 | tf_op jit(solution)/shard_map/ppermute | solution.py:217
  87.1 10.6 %collective-permute-start.3 = (f32[32,128]{1,0:T(8,128)S(1)}, f32[32,128]{1,0:T(8,128)S(1)}, u32[]{:S(2)}, u32[]{:S(2)}) collective-permute-start(f32[32,128]{1,0:T(8,128)S(1)} %add_add_fusion), channel_id=1, source_target_pairs={{0,64},{16,80},{32,96},{48,112},{64,0},{80,16},{96,32},{112,48},{1... | collective-permute-start | bytes 49160 | tf_op jit(solution)/shard_map/ppermute | solution.py:217
  90.9 1.1 %copy-start = (f32[3072,128]{1,0:T(8,128)}, f32[3072,128]{1,0:T(8,128)S(1)}, u32[]{:S(2)}) copy-start(f32[3072,128]{1,0:T(8,128)S(1)} %get-tuple-element.15.rows_ref) | copy-start | bytes 4718596
  98.6 1.4 %copy-start.1 = (f32[3072,128]{1,0:T(8,128)S(1)}, f32[3072,128]{1,0:T(8,128)}, u32[]{:S(2)}) copy-start(f32[3072,128]{1,0:T(8,128)} %copy-done) | copy-start | bytes 4718596

commit v13 on v12

--- a/solution.py
+++ b/solution.py
@@ -157,10 +157,9 @@
     y_refs[0][:, base // HALVES :] = grad[...].astype(bf16).reshape(fields, tile, LANES)
 
 
-def cast_rows(y_ref, rows_ref):
-    fields = y_ref.shape[0]
-    share = rows_ref.shape[0] // fields
-    for p in range(fields):
+def cast_rows(y_ref, rows_ref, peers):
+    share = rows_ref.shape[0] // y_ref.shape[0]
+    for p in peers:
         rows_ref[p * share : (p + 1) * share] = y_ref[p, :share].astype(jnp.float32)
 
 
@@ -169,23 +168,32 @@
     share = rows_ref.shape[0] // fields
     copy = pltpu.make_async_copy(y_ref.at[:, pl.ds(share, length)], mixed_hbm.at[0], sem)
     copy.start()
-    cast_rows(y_ref, rows_ref)
+    cast_rows(y_ref, rows_ref, range(fields))
     copy.wait()
 
 
-def late_kernel(y_ref, rows_ref, _, mixed_hbm, dfeat_hbm, more, dfeat, sems):
+def late_kernel(y_hbm, rows_ref, _, mixed_hbm, dfeat_hbm, y, more, dfeat, sems):
     tile, width, samples = dfeat.shape
     rest = width - LANES
     packed = tile + tile // 2
     fields, length = mixed_hbm.shape[1:3]
     share = rows_ref.shape[0] // fields
-    copies = [
-        pltpu.make_async_copy(
-            y_ref.at[:, pl.ds(share, length)], mixed_hbm.at[1], sems.at[2 * GROUPS]
+    some = fields // GROUPS
+    loads = []
+    for g in range(GROUPS):
+        here = pl.ds(g * some, some)
+        loads.append(pltpu.make_async_copy(y_hbm.at[here], y.at[here], sems.at[2 * GROUPS + g]))
+        loads[-1].start()
+    copies = []
+    for g in range(GROUPS):
+        here = pl.ds(g * some, some)
+        loads[g].wait()
+        copy = pltpu.make_async_copy(
+            y.at[here, pl.ds(share, length)], mixed_hbm.at[1, here], sems.at[3 * GROUPS + g]
         )
-    ]
-    copies[0].start()
-    cast_rows(y_ref, more)
+        copy.start()
+        copies.append(copy)
+        cast_rows(y, more, range(g * some, (g + 1) * some))
 
     def block(row):
         halves = [
@@ -303,17 +311,18 @@
     mixed, emb_grad = pl.pallas_call(
         late_kernel,
         out_shape=(mixed_out, jax.ShapeDtypeStruct((tile, width, samp_rows), bf16)),
-        in_specs=[vmem, vmem, hbm],
+        in_specs=[hbm, vmem, hbm],
         out_specs=(hbm, hbm),
         input_output_aliases={2: 0},
         scratch_shapes=[
+            pltpu.VMEM(z.shape, bf16),
             pltpu.VMEM(half_rows, f32),
             by_row,
-            pltpu.SemaphoreType.DMA((2 * GROUPS + 1,)),
+            pltpu.SemaphoreType.DMA((4 * GROUPS,)),
         ],
         compiler_params=params,
         cost_estimate=cost(10**9, 8 * 10**6),
-    )(z, sorted_rows, mixed)
+    )(stay(z), sorted_rows, mixed)
     return mixed.reshape(cot.shape), jnp.transpose(emb_grad, (2, 0, 1)), weight_grad
 
 

time: 103 us -> 105 us (1.019)
  local copies, waits for them, and re-layouts: 2.55 us -> 0 us
  Pallas kernels: 11.9 us -> 14.3 us
  waiting for transfers between devices: 9.82 us -> 11 us
    unnamed x6 -> x0, local copies, waits for them, and re-layouts: 2.55 us -> none
    pallas_call x1, Pallas kernels: 2.26 us -> 3.51 us  [per_device(): pl.pallas_call(late_kernel, out_shape=(mixed_out, jax.ShapeDtypeStruct((t...]
    ppermute x4, waiting for transfers between devices: 9.57 us -> 10.7 us  [partner(): return lax.ppermute(value, 'dp', [(i, i ^ flip) for i in range(size)])]
    pallas_call x1, Pallas kernels: 5.14 us -> 6.22 us  [per_device(): pl.pallas_call(functools.partial(block_kernel, width ** (-0.5), tile, wid...]
where the time goes in v13:
time: 105 us; the launch traced here: 104 us
  blocking collectives  65.1 us (62%)
  Pallas kernels  14.3 us (14%)
  starting transfers between devices  11.5 us (11%)
  waiting for transfers between devices  11 us (10%)
  between operations  1.32 us (1%)
    all_to_all x1, blocking collectives, per_device(): x = lax.all_to_all(x, 'field', 0, 0)  41.8 us
    all_to_all x1, blocking collectives, per_device(): y = lax.all_to_all(y, 'field', 0, 0)  23.3 us
    ppermute x4, waiting for transfers between devices, partner(): return lax.ppermute(value, 'dp', [(i, i ^ flip) for i in range(size)])  10.7 us
    ppermute x4, starting transfers between devices, partner(): return lax.ppermute(value, 'dp', [(i, i ^ flip) for i in range(size)])  7.15 us
    pallas_call x1, Pallas kernels, per_device(): pl.pallas_call(functools.partial(block_kernel, width ** (-0.5), tile, wid...  6.22 us
    all_to_all x1, starting transfers between devices, per_device(): z = lax.all_to_all(z, 'field', 0, 0)  4.39 us
    pallas_call x1, Pallas kernels, per_device(): pl.pallas_call(pack_kernel, out_shape=jax.ShapeDtypeStruct((fields, each...  3.73 us
    pallas_call x1, Pallas kernels, per_device(): pl.pallas_call(late_kernel, out_shape=(mixed_out, jax.ShapeDtypeStruct((t...  3.51 us
  transfers between devices with their start and end apart: 5, of which 4 were waited for; matrix products, arithmetic and copies ran while one was open for 1% of the time, Pallas kernels for 1%

profile of v13, /device:TPU:0, one launch (start us, length us, event | category | flops | bytes accessed | tf_op | source)
XLA Modules:
  0.0 103.9 jit_solution(2227831951502784557)
XLA Ops:
  1.3 3.7 %shard_map.76 = bf16[16,688,128]{2,1,0:T(8,128)(2,1)S(1)} custom-call(bf16[32,192,128]{2,1,0:T(8,128)(2,1)} %bitcast.5, bf16[2,16,128,128]{3,2,1,0:T(8,128)(2,1)} %bitcast.6, bf16[32,128]{1,0:T(8,128)(2,1)} %comp_hbm.1, s32[2,72]{1,0:T(2,128)} %bitcast.8, s32[1]{0:T(128)S(6)} %copy.10.counts_ref), custom_call_target="tpu_custom_call" | custom-call | flops 1000000000 | bytes 8000000 | tf_op jit(solution)/shard_map/pallas_call | solution.py:254
  5.0 41.8 %all_to_all.15.x_ref = bf16[16,688,128]{2,1,0:T(8,128)(2,1)S(1)} all-to-all(bf16[16,688,128]{2,1,0:T(8,128)(2,1)S(1)} %shard_map.76), channel_id=1, replica_groups=mesh['dp'=8,'field'=16] {'field'}, dimensions={0} | all-to-all | bytes 5636096 | tf_op jit(solution)/shard_map/all_to_all | solution.py:275
  46.8 6.2 %shard_map.77 = (bf16[16,352,128]{2,1,0:T(8,128)(2,1)S(1)}, bf16[16,320,128]{2,1,0:T(8,128)(2,1)}) custom-call(bf16[16,688,128]{2,1,0:T(8,128)(2,1)S(1)} %all_to_all.15.x_ref), custom_call_target="tpu_custom_call" | custom-call | flops 4000000000 | bytes 6000000 | tf_op jit(solution)/shard_map/pallas_call | solution.py:276
  53.0 23.3 %all_to_all.16.y_ref = bf16[16,352,128]{2,1,0:T(8,128)(2,1)S(1)} all-to-all(bf16[16,352,128]{2,1,0:T(8,128)(2,1)S(1)} %get-tuple-element.11), channel_id=1, replica_groups=mesh['dp'=8,'field'=16] {'field'}, dimensions={0} | all-to-all | bytes 2883584 | tf_op jit(solution)/shard_map/all_to_all | solution.py:294
  76.3 4.4 %all-to-all-start.2 = ((bf16[16,320,128]{2,1,0:T(8,128)(2,1)}), bf16[16,320,128]{2,1,0:T(8,128)(2,1)}, u32[]{:S(2)}, u32[]{:S(2)}) async-start(bf16[16,320,128]{2,1,0:T(8,128)(2,1)} %get-tuple-element.13), calls=%async_computation.2 | async-start | bytes 2621440 | tf_op jit(solution)/shard_map/all_to_all | solution.py:296
  80.7 2.8 %collective-permute-start.2 = (f32[32,128]{1,0:T(8,128)S(1)}, f32[32,128]{1,0:T(8,128)S(1)}, u32[]{:S(2)}, u32[]{:S(2)}) collective-permute-start(f32[32,128]{1,0:T(8,128)S(1)} %convert_reduce_fusion), channel_id=1, source_target_pairs={{0,48},{16,32},{32,16},{48,0},{64,112},{80,96},{96,80},{112,64},{1... | collective-permute-start | bytes 49160 | tf_op jit(solution)/shard_map/ppermute | solution.py:225
  83.6 0.8 collective-permute-start.1
  84.4 0.6 collective-permute-start
  84.9 0.9 collective-permute-done.2
  85.8 3.0 %collective-permute-done.1 = f32[32,128]{1,0:T(8,128)S(1)} collective-permute-done((f32[32,128]{1,0:T(8,128)S(1)}, f32[32,128]{1,0:T(8,128)S(1)}, u32[]{:S(2)}, u32[]{:S(2)}) %collective-permute-start.1) | collective-permute-done | bytes 16416 | tf_op jit(solution)/shard_map/ppermute | solution.py:225
  88.8 0.0 collective-permute-done
  88.8 3.0 %collective-permute-start.3 = (f32[32,128]{1,0:T(8,128)S(1)}, f32[32,128]{1,0:T(8,128)S(1)}, u32[]{:S(2)}, u32[]{:S(2)}) collective-permute-start(f32[32,128]{1,0:T(8,128)S(1)} %add_add_fusion), channel_id=1, source_target_pairs={{0,64},{16,80},{32,96},{48,112},{64,0},{80,16},{96,32},{112,48},{1... | collective-permute-start | bytes 49160 | tf_op jit(solution)/shard_map/ppermute | solution.py:225
  91.8 0.8 shard_map.78
  92.6 6.8 %collective-permute-done.3 = f32[32,128]{1,0:T(8,128)S(1)} collective-permute-done((f32[32,128]{1,0:T(8,128)S(1)}, f32[32,128]{1,0:T(8,128)S(1)}, u32[]{:S(2)}, u32[]{:S(2)}) %collective-permute-start.3) | collective-permute-done | bytes 16416 | tf_op jit(solution)/shard_map/ppermute | solution.py:225
  99.4 0.6 add_multiply_fusion
  100.0 0.4 all-to-all-done.2.y_hbm
  100.4 3.5 %shard_map.79 = (bf16[2,16,128,128]{3,2,1,0:T(8,128)(2,1)}, bf16[32,192,128]{2,1,0:T(8,128)(2,1)}) custom-call(bf16[16,320,128]{2,1,0:T(8,128)(2,1)} %all-to-all-done.2.y_hbm, f32[3072,128]{1,0:T(8,128)S(1)} %get-tuple-element.15.rows_ref, bf16[2,16,128,128]{3,2,1,0:T(8,128)(2,1)} %get-tuple-element.16._), custom_call_target="tpu_custom_call", output_to_operand_aliasing={{0}: (2, {})} | custom-call | flops 1000000000 | bytes 8000000 | tf_op jit(solution)/shard_map/pallas_call | solution.py:311
  (2 shorter events, 0.0 us)
Async XLA Ops:
  76.3 24.0 %all-to-all-start.2 = ((bf16[16,320,128]{2,1,0:T(8,128)(2,1)}), bf16[16,320,128]{2,1,0:T(8,128)(2,1)}, u32[]{:S(2)}, u32[]{:S(2)}) async-start(bf16[16,320,128]{2,1,0:T(8,128)(2,1)} %get-tuple-element.13), calls=%async_computation.2 | async-start | bytes 2621440 | tf_op jit(solution)/shard_map/all_to_all | solution.py:296
  80.7 5.0 %collective-permute-start.2 = (f32[32,128]{1,0:T(8,128)S(1)}, f32[32,128]{1,0:T(8,128)S(1)}, u32[]{:S(2)}, u32[]{:S(2)}) collective-permute-start(f32[32,128]{1,0:T(8,128)S(1)} %convert_reduce_fusion), channel_id=1, source_target_pairs={{0,48},{16,32},{32,16},{48,0},{64,112},{80,96},{96,80},{112,64},{1... | collective-permute-start | bytes 49160 | tf_op jit(solution)/shard_map/ppermute | solution.py:225
  83.6 5.2 %collective-permute-start.1 = (f32[32,128]{1,0:T(8,128)S(1)}, f32[32,128]{1,0:T(8,128)S(1)}, u32[]{:S(2)}, u32[]{:S(2)}) collective-permute-start(f32[32,128]{1,0:T(8,128)S(1)} %convert_reduce_fusion), channel_id=1, source_target_pairs={{0,32},{16,48},{32,0},{48,16},{64,96},{80,112},{96,64},{112,80},{1... | collective-permute-start | bytes 49160 | tf_op jit(solution)/shard_map/ppermute | solution.py:225
  84.4 4.5 %collective-permute-start = (f32[32,128]{1,0:T(8,128)S(1)}, f32[32,128]{1,0:T(8,128)S(1)}, u32[]{:S(2)}, u32[]{:S(2)}) collective-permute-start(f32[32,128]{1,0:T(8,128)S(1)} %convert_reduce_fusion), channel_id=1, source_target_pairs={{0,16},{16,0},{32,48},{48,32},{64,80},{80,64},{96,112},{112,96},{1... | collective-permute-start | bytes 49160 | tf_op jit(solution)/shard_map/ppermute | solution.py:225
  88.8 10.5 %collective-permute-start.3 = (f32[32,128]{1,0:T(8,128)S(1)}, f32[32,128]{1,0:T(8,128)S(1)}, u32[]{:S(2)}, u32[]{:S(2)}) collective-permute-start(f32[32,128]{1,0:T(8,128)S(1)} %add_add_fusion), channel_id=1, source_target_pairs={{0,64},{16,80},{32,96},{48,112},{64,0},{80,16},{96,32},{112,48},{1... | collective-permute-start | bytes 49160 | tf_op jit(solution)/shard_map/ppermute | solution.py:225

commit v14 on v12

--- a/solution.py
+++ b/solution.py
@@ -164,21 +164,28 @@
         rows_ref[p * share : (p + 1) * share] = y_ref[p, :share].astype(jnp.float32)
 
 
-def early_kernel(y_ref, mixed_hbm, rows_ref, sem):
+def early_kernel(y_ref, mixed_hbm, rows_hbm, rows, sems):
     fields, length = mixed_hbm.shape[1:3]
-    share = rows_ref.shape[0] // fields
-    copy = pltpu.make_async_copy(y_ref.at[:, pl.ds(share, length)], mixed_hbm.at[0], sem)
+    share = rows.shape[0] // fields
+    copy = pltpu.make_async_copy(
+        y_ref.at[:, pl.ds(share, length)], mixed_hbm.at[0], sems.at[0]
+    )
     copy.start()
-    cast_rows(y_ref, rows_ref)
+    cast_rows(y_ref, rows)
+    store = pltpu.make_async_copy(rows, rows_hbm, sems.at[1])
+    store.start()
     copy.wait()
-
-
-def late_kernel(y_ref, rows_ref, _, mixed_hbm, dfeat_hbm, more, dfeat, sems):
+    store.wait()
+
+
+def late_kernel(y_ref, rows_hbm, _, mixed_hbm, dfeat_hbm, rows_ref, more, dfeat, sems):
     tile, width, samples = dfeat.shape
     rest = width - LANES
     packed = tile + tile // 2
     fields, length = mixed_hbm.shape[1:3]
     share = rows_ref.shape[0] // fields
+    load = pltpu.make_async_copy(rows_hbm, rows_ref, sems.at[2 * GROUPS + 1])
+    load.start()
     copies = [
         pltpu.make_async_copy(
             y_ref.at[:, pl.ds(share, length)], mixed_hbm.at[1], sems.at[2 * GROUPS]
@@ -186,6 +193,7 @@
     ]
     copies[0].start()
     cast_rows(y_ref, more)
+    load.wait()
 
     def block(row):
         halves = [
@@ -295,25 +303,26 @@
         early_kernel,
         out_shape=(mixed_out, jax.ShapeDtypeStruct(half_rows, f32)),
         in_specs=[vmem],
-        out_specs=(hbm, vmem),
-        scratch_shapes=[pltpu.SemaphoreType.DMA],
+        out_specs=(hbm, hbm),
+        scratch_shapes=[pltpu.VMEM(half_rows, f32), pltpu.SemaphoreType.DMA((2,))],
         compiler_params=params,
         cost_estimate=cost(10**8, 4 * 10**6),
     )(y)
     mixed, emb_grad = pl.pallas_call(
         late_kernel,
         out_shape=(mixed_out, jax.ShapeDtypeStruct((tile, width, samp_rows), bf16)),
-        in_specs=[vmem, vmem, hbm],
+        in_specs=[vmem, hbm, hbm],
         out_specs=(hbm, hbm),
         input_output_aliases={2: 0},
         scratch_shapes=[
             pltpu.VMEM(half_rows, f32),
+            pltpu.VMEM(half_rows, f32),
             by_row,
-            pltpu.SemaphoreType.DMA((2 * GROUPS + 1,)),
+            pltpu.SemaphoreType.DMA((2 * GROUPS + 2,)),
         ],
         compiler_params=params,
         cost_estimate=cost(10**9, 8 * 10**6),
-    )(z, sorted_rows, mixed)
+    )(z, stay(sorted_rows), mixed)
     return mixed.reshape(cot.shape), jnp.transpose(emb_grad, (2, 0, 1)), weight_grad
 
 

time: 103 us -> 103 us (level)
  Pallas kernels: 11.9 us -> 13.4 us
  local copies, waits for them, and re-layouts: 2.55 us -> 1.15 us
    pallas_call x1, Pallas kernels: 2.26 us -> 3.75 us  [per_device(): pl.pallas_call(late_kernel, out_shape=(mixed_out, jax.ShapeDtypeStruct((t...]
    unnamed x6 -> x4, local copies, waits for them, and re-layouts: 2.55 us -> 1.15 us
where the time goes in v14:
time: 103 us; the launch traced here: 102 us
  blocking collectives  65.1 us (63%)
  Pallas kernels  13.4 us (13%)
  starting transfers between devices  10.9 us (11%)
  waiting for transfers between devices  9.8 us (10%)
  between operations  1.33 us (1%)
  local copies, waits for them, and re-layouts  1.15 us (1%)
    all_to_all x1, blocking collectives, per_device(): x = lax.all_to_all(x, 'field', 0, 0)  41.8 us
    all_to_all x1, blocking collectives, per_device(): y = lax.all_to_all(y, 'field', 0, 0)  23.3 us
    ppermute x4, waiting for transfers between devices, partner(): return lax.ppermute(value, 'dp', [(i, i ^ flip) for i in range(size)])  9.56 us
    ppermute x4, starting transfers between devices, partner(): return lax.ppermute(value, 'dp', [(i, i ^ flip) for i in range(size)])  7.16 us
    pallas_call x1, Pallas kernels, per_device(): pl.pallas_call(functools.partial(block_kernel, width ** (-0.5), tile, wid...  5.14 us
    pallas_call x1, Pallas kernels, per_device(): pl.pallas_call(late_kernel, out_shape=(mixed_out, jax.ShapeDtypeStruct((t...  3.75 us
    pallas_call x1, Pallas kernels, per_device(): pl.pallas_call(pack_kernel, out_shape=jax.ShapeDtypeStruct((fields, each...  3.73 us
    all_to_all x1, starting transfers between devices, per_device(): z = lax.all_to_all(z, 'field', 0, 0)  3.7 us
  transfers between devices with their start and end apart: 5, of which 4 were waited for; matrix products, arithmetic and copies ran while one was open for 1% of the time, Pallas kernels for 1%

profile of v14, /device:TPU:0, one launch (start us, length us, event | category | flops | bytes accessed | tf_op | source)
XLA Modules:
  0.0 102.3 jit_solution(16859800712460523784)
XLA Ops:
  1.3 3.7 %shard_map.76 = bf16[16,688,128]{2,1,0:T(8,128)(2,1)S(1)} custom-call(bf16[32,192,128]{2,1,0:T(8,128)(2,1)} %bitcast.5, bf16[2,16,128,128]{3,2,1,0:T(8,128)(2,1)} %bitcast.6, bf16[32,128]{1,0:T(8,128)(2,1)} %comp_hbm.1, s32[2,72]{1,0:T(2,128)} %bitcast.8, s32[1]{0:T(128)S(6)} %copy.10.counts_ref), custom_call_target="tpu_custom_call" | custom-call | flops 1000000000 | bytes 8000000 | tf_op jit(solution)/shard_map/pallas_call | solution.py:254
  5.0 41.8 %all_to_all.15.x_ref = bf16[16,688,128]{2,1,0:T(8,128)(2,1)S(1)} all-to-all(bf16[16,688,128]{2,1,0:T(8,128)(2,1)S(1)} %shard_map.76), channel_id=1, replica_groups=mesh['dp'=8,'field'=16] {'field'}, dimensions={0} | all-to-all | bytes 5636096 | tf_op jit(solution)/shard_map/all_to_all | solution.py:275
  46.8 5.1 %shard_map.77 = (bf16[16,352,128]{2,1,0:T(8,128)(2,1)S(1)}, bf16[16,320,128]{2,1,0:T(8,128)(2,1)S(1)}) custom-call(bf16[16,688,128]{2,1,0:T(8,128)(2,1)S(1)} %all_to_all.15.x_ref), custom_call_target="tpu_custom_call" | custom-call | flops 4000000000 | bytes 6000000 | tf_op jit(solution)/shard_map/pallas_call | solution.py:276
  51.9 0.0 copy-start.1
  51.9 23.3 %all_to_all.16.y_ref = bf16[16,352,128]{2,1,0:T(8,128)(2,1)S(1)} all-to-all(bf16[16,352,128]{2,1,0:T(8,128)(2,1)S(1)} %get-tuple-element.11), channel_id=1, replica_groups=mesh['dp'=8,'field'=16] {'field'}, dimensions={0} | all-to-all | bytes 2883584 | tf_op jit(solution)/shard_map/all_to_all | solution.py:294
  75.3 0.0 copy-done.1
  75.3 3.7 %all-to-all-start.2 = ((bf16[16,320,128]{2,1,0:T(8,128)(2,1)}), bf16[16,320,128]{2,1,0:T(8,128)(2,1)S(1)}, u32[]{:S(2)}, u32[]{:S(2)}) async-start(bf16[16,320,128]{2,1,0:T(8,128)(2,1)} %copy-done.1), calls=%async_computation.2 | async-start | bytes 2621440 | tf_op jit(solution)/shard_map/all_to_all | solution.py:296
  79.0 2.8 %collective-permute-start.2 = (f32[32,128]{1,0:T(8,128)S(1)}, f32[32,128]{1,0:T(8,128)S(1)}, u32[]{:S(2)}, u32[]{:S(2)}) collective-permute-start(f32[32,128]{1,0:T(8,128)S(1)} %convert_reduce_fusion), channel_id=1, source_target_pairs={{0,48},{16,32},{32,16},{48,0},{64,112},{80,96},{96,80},{112,64},{1... | collective-permute-start | bytes 49160 | tf_op jit(solution)/shard_map/ppermute | solution.py:225
  81.8 0.8 collective-permute-start.1
  82.6 0.5 collective-permute-start
  83.2 0.9 collective-permute-done.2
  84.0 3.1 %collective-permute-done.1 = f32[32,128]{1,0:T(8,128)S(1)} collective-permute-done((f32[32,128]{1,0:T(8,128)S(1)}, f32[32,128]{1,0:T(8,128)S(1)}, u32[]{:S(2)}, u32[]{:S(2)}) %collective-permute-start.1) | collective-permute-done | bytes 16416 | tf_op jit(solution)/shard_map/ppermute | solution.py:225
  87.1 0.0 collective-permute-done
  87.1 3.0 %collective-permute-start.3 = (f32[32,128]{1,0:T(8,128)S(1)}, f32[32,128]{1,0:T(8,128)S(1)}, u32[]{:S(2)}, u32[]{:S(2)}) collective-permute-start(f32[32,128]{1,0:T(8,128)S(1)} %add_add_fusion), channel_id=1, source_target_pairs={{0,64},{16,80},{32,96},{48,112},{64,0},{80,16},{96,32},{112,48},{1... | collective-permute-start | bytes 49160 | tf_op jit(solution)/shard_map/ppermute | solution.py:225
  90.1 0.8 shard_map.78
  90.9 0.0 copy-start
  90.9 1.1 %copy-done = f32[3072,128]{1,0:T(8,128)} copy-done((f32[3072,128]{1,0:T(8,128)}, f32[3072,128]{1,0:T(8,128)S(1)}, u32[]{:S(2)}) %copy-start) | copy-done | bytes 1572888
  92.1 5.6 %collective-permute-done.3 = f32[32,128]{1,0:T(8,128)S(1)} collective-permute-done((f32[32,128]{1,0:T(8,128)S(1)}, f32[32,128]{1,0:T(8,128)S(1)}, u32[]{:S(2)}, u32[]{:S(2)}) %collective-permute-start.3) | collective-permute-done | bytes 16416 | tf_op jit(solution)/shard_map/ppermute | solution.py:225
  97.7 0.6 add_multiply_fusion
  98.3 0.2 all-to-all-done.2.y_ref
  98.6 3.7 %shard_map.79 = (bf16[2,16,128,128]{3,2,1,0:T(8,128)(2,1)}, bf16[32,192,128]{2,1,0:T(8,128)(2,1)}) custom-call(bf16[16,320,128]{2,1,0:T(8,128)(2,1)S(1)} %all-to-all-done.2.y_ref, f32[3072,128]{1,0:T(8,128)} %copy-done, bf16[2,16,128,128]{3,2,1,0:T(8,128)(2,1)} %get-tuple-element.16._), custom_call_target="tpu_custom_call", output_to_operand_aliasing={{0}: (2, {})} | custom-call | flops 1000000000 | bytes 8000000 | tf_op jit(solution)/shard_map/pallas_call | solution.py:311
  (2 shorter events, 0.0 us)
Async XLA Ops:
  51.9 23.3 %copy-start.1 = (bf16[16,320,128]{2,1,0:T(8,128)(2,1)}, bf16[16,320,128]{2,1,0:T(8,128)(2,1)S(1)}, u32[]{:S(2)}) copy-start(bf16[16,320,128]{2,1,0:T(8,128)(2,1)S(1)} %get-tuple-element.13) | copy-start | bytes 3932164
  75.3 23.3 %all-to-all-start.2 = ((bf16[16,320,128]{2,1,0:T(8,128)(2,1)}), bf16[16,320,128]{2,1,0:T(8,128)(2,1)S(1)}, u32[]{:S(2)}, u32[]{:S(2)}) async-start(bf16[16,320,128]{2,1,0:T(8,128)(2,1)} %copy-done.1), calls=%async_computation.2 | async-start | bytes 2621440 | tf_op jit(solution)/shard_map/all_to_all | solution.py:296
  79.0 5.0 %collective-permute-start.2 = (f32[32,128]{1,0:T(8,128)S(1)}, f32[32,128]{1,0:T(8,128)S(1)}, u32[]{:S(2)}, u32[]{:S(2)}) collective-permute-start(f32[32,128]{1,0:T(8,128)S(1)} %convert_reduce_fusion), channel_id=1, source_target_pairs={{0,48},{16,32},{32,16},{48,0},{64,112},{80,96},{96,80},{112,64},{1... | collective-permute-start | bytes 49160 | tf_op jit(solution)/shard_map/ppermute | solution.py:225
  81.8 5.2 %collective-permute-start.1 = (f32[32,128]{1,0:T(8,128)S(1)}, f32[32,128]{1,0:T(8,128)S(1)}, u32[]{:S(2)}, u32[]{:S(2)}) collective-permute-start(f32[32,128]{1,0:T(8,128)S(1)} %convert_reduce_fusion), channel_id=1, source_target_pairs={{0,32},{16,48},{32,0},{48,16},{64,96},{80,112},{96,64},{112,80},{1... | collective-permute-start | bytes 49160 | tf_op jit(solution)/shard_map/ppermute | solution.py:225
  82.6 4.5 %collective-permute-start = (f32[32,128]{1,0:T(8,128)S(1)}, f32[32,128]{1,0:T(8,128)S(1)}, u32[]{:S(2)}, u32[]{:S(2)}) collective-permute-start(f32[32,128]{1,0:T(8,128)S(1)} %convert_reduce_fusion), channel_id=1, source_target_pairs={{0,16},{16,0},{32,48},{48,32},{64,80},{80,64},{96,112},{112,96},{1... | collective-permute-start | bytes 49160 | tf_op jit(solution)/shard_map/ppermute | solution.py:225
  87.1 10.6 %collective-permute-start.3 = (f32[32,128]{1,0:T(8,128)S(1)}, f32[32,128]{1,0:T(8,128)S(1)}, u32[]{:S(2)}, u32[]{:S(2)}) collective-permute-start(f32[32,128]{1,0:T(8,128)S(1)} %add_add_fusion), channel_id=1, source_target_pairs={{0,64},{16,80},{32,96},{48,112},{64,0},{80,16},{96,32},{112,48},{1... | collective-permute-start | bytes 49160 | tf_op jit(solution)/shard_map/ppermute | solution.py:225
  90.9 1.1 %copy-start = (f32[3072,128]{1,0:T(8,128)}, f32[3072,128]{1,0:T(8,128)S(1)}, u32[]{:S(2)}) copy-start(f32[3072,128]{1,0:T(8,128)S(1)} %get-tuple-element.15.rows_hbm) | copy-start | bytes 4718596

commit v15 on v12

--- a/solution.py
+++ b/solution.py
@@ -161,7 +161,7 @@
     fields = y_ref.shape[0]
     share = rows_ref.shape[0] // fields
     for p in range(fields):
-        rows_ref[p * share : (p + 1) * share] = y_ref[p, :share].astype(jnp.float32)
+        rows_ref[p * share : (p + 1) * share] = y_ref[p, :share].astype(rows_ref.dtype)
 
 
 def early_kernel(y_ref, mixed_hbm, rows_ref, sem):
@@ -173,7 +173,7 @@
     copy.wait()
 
 
-def late_kernel(y_ref, rows_ref, _, mixed_hbm, dfeat_hbm, more, dfeat, sems):
+def late_kernel(y_ref, early_ref, _, mixed_hbm, dfeat_hbm, rows_ref, more, dfeat, sems):
     tile, width, samples = dfeat.shape
     rest = width - LANES
     packed = tile + tile // 2
@@ -185,6 +185,7 @@
         )
     ]
     copies[0].start()
+    rows_ref[...] = early_ref[...].astype(jnp.float32)
     cast_rows(y_ref, more)
 
     def block(row):
@@ -293,7 +294,7 @@
     half_rows = (packed * samp_rows // HALVES, LANES)
     mixed, sorted_rows = pl.pallas_call(
         early_kernel,
-        out_shape=(mixed_out, jax.ShapeDtypeStruct(half_rows, f32)),
+        out_shape=(mixed_out, jax.ShapeDtypeStruct(half_rows, bf16)),
         in_specs=[vmem],
         out_specs=(hbm, vmem),
         scratch_shapes=[pltpu.SemaphoreType.DMA],
@@ -308,6 +309,7 @@
         input_output_aliases={2: 0},
         scratch_shapes=[
             pltpu.VMEM(half_rows, f32),
+            pltpu.VMEM(half_rows, f32),
             by_row,
             pltpu.SemaphoreType.DMA((2 * GROUPS + 1,)),
         ],

time: 103 us -> 102 us (level)
  local copies, waits for them, and re-layouts: 2.55 us -> 0.01 us
  waiting for transfers between devices: 9.82 us -> 11 us
    unnamed x6 -> x2, local copies, waits for them, and re-layouts: 2.55 us -> 0.01 us
    ppermute x4, waiting for transfers between devices: 9.57 us -> 10.7 us  [partner(): return lax.ppermute(value, 'dp', [(i, i ^ flip) for i in range(size)])]
where the time goes in v15:
time: 102 us; the launch traced here: 101 us
  blocking collectives  65.1 us (64%)
  Pallas kernels  12 us (12%)
  waiting for transfers between devices  11 us (11%)
  starting transfers between devices  10.9 us (11%)
  between operations  1.32 us (1%)
    all_to_all x1, blocking collectives, per_device(): x = lax.all_to_all(x, 'field', 0, 0)  41.8 us
    all_to_all x1, blocking collectives, per_device(): y = lax.all_to_all(y, 'field', 0, 0)  23.3 us
    ppermute x4, waiting for transfers between devices, partner(): return lax.ppermute(value, 'dp', [(i, i ^ flip) for i in range(size)])  10.7 us
    ppermute x4, starting transfers between devices, partner(): return lax.ppermute(value, 'dp', [(i, i ^ flip) for i in range(size)])  7.16 us
    pallas_call x1, Pallas kernels, per_device(): pl.pallas_call(functools.partial(block_kernel, width ** (-0.5), tile, wid...  5.14 us
    pallas_call x1, Pallas kernels, per_device(): pl.pallas_call(pack_kernel, out_shape=jax.ShapeDtypeStruct((fields, each...  3.73 us
    all_to_all x1, starting transfers between devices, per_device(): z = lax.all_to_all(z, 'field', 0, 0)  3.7 us
    pallas_call x1, Pallas kernels, per_device(): pl.pallas_call(late_kernel, out_shape=(mixed_out, jax.ShapeDtypeStruct((t...  2.35 us
  transfers between devices with their start and end apart: 5, of which 4 were waited for; matrix products, arithmetic and copies ran while one was open for 1% of the time, Pallas kernels for 1%

profile of v15, /device:TPU:0, one launch (start us, length us, event | category | flops | bytes accessed | tf_op | source)
XLA Modules:
  0.0 100.9 jit_solution(7080136096095624591)
XLA Ops:
  1.3 3.7 %shard_map.76 = bf16[16,688,128]{2,1,0:T(8,128)(2,1)S(1)} custom-call(bf16[32,192,128]{2,1,0:T(8,128)(2,1)} %bitcast.5, bf16[2,16,128,128]{3,2,1,0:T(8,128)(2,1)} %bitcast.6, bf16[32,128]{1,0:T(8,128)(2,1)} %comp_hbm.1, s32[2,72]{1,0:T(2,128)} %bitcast.7, s32[1]{0:T(128)S(6)} %copy.10.counts_ref), custom_call_target="tpu_custom_call" | custom-call | flops 1000000000 | bytes 8000000 | tf_op jit(solution)/shard_map/pallas_call | solution.py:247
  5.0 41.8 %all_to_all.15.x_ref = bf16[16,688,128]{2,1,0:T(8,128)(2,1)S(1)} all-to-all(bf16[16,688,128]{2,1,0:T(8,128)(2,1)S(1)} %shard_map.76), channel_id=1, replica_groups=mesh['dp'=8,'field'=16] {'field'}, dimensions={0} | all-to-all | bytes 5636096 | tf_op jit(solution)/shard_map/all_to_all | solution.py:268
  46.8 5.1 %shard_map.77 = (bf16[16,352,128]{2,1,0:T(8,128)(2,1)S(1)}, bf16[16,320,128]{2,1,0:T(8,128)(2,1)S(1)}) custom-call(bf16[16,688,128]{2,1,0:T(8,128)(2,1)S(1)} %all_to_all.15.x_ref), custom_call_target="tpu_custom_call" | custom-call | flops 4000000000 | bytes 6000000 | tf_op jit(solution)/shard_map/pallas_call | solution.py:269
  51.9 0.0 copy-start
  51.9 23.3 %all_to_all.16.y_ref = bf16[16,352,128]{2,1,0:T(8,128)(2,1)S(1)} all-to-all(bf16[16,352,128]{2,1,0:T(8,128)(2,1)S(1)} %get-tuple-element.11), channel_id=1, replica_groups=mesh['dp'=8,'field'=16] {'field'}, dimensions={0} | all-to-all | bytes 2883584 | tf_op jit(solution)/shard_map/all_to_all | solution.py:287
  75.3 0.0 copy-done
  75.3 3.7 %all-to-all-start.2 = ((bf16[16,320,128]{2,1,0:T(8,128)(2,1)}), bf16[16,320,128]{2,1,0:T(8,128)(2,1)S(1)}, u32[]{:S(2)}, u32[]{:S(2)}) async-start(bf16[16,320,128]{2,1,0:T(8,128)(2,1)} %copy-done), calls=%async_computation.2 | async-start | bytes 2621440 | tf_op jit(solution)/shard_map/all_to_all | solution.py:289
  79.0 2.8 %collective-permute-start.2 = (f32[32,128]{1,0:T(8,128)S(1)}, f32[32,128]{1,0:T(8,128)S(1)}, u32[]{:S(2)}, u32[]{:S(2)}) collective-permute-start(f32[32,128]{1,0:T(8,128)S(1)} %convert_reduce_fusion), channel_id=1, source_target_pairs={{0,48},{16,32},{32,16},{48,0},{64,112},{80,96},{96,80},{112,64},{1... | collective-permute-start | bytes 49160 | tf_op jit(solution)/shard_map/ppermute | solution.py:218
  81.8 0.8 collective-permute-start.1
  82.6 0.5 collective-permute-start
  83.2 0.9 collective-permute-done.2
  84.0 3.1 %collective-permute-done.1 = f32[32,128]{1,0:T(8,128)S(1)} collective-permute-done((f32[32,128]{1,0:T(8,128)S(1)}, f32[32,128]{1,0:T(8,128)S(1)}, u32[]{:S(2)}, u32[]{:S(2)}) %collective-permute-start.1) | collective-permute-done | bytes 16416 | tf_op jit(solution)/shard_map/ppermute | solution.py:218
  87.1 0.0 collective-permute-done
  87.1 3.0 %collective-permute-start.3 = (f32[32,128]{1,0:T(8,128)S(1)}, f32[32,128]{1,0:T(8,128)S(1)}, u32[]{:S(2)}, u32[]{:S(2)}) collective-permute-start(f32[32,128]{1,0:T(8,128)S(1)} %add_add_fusion), channel_id=1, source_target_pairs={{0,64},{16,80},{32,96},{48,112},{64,0},{80,16},{96,32},{112,48},{1... | collective-permute-start | bytes 49160 | tf_op jit(solution)/shard_map/ppermute | solution.py:218
  90.1 0.8 shard_map.78
  90.9 6.8 %collective-permute-done.3 = f32[32,128]{1,0:T(8,128)S(1)} collective-permute-done((f32[32,128]{1,0:T(8,128)S(1)}, f32[32,128]{1,0:T(8,128)S(1)}, u32[]{:S(2)}, u32[]{:S(2)}) %collective-permute-start.3) | collective-permute-done | bytes 16416 | tf_op jit(solution)/shard_map/ppermute | solution.py:218
  97.7 0.6 add_multiply_fusion
  98.3 0.2 all-to-all-done.2.y_ref
  98.6 2.3 %shard_map.79 = (bf16[2,16,128,128]{3,2,1,0:T(8,128)(2,1)}, bf16[32,192,128]{2,1,0:T(8,128)(2,1)}) custom-call(bf16[16,320,128]{2,1,0:T(8,128)(2,1)S(1)} %all-to-all-done.2.y_ref, bf16[3072,128]{1,0:T(8,128)(2,1)S(1)} %get-tuple-element.15.early_ref, bf16[2,16,128,128]{3,2,1,0:T(8,128)(2,1)} %get-tuple-element.16._), custom_call_target="tpu_custom_call", output_to_operand_aliasing={{0}: (2, {})} | custom-call | flops 1000000000 | bytes 8000000 | tf_op jit(solution)/shard_map/pallas_call | solution.py:304
  (2 shorter events, 0.0 us)
Async XLA Ops:
  51.9 23.3 %copy-start = (bf16[16,320,128]{2,1,0:T(8,128)(2,1)}, bf16[16,320,128]{2,1,0:T(8,128)(2,1)S(1)}, u32[]{:S(2)}) copy-start(bf16[16,320,128]{2,1,0:T(8,128)(2,1)S(1)} %get-tuple-element.13) | copy-start | bytes 3932164
  75.3 23.3 %all-to-all-start.2 = ((bf16[16,320,128]{2,1,0:T(8,128)(2,1)}), bf16[16,320,128]{2,1,0:T(8,128)(2,1)S(1)}, u32[]{:S(2)}, u32[]{:S(2)}) async-start(bf16[16,320,128]{2,1,0:T(8,128)(2,1)} %copy-done), calls=%async_computation.2 | async-start | bytes 2621440 | tf_op jit(solution)/shard_map/all_to_all | solution.py:289
  79.0 5.0 %collective-permute-start.2 = (f32[32,128]{1,0:T(8,128)S(1)}, f32[32,128]{1,0:T(8,128)S(1)}, u32[]{:S(2)}, u32[]{:S(2)}) collective-permute-start(f32[32,128]{1,0:T(8,128)S(1)} %convert_reduce_fusion), channel_id=1, source_target_pairs={{0,48},{16,32},{32,16},{48,0},{64,112},{80,96},{96,80},{112,64},{1... | collective-permute-start | bytes 49160 | tf_op jit(solution)/shard_map/ppermute | solution.py:218
  81.8 5.2 %collective-permute-start.1 = (f32[32,128]{1,0:T(8,128)S(1)}, f32[32,128]{1,0:T(8,128)S(1)}, u32[]{:S(2)}, u32[]{:S(2)}) collective-permute-start(f32[32,128]{1,0:T(8,128)S(1)} %convert_reduce_fusion), channel_id=1, source_target_pairs={{0,32},{16,48},{32,0},{48,16},{64,96},{80,112},{96,64},{112,80},{1... | collective-permute-start | bytes 49160 | tf_op jit(solution)/shard_map/ppermute | solution.py:218
  82.6 4.5 %collective-permute-start = (f32[32,128]{1,0:T(8,128)S(1)}, f32[32,128]{1,0:T(8,128)S(1)}, u32[]{:S(2)}, u32[]{:S(2)}) collective-permute-start(f32[32,128]{1,0:T(8,128)S(1)} %convert_reduce_fusion), channel_id=1, source_target_pairs={{0,16},{16,0},{32,48},{48,32},{64,80},{80,64},{96,112},{112,96},{1... | collective-permute-start | bytes 49160 | tf_op jit(solution)/shard_map/ppermute | solution.py:218
  87.1 10.6 %collective-permute-start.3 = (f32[32,128]{1,0:T(8,128)S(1)}, f32[32,128]{1,0:T(8,128)S(1)}, u32[]{:S(2)}, u32[]{:S(2)}) collective-permute-start(f32[32,128]{1,0:T(8,128)S(1)} %add_add_fusion), channel_id=1, source_target_pairs={{0,64},{16,80},{32,96},{48,112},{64,0},{80,16},{96,32},{112,48},{1... | collective-permute-start | bytes 49160 | tf_op jit(solution)/shard_map/ppermute | solution.py:218
